TPU v7x, 256 devices: a whole 4x4x8 slice. The times are simulated.
256 devices in a mesh: bg: 64 (over z, x, core), type: 4 (over y).
Axes of the slice: x: 4, y: 4, z: 8, core: 2. Of those that a mesh axis runs over, the one named last changes fastest.
Arguments:
- seed_slab: float32 [8192, 36864], P('bg', 'type'), as said below
- row_target: int32 [8192], P('bg'), may hold values from 50 to 1999
- county_id: int32 [8192], P('bg'), may hold values from 0 to 63, as said below
- county_target: int32 [64, 36864], P(None, 'type'), may hold values from 1 to 999
Outputs:
- fitted: float32 [8192, 36864], P('bg', 'type')
Inputs may be any that keep to these rules, and one draw needn't show every extreme that they name: county_id never falls along the block groups, and every county 0 to 63 has one or more block groups. `seed_slab`: positive.
All inputs are finite; a program needn't handle non-finite values.
Results may differ from a plain program's by a relative error of at most 0.0001.
Values sent between devices are 32-bit elements; how exact they have to be, the bound alone decides.
No kernel may reach another device: no remote copies, remote signals or barrier semaphores. Data moves between devices by JAX's collectives and lax.ppermute only.
A program may use at most 64 MiB of HBM per device.

v0:
```python
import jax
import jax.numpy as jnp
from jax import lax
from jax.sharding import PartitionSpec as P

CYCLES = 2


def local(seed_slab, row_target, county_id, county_target):
    highest = lax.Precision.HIGHEST
    weights = seed_slab
    row_goal = row_target.astype(jnp.float32)
    shares = county_target.astype(jnp.float32)
    counties = shares.shape[0]
    county_range = jnp.arange(counties, dtype=jnp.int32)
    contract_rows = (((0,), (0,)), ((), ()))
    county_member = (county_id[:, None] == county_range[None, :]).astype(jnp.float32)
    people = lax.psum(jnp.sum(county_member * row_goal[:, None], axis=0), "bg")
    share_total = lax.psum(jnp.sum(shares, axis=1), "type")
    county_goal = shares * (people / share_total)[:, None]
    for cycle in range(CYCLES):
        row_sum = lax.psum(jnp.sum(weights, axis=1), "type")
        weights = weights * (row_goal / row_sum)[:, None]
        partial_value = lax.dot_general(
            county_member,
            weights,
            contract_rows,
            precision=highest,
            preferred_element_type=jnp.float32,
        )
        county_sum = lax.psum(partial_value, "bg")
        factor = county_goal / county_sum
        weights = weights * jnp.dot(
            county_member, factor, precision=highest, preferred_element_type=jnp.float32
        )
    return 100.0 * weights


def solution(mesh):
    return jax.shard_map(
        local,
        mesh=mesh,
        in_specs=(P("bg", "type"), P("bg"), P("bg"), P(None, "type")),
        out_specs=P("bg", "type"),
        check_vma=False,
    )
```

profile of v0, /device:TPU:1, one launch (start us, length us, event | category | flops | bytes accessed | tf_op | source)
XLA Modules:
  0.0 444.6 jit_solution(17603729768763497075)
XLA Ops:
  6.5 0.0 all-reduce.4.cloned.1.call-start
  6.5 1.9 convert_reduce_fusion
  8.5 0.0 copy-start.2
  8.5 0.0 copy-start.1
  8.5 2.6 reduce_sum.36
  11.1 9.6 %all-reduce = (f32[128]{0:T(128)S(1)}, f32[64]{0:T(128)S(1)}) all-reduce(f32[128]{0:T(128)S(1)} %reduce_sum.36, f32[64]{0:T(128)S(1)} %convert_reduce_fusion), channel_id=1, replica_groups=mesh['bg'=64,'type'=4] {'type'}, use_global_device_ids=true, to_apply=%region_1.0 | all-reduce | flops 192 | bytes 1536 | tf_op jit(solution)/shard_map/psum | solution.py:22
  20.7 0.0 copy-done.2
  20.7 0.0 copy-done.1
  20.7 5.9 %fusion.3 = f32[64,9216]{1,0:T(8,128)} fusion(f32[128,9216]{1,0:T(8,128)} %param.4, f32[128]{0:T(128)S(1)} %convert_divide_fusion.1, s32[128]{0:T(128)S(1)} %copy-done.1), kind=kOutput, calls=%fused_computation.5 | convolution fusion | flops 907157504 | bytes 7078912 | tf_op jit(solution)/shard_map/dot_general | solution.py:24
  26.6 0.0 copy-start
  26.6 0.0 all-reduce.4.cloned.1.call-update
  26.6 0.0 all-reduce.6.cloned.1.call-start
  26.7 0.1 select_reduce_fusion
  26.8 129.4 %psum.43 = f32[64]{0:T(128)S(1)} all-reduce(f32[64]{0:T(128)S(1)} %select_reduce_fusion), channel_id=1, replica_groups=mesh['bg'=64,'type'=4] {'bg'}, use_global_device_ids=true, to_apply=%region_3.0 | all-reduce | flops 64 | bytes 512 | tf_op jit(solution)/shard_map/psum | solution.py:18
  156.2 62.3 %all-reduce.4.cloned.1.call-done = f32[64,9216]{1,0:T(8,128)} async-done(((f32[64,9216]{1,0:T(8,128)}), f32[64,9216]{1,0:T(8,128)}) %all-reduce.4.cloned.1.call-update) | async-done | bytes 2359312 | tf_op jit(solution)/shard_map/psum | solution.py:31
  218.5 0.0 copy-done
  218.5 7.9 %fusion.15 = (f32[128]{0:T(128)S(1)}, f32[128,9216]{1,0:T(8,128)}) fusion(f32[64,9216]{1,0:T(8,128)} %all-reduce.4.cloned.1.call-done, s32[64,9216]{1,0:T(8,128)S(1)} %copy-done, f32[64]{0:T(128)S(1)} %div.16, s32[128]{0:T(128)S(1)} %copy-done.1, f32[128,9216]{1,0:T(8,128)} %param.4, f32[128]{0:T(128)S(1)} %convert_divide_fusion.1), kind=kOutput, calls=%fused_computation.23 | convolution fusion | flops 911286144 | bytes 14157568 | tf_op jit(solution)/shard_map/dot_general | solution.py:33
  226.4 8.4 %psum.46 = f32[128]{0:T(128)S(1)} all-reduce(f32[128]{0:T(128)S(1)} %get-tuple-element.7), channel_id=1, replica_groups=mesh['bg'=64,'type'=4] {'type'}, use_global_device_ids=true, to_apply=%region_8.0 | all-reduce | flops 128 | bytes 1024 | tf_op jit(solution)/shard_map/psum | solution.py:22
  234.9 5.9 %fusion.1 = f32[64,9216]{1,0:T(8,128)} fusion(f32[128,9216]{1,0:T(8,128)} %get-tuple-element.8, f32[128]{0:T(128)S(1)} %convert_divide_fusion, s32[128]{0:T(128)S(1)} %copy-done.1), kind=kOutput, calls=%fused_computation.3 | convolution fusion | flops 907157504 | bytes 7078912 | tf_op jit(solution)/shard_map/dot_general | solution.py:24
  240.7 0.0 all-reduce.6.cloned.1.call-update
  240.8 189.1 %all-reduce.6.cloned.1.call-done = f32[64,9216]{1,0:T(8,128)} async-done(((f32[64,9216]{1,0:T(8,128)}), f32[64,9216]{1,0:T(8,128)}) %all-reduce.6.cloned.1.call-update) | async-done | bytes 2359312 | tf_op jit(solution)/shard_map/psum | solution.py:31
  429.9 7.9 %fusion = f32[128,9216]{1,0:T(8,128)} fusion(f32[128,9216]{1,0:T(8,128)} %get-tuple-element.8, f32[64,9216]{1,0:T(8,128)} %all-reduce.6.cloned.1.call-done, f32[128]{0:T(128)S(1)} %convert_divide_fusion, s32[64,9216]{1,0:T(8,128)S(1)} %copy-done, f32[64]{0:T(128)S(1)} %div.16, s32[128]{0:T(128)S(1)} %copy-done.1), kind=kOutput, calls=%fused_computation.1 | convolution fusion | flops 911286272 | bytes 14157056 | tf_op jit(solution)/shard_map/dot_general | solution.py:33
  (4 shorter events, 0.0 us)
Async XLA Ops:
  6.5 212.0 %all-reduce.4.cloned.1.call-start = ((), (), s32[]{:S(2)}) async-start(), calls=%async_computation | async-start | bytes 4718592 | tf_op jit(solution)/shard_map/psum | solution.py:31
  8.5 12.2 %copy-start.2 = (s32[128]{0:T(128)S(1)}, s32[128]{0:T(128)}, u32[]{:S(2)}) copy-start(s32[128]{0:T(128)} %param.5) | copy-start | bytes 1540
  8.5 12.2 %copy-start.1 = (s32[128]{0:T(128)S(1)}, s32[128]{0:T(128)}, u32[]{:S(2)}) copy-start(s32[128]{0:T(128)} %param.6) | copy-start | bytes 1540
  26.6 191.9 %copy-start = (s32[64,9216]{1,0:T(8,128)S(1)}, s32[64,9216]{1,0:T(8,128)}, u32[]{:S(2)}) copy-start(s32[64,9216]{1,0:T(8,128)} %param.7) | copy-start | bytes 7077892
  26.6 403.3 %all-reduce.6.cloned.1.call-start = ((), (), s32[]{:S(2)}) async-start(), calls=%async_computation.1 | async-start | bytes 4718592 | tf_op jit(solution)/shard_map/psum | solution.py:31
Sparse Core Ops, SparseCore 0:
  26.7 191.7 all-reduce.3
  240.9 188.9 all-reduce.5
where the time goes:
time: 446 us; the launch traced here: 445 us
  waiting for transfers between devices  251 us (56%)
  blocking collectives  147 us (33%)
  matrix products  27.6 us (6%)
  between operations  13.4 us (3%)
  other arithmetic  4.69 us (1%)
    psum x2, waiting for transfers between devices, local(): county_sum = lax.psum(partial_value, 'bg')  251 us
    psum x1, blocking collectives, local(): people = lax.psum(jnp.sum(county_member * row_goal[:, None], axis=0), 'bg')  129 us
    psum x2, blocking collectives, local(): row_sum = lax.psum(jnp.sum(weights, axis=1), 'type')  18 us
    dot_general x2, matrix products, local(): jnp.dot(county_member, factor, precision=highest, preferred_element_type=...  15.9 us
    dot_general x2, matrix products, local(): lax.dot_general(county_member, weights, contract_rows, precision=highest,...  11.8 us
  transfers between devices with their start and end apart: 2, of which 2 were waited for; matrix products, arithmetic and copies ran while one was open for 0% of the time, Pallas kernels for 0%

commit v1 on v0

v1 whole, which is shorter than its diff:
```python
import functools

import jax
import jax.numpy as jnp
from jax import lax
from jax.experimental import pallas as pl
from jax.experimental.pallas import tpu as pltpu
from jax.sharding import PartitionSpec as P

LANES = 128
SUB = 8
PLANE = 8
CHUNKS = 4
COUNT = 255
NAMES = 128
VMEM_LIMIT = 40 * 1024 * 1024
VMEM = pl.BlockSpec(memory_space=pltpu.VMEM)
SMEM = pl.BlockSpec(memory_space=pltpu.SMEM)
PARAMS = pltpu.CompilerParams(vmem_limit_bytes=VMEM_LIMIT)


def f32(*shape):
    return jax.ShapeDtypeStruct(shape, jnp.float32)


def tile(t):
    return pl.ds(t * LANES, LANES)


def rows_of(b):
    return pl.ds(pl.multiple_of(b * SUB, SUB), SUB)


def column(row):
    return jnp.broadcast_to(row, (LANES, LANES)).T


def fold(parts):
    sub = lax.broadcasted_iota(jnp.int32, (SUB, LANES), 0)
    order, step = list(parts), 1
    while step < SUB:
        mask = (sub & step) == 0
        merged = []
        for a, b in zip(order[0::2], order[1::2]):
            merged.append(jnp.where(mask, a, b) + pltpu.roll(jnp.where(mask, b, a), SUB - step, 0))
        order, step = merged, 2 * step
    return order[0]


def seg_blocks(seg_ref, k):
    first = seg_ref[k]
    end = seg_ref[k + 1]
    return first >> 3, (end + 7) >> 3, seg_ref[NAMES + k]


def first_kernel(tiles, cid_ref, cid_row, goal_row, w_ref, tgt_ref, msg_ref, seg_ref, cols_ref, acc_w, acc_t):
    step = pl.program_id(0)

    @pl.when(step == 0)
    def _():
        rows = cid_ref.shape[0]

        def scan(g, n):
            c = cid_ref[g]
            new = jnp.logical_or(g == 0, c != cid_ref[jnp.maximum(g - 1, 0)])

            @pl.when(new)
            def _():
                seg_ref[n] = g
                seg_ref[NAMES + n] = c

            return n + new.astype(jnp.int32)

        n = lax.fori_loop(0, rows, scan, 0)
        seg_ref[n] = rows
        seg_ref[COUNT] = n
        cols_ref[0] = column(cid_row[...].astype(jnp.float32))
        cols_ref[1] = column(goal_row[...].astype(jnp.float32))
        acc_w[...] = jnp.zeros_like(acc_w)
        acc_t[...] = jnp.zeros_like(acc_t)

    for b in range(acc_w.shape[0] // SUB):
        rows = slice(b * SUB, (b + 1) * SUB)
        acc = acc_w[rows, :]
        for t in range(tiles):
            acc = acc + w_ref[rows, t * LANES : (t + 1) * LANES]
        acc_w[rows, :] = acc
    for b in range(tgt_ref.shape[0] // SUB):
        rows = slice(b * SUB, (b + 1) * SUB)
        acc = acc_t[rows, :]
        for t in range(tiles):
            acc = acc + tgt_ref[rows, t * LANES : (t + 1) * LANES].astype(jnp.float32)
        acc_t[rows, :] = acc

    @pl.when(step == pl.num_programs(0) - 1)
    def _():
        row_sum = jnp.sum(acc_w[...].T, axis=0, keepdims=True)
        share = jnp.sum(acc_t[...].T, axis=0, keepdims=True)
        message(msg_ref, row_sum, share)


def message(msg_ref, row_sum, share):
    sub = lax.broadcasted_iota(jnp.int32, (SUB, LANES), 0)
    block = jnp.where(sub == 0, row_sum, jnp.where(sub == 1, share, 0.0))
    for d in range(msg_ref.shape[0]):
        msg_ref[d] = block


def received(recv_ref):
    total = recv_ref[0]
    for d in range(1, recv_ref.shape[0]):
        total = total + recv_ref[d]
    return total


def sums_kernel(second, *refs):
    if second:
        seg_ref, recv_ref, goal_row, w_ref, cols_ref, r1_ref, fac_ref, send_ref, sums_ref, rcol_ref = refs
    else:
        seg_ref, recv_ref, goal_row, w_ref, cols_ref, send_ref, sums_ref, rcol_ref = refs
    tiles = w_ref.shape[1] // LANES
    half = tiles // 2
    width = tiles // CHUNKS
    rcol_ref[...] = column(goal_row[...].astype(jnp.float32) / received(recv_ref)[0:1])
    n = seg_ref[COUNT]
    sub = lax.broadcasted_iota(jnp.int32, (SUB, LANES), 0)

    def county(k, carry):
        b0, b1, c = seg_blocks(seg_ref, k)
        name = c.astype(jnp.float32)

        def persons(b, acc):
            rows = rows_of(b)
            return acc + jnp.where(cols_ref[0, rows, :] == name, cols_ref[1, rows, :], 0.0)

        people = jnp.sum(lax.fori_loop(b0, b1, persons, jnp.zeros((SUB, LANES), jnp.float32)), axis=0, keepdims=True)
        sums_ref[k, tiles : tiles + SUB, :] = jnp.where(sub == 0, people, jnp.where(sub == 1, name, 0.0))
        parts = []
        for q in range(CHUNKS):
            own = range(q * width, (q + 1) * width)
            if second:
                factor = [jnp.broadcast_to(fac_ref[k, t : t + 1, :], (SUB, LANES)) for t in own]

            def block(b, accs):
                rows = rows_of(b)
                mask = cols_ref[0, rows, :] == name
                out = []
                if second:
                    r1 = jnp.where(mask, r1_ref[rows, :], 0.0)
                    r2 = rcol_ref[rows, :]
                    for i, t in enumerate(own):
                        out.append(accs[i] + w_ref[rows, tile(t)] * r1 * factor[i] * r2)
                else:
                    r1 = jnp.where(mask, rcol_ref[rows, :], 0.0)
                    for i, t in enumerate(own):
                        out.append(accs[i] + w_ref[rows, tile(t)] * r1)
                return tuple(out)

            parts.extend(lax.fori_loop(b0, b1, block, tuple(jnp.zeros((SUB, LANES), jnp.float32) for _ in own)))
            while len(parts) >= SUB:
                at = (q + 1) * width - len(parts)
                sums_ref[k, at : at + SUB, :] = fold(parts[:SUB])
                parts = parts[SUB:]
        return carry

    lax.fori_loop(0, n, county, 0)
    for d in range(PLANE):
        h = d % 2
        for e, k in ((0, 0), (1, n - 1)):
            send_ref[d, e, 0:half, :] = sums_ref[k, h * half : (h + 1) * half, :]
            send_ref[d, e, half : half + 4, :] = sums_ref[k, tiles : tiles + 4, :]


def plane_kernel(got_ref, send_ref):
    planes, rows = send_ref.shape[:2]
    z = lax.axis_index("bg") // PLANE
    name = rows - 3
    first = got_ref[0, 0, name : name + 1, :]
    last = got_ref[PLANE - 1, 1, name : name + 1, :]
    head = jnp.zeros((rows, LANES), jnp.float32)
    tail = head
    for j in range(PLANE):
        head = head + jnp.where(got_ref[j, 0, name : name + 1, :] == first, got_ref[j, 0], 0.0)
        tail = tail + jnp.where(got_ref[j, 1, name : name + 1, :] == last, got_ref[j, 1], 0.0)
    sub = lax.broadcasted_iota(jnp.int32, (rows, LANES), 0)
    head = jnp.where(sub == name, first, head)
    tail = jnp.where(sub == name, last, tail)
    for j in range(planes):

        @pl.when(j > z)
        def _():
            send_ref[j] = tail

        @pl.when(j <= z)
        def _():
            send_ref[j] = head


def edge_kernel(got_ref, far_ref, own_ref, other_ref):
    planes, rows = far_ref.shape[:2]
    me = lax.axis_index("bg")
    z = me // PLANE
    here = me % PLANE
    name = rows - 3
    sub = lax.broadcasted_iota(jnp.int32, (rows, LANES), 0)

    for out_ref, i in ((own_ref, here), (other_ref, here ^ 1)):
        for e in range(2):
            mine = got_ref[i, e]
            county = got_ref[i, e, name : name + 1, :]
            total = mine
            for j in range(PLANE):
                side = jnp.where(j < i, 1, 0)
                hit = jnp.logical_and(got_ref[j, side, name : name + 1, :] == county, j != i)
                total = total + jnp.where(hit, got_ref[j, side], 0.0)
            for j in range(planes):
                hit = jnp.logical_and(far_ref[j, name : name + 1, :] == county, j != z)
                total = total + jnp.where(hit, far_ref[j], 0.0)
            out_ref[e] = jnp.where(sub == name, county, total)


def factors(seg_ref, recv_ref, sums_ref, own_ref, other_ref, tgt_ref, fac_ref, edge_ref, share_ref):
    tiles = tgt_ref.shape[1] // LANES
    half = tiles // 2
    core = lax.axis_index("bg") % 2
    n = seg_ref[COUNT]
    share = received(recv_ref)[1:2]
    lane = lax.broadcasted_iota(jnp.int32, (1, LANES), 1)
    sub = lax.broadcasted_iota(jnp.int32, (SUB, LANES), 0)

    for mine, left_ref, right_ref in ((0, own_ref, other_ref), (1, other_ref, own_ref)):

        @pl.when(core == mine)
        def _():
            for e in range(2):
                edge_ref[e, 0:half, :] = left_ref[e, 0:half, :]
                edge_ref[e, half:tiles, :] = right_ref[e, 0:half, :]
                edge_ref[e, tiles : tiles + 4, :] = left_ref[e, half : half + 4, :]

    def factor(k, total_ref):
        c = seg_ref[NAMES + k]
        rows = rows_of(c >> 3)
        mask = sub == (c & 7)
        for t in range(0, tiles, SUB):
            parts = [jnp.where(mask, tgt_ref[rows, tile(t + i)].astype(jnp.float32), 0.0) for i in range(SUB)]
            share_ref[t : t + SUB, :] = fold(parts)
        whole = jnp.sum(jnp.where(lane == c, share, 0.0), axis=1, keepdims=True)
        scale = total_ref[tiles : tiles + 1, :] / whole
        fac_ref[k] = share_ref[...] * scale / total_ref[0:tiles, :]

    factor(0, edge_ref.at[0])
    factor(n - 1, edge_ref.at[1])

    @pl.loop(1, n - 1)
    def _(k):
        factor(k, sums_ref.at[k])


def rows_kernel(
    seg_ref, recv_ref, w_ref, cols_ref, r1_ref, sums_ref, own_ref, other_ref, tgt_ref, fac_ref, msg_ref, edge_ref, share_ref, acc_ref
):
    tiles = w_ref.shape[1] // LANES
    factors(seg_ref, recv_ref, sums_ref, own_ref, other_ref, tgt_ref, fac_ref, edge_ref, share_ref)
    acc_ref[...] = jnp.zeros_like(acc_ref)

    def county(k, carry):
        b0, b1, c = seg_blocks(seg_ref, k)
        name = c.astype(jnp.float32)

        def block(b, inner):
            rows = rows_of(b)
            mask = cols_ref[0, rows, :] == name
            r1 = jnp.where(mask, r1_ref[rows, :], 0.0)
            sums = [None] * 4
            for t in range(tiles):
                x = w_ref[rows, tile(t)] * r1 * fac_ref[k, t : t + 1, :]
                sums[t % 4] = x if sums[t % 4] is None else sums[t % 4] + x
            acc_ref[rows, :] += (sums[0] + sums[1]) + (sums[2] + sums[3])
            return inner

        return lax.fori_loop(b0, b1, block, carry)

    lax.fori_loop(0, seg_ref[COUNT], county, 0)
    message(msg_ref, jnp.sum(acc_ref[...].T, axis=0, keepdims=True), jnp.zeros((1, LANES), jnp.float32))


def last_kernel(
    tiles_here, seg_ref, recv_ref, w_ref, cols_ref, r1_ref, r2_ref, fac_ref, sums_ref, own_ref, other_ref, tgt_ref, out_ref, fac2_ref, edge_ref, share_ref
):
    step = pl.program_id(0)

    @pl.when(step == 0)
    def _():
        factors(seg_ref, recv_ref, sums_ref, own_ref, other_ref, tgt_ref, fac2_ref, edge_ref, share_ref)

    base = step * tiles_here

    def county(k, carry):
        b0, b1, c = seg_blocks(seg_ref, k)
        name = c.astype(jnp.float32)
        one = [jnp.broadcast_to(fac_ref[k, pl.ds(base + t, 1), :], (SUB, LANES)) for t in range(tiles_here)]
        two = [jnp.broadcast_to(100.0 * fac2_ref[k, pl.ds(base + t, 1), :], (SUB, LANES)) for t in range(tiles_here)]

        def block(b, inner):
            rows = rows_of(b)
            mask = cols_ref[0, rows, :] == name
            r1 = r1_ref[rows, :]
            r2 = r2_ref[rows, :]
            for t in range(tiles_here):
                x = w_ref[rows, tile(t)] * r1 * one[t] * r2 * two[t]
                pltpu.store(out_ref.at[rows, tile(t)], x, mask=mask)
            return inner

        return lax.fori_loop(b0, b1, block, carry)

    lax.fori_loop(0, seg_ref[COUNT], county, 0)


def local(planes, parts, seed_slab, row_target, county_id, county_target):
    rows, width = seed_slab.shape
    counties = county_target.shape[0]
    tiles = width // LANES
    half_rows = tiles // 2 + 4
    cid_row = county_id.reshape(1, rows)
    goal_row = row_target.reshape(1, rows)
    block = width // CHUNKS

    def whole(*shape):
        return pl.BlockSpec(shape, lambda i: (0,) * len(shape))

    msg, seg, cols = pl.pallas_call(
        functools.partial(first_kernel, block // LANES),
        grid=(CHUNKS,),
        out_shape=(f32(parts, SUB, LANES), jax.ShapeDtypeStruct((256,), jnp.int32), f32(2, rows, LANES)),
        in_specs=[
            SMEM,
            whole(1, rows),
            whole(1, rows),
            pl.BlockSpec((rows, block), lambda i: (0, i)),
            pl.BlockSpec((counties, block), lambda i: (0, i)),
        ],
        out_specs=(whole(parts, SUB, LANES), SMEM, whole(2, rows, LANES)),
        scratch_shapes=[pltpu.VMEM((rows, LANES), jnp.float32), pltpu.VMEM((LANES, LANES), jnp.float32)],
        compiler_params=PARAMS,
        name="row_sums",
    )(county_id, cid_row, goal_row, seed_slab, county_target)

    def over_type(x):
        return lax.all_to_all(x, "type", 0, 0)

    planes_of = [[PLANE * z + s for s in range(PLANE)] for z in range(planes)]
    lines_of = [[PLANE * z + s for z in range(planes)] for s in range(PLANE)]
    pair = [(i, i ^ 1) for i in range(planes * PLANE)]

    def edges(send):
        got = lax.all_to_all(send, "bg", 0, 0, axis_index_groups=planes_of)
        out = pl.pallas_call(
            plane_kernel,
            out_shape=f32(planes, half_rows, LANES),
            in_specs=[VMEM],
            out_specs=VMEM,
            compiler_params=PARAMS,
            name="plane_sums",
        )(got)
        far = lax.all_to_all(out, "bg", 0, 0, axis_index_groups=lines_of)
        own, other = pl.pallas_call(
            edge_kernel,
            out_shape=(f32(2, half_rows, LANES), f32(2, half_rows, LANES)),
            in_specs=[VMEM, VMEM],
            out_specs=(VMEM, VMEM),
            compiler_params=PARAMS,
            name="edge_sums",
        )(got, far)
        return own, lax.ppermute(other, "bg", pair)

    sums_shapes = (f32(PLANE, 2, half_rows, LANES), f32(counties, tiles + SUB, LANES), f32(rows, LANES))
    recv1 = over_type(msg)
    send, sums, r1 = pl.pallas_call(
        functools.partial(sums_kernel, False),
        out_shape=sums_shapes,
        in_specs=[SMEM] + [VMEM] * 4,
        out_specs=(VMEM,) * 3,
        compiler_params=PARAMS,
        name="county_sums_1",
    )(seg, recv1, goal_row, seed_slab, cols)
    own, other = edges(send)
    edge_scratch = [pltpu.VMEM((2, tiles + SUB, LANES), jnp.float32), pltpu.VMEM((tiles, LANES), jnp.float32)]
    fac, msg = pl.pallas_call(
        rows_kernel,
        out_shape=(f32(counties, tiles, LANES), f32(parts, SUB, LANES)),
        in_specs=[SMEM] + [VMEM] * 8,
        out_specs=(VMEM, VMEM),
        scratch_shapes=edge_scratch + [pltpu.VMEM((rows, LANES), jnp.float32)],
        compiler_params=PARAMS,
        name="row_sums_2",
    )(seg, recv1, seed_slab, cols, r1, sums, own, other, county_target)
    recv2 = over_type(msg)
    send, sums, r2 = pl.pallas_call(
        functools.partial(sums_kernel, True),
        out_shape=sums_shapes,
        in_specs=[SMEM] + [VMEM] * 6,
        out_specs=(VMEM,) * 3,
        compiler_params=PARAMS,
        name="county_sums_2",
    )(seg, recv2, goal_row, seed_slab, cols, r1, fac)
    own, other = edges(send)
    return pl.pallas_call(
        functools.partial(last_kernel, block // LANES),
        grid=(CHUNKS,),
        out_shape=f32(rows, width),
        in_specs=[
            SMEM,
            whole(parts, SUB, LANES),
            pl.BlockSpec((rows, block), lambda i: (0, i)),
            whole(2, rows, LANES),
            whole(rows, LANES),
            whole(rows, LANES),
            whole(counties, tiles, LANES),
            whole(counties, tiles + SUB, LANES),
            whole(2, half_rows, LANES),
            whole(2, half_rows, LANES),
            whole(counties, width),
        ],
        out_specs=pl.BlockSpec((rows, block), lambda i: (0, i)),
        scratch_shapes=[pltpu.VMEM((counties, tiles, LANES), jnp.float32)] + edge_scratch,
        compiler_params=PARAMS,
        name="fitted",
    )(seg, recv1, seed_slab, cols, r1, r2, fac, sums, own, other, county_target)


def solution(mesh):
    return jax.shard_map(
        functools.partial(local, mesh.shape["bg"] // PLANE, mesh.shape["type"]),
        mesh=mesh,
        in_specs=(P("bg", "type"), P("bg"), P("bg"), P(None, "type")),
        out_specs=P("bg", "type"),
        check_vma=False,
    )
```

time: 446 us -> 93.7 us (0.21)
  waiting for transfers between devices: 251 us -> 1.74 us
  blocking collectives: 147 us -> 68 us
  matrix products: 27.6 us -> 0 us
  between operations: 13.4 us -> 0.06 us
  Pallas kernels: 0 us -> 13.2 us
  local copies, waits for them, and re-layouts: 0.02 us -> 5.32 us
  starting transfers between devices: 0.04 us -> 5.2 us
  other arithmetic: 4.69 us -> 0 us
    psum x2 -> x0, waiting for transfers between devices: 251 us -> none  [local(): county_sum = lax.psum(partial_value, 'bg')]
    psum x3 -> x0, blocking collectives: 147 us -> none  [the longest x1 129 us: local(): people = lax.psum(jnp.sum(county_member * row_goal[:, None], axis=0), 'bg')]
    all_to_all x0 -> x6, blocking collectives: none -> 68 us  [the longest x2 27.3 us: edges(): far = lax.all_to_all(out, 'bg', 0, 0, axis_index_groups=lines_of)]
    dot_general x4 -> x0, matrix products: 27.6 us -> none  [the longest x2 15.9 us: local(): jnp.dot(county_member, factor, precision=highest, preferred_element_type=...]
    pallas_call x0 -> x9, Pallas kernels: none -> 13.2 us  [the longest x1 3.92 us: local(): pl.pallas_call(functools.partial(last_kernel, block // LANES), grid=(CHUN...]
    unnamed x6 -> x14, local copies, waits for them, and re-layouts: 0.02 us -> 5.32 us
    ppermute x0 -> x2, starting transfers between devices: none -> 5.2 us  [edges(): return (own, lax.ppermute(other, 'bg', pair))]
    reduce_sum x3 -> x0, other arithmetic: 4.66 us -> none  [the longest x1 2.64 us: local(): row_sum = lax.psum(jnp.sum(weights, axis=1), 'type')]
where the time goes in v1:
time: 93.7 us; the launch traced here: 93.5 us
  blocking collectives  68 us (73%)
  Pallas kernels  13.2 us (14%)
  local copies, waits for them, and re-layouts  5.32 us (6%)
  starting transfers between devices  5.2 us (6%)
  waiting for transfers between devices  1.74 us (2%)
    all_to_all x2, blocking collectives, edges(): far = lax.all_to_all(out, 'bg', 0, 0, axis_index_groups=lines_of)  27.3 us
    all_to_all x2, blocking collectives, edges(): got = lax.all_to_all(send, 'bg', 0, 0, axis_index_groups=planes_of)  25.1 us
    all_to_all x2, blocking collectives, over_type(): return lax.all_to_all(x, 'type', 0, 0)  15.6 us
    unnamed x14, local copies, waits for them, and re-layouts  5.32 us
    ppermute x2, starting transfers between devices, edges(): return (own, lax.ppermute(other, 'bg', pair))  5.2 us
    pallas_call x1, Pallas kernels, local(): pl.pallas_call(functools.partial(last_kernel, block // LANES), grid=(CHUN...  3.92 us
    pallas_call x1, Pallas kernels, local(): pl.pallas_call(functools.partial(first_kernel, block // LANES), grid=(CHU...  3.8 us
    pallas_call x1, Pallas kernels, local(): pl.pallas_call(functools.partial(sums_kernel, True), out_shape=sums_shape...  2.02 us
  transfers between devices with their start and end apart: 2, of which 2 were waited for; matrix products, arithmetic and copies ran while one was open for 0% of the time, Pallas kernels for 0%

profile of v1, /device:TPU:1, one launch (start us, length us, event | category | flops | bytes accessed | tf_op | source)
XLA Modules:
  0.0 93.5 jit_solution(8984776397273854192)
XLA Ops:
  0.0 2.3 %copy-done = f32[128,9216]{1,0:T(8,128)S(1)} copy-done((f32[128,9216]{1,0:T(8,128)S(1)}, f32[128,9216]{1,0:T(8,128)}, u32[]{:S(2)}) %copy-start) | copy-done | bytes 4718616
  2.3 1.7 %copy-done.2 = s32[64,9216]{1,0:T(8,128)S(1)} copy-done((s32[64,9216]{1,0:T(8,128)S(1)}, s32[64,9216]{1,0:T(8,128)}, u32[]{:S(2)}) %copy-start.2) | copy-done | bytes 2359320
  4.0 0.7 copy-done.4
  4.7 0.7 copy-done.6
  5.3 3.8 %row_sums.1 = (f32[4,8,128]{2,1,0:T(8,128)S(1)}, s32[256]{0:T(256)S(1)}, f32[2,128,128]{2,1,0:T(8,128)S(1)}) custom-call(s32[128]{0:T(128)S(1)} %copy-done.6, s32[1,128]{1,0:T(1,128)S(1)} %bitcast.5, s32[1,128]{1,0:T(1,128)S(1)} %bitcast.2, f32[128,9216]{1,0:T(8,128)S(1)} %copy-done, s32[64,9216]{1,0:T(8,128)S(1)} %copy-done.2), custom_call_target="tpu_custom_call" | custom-call | tf_op jit(solution)/shard_map/row_sums/pallas_call | solution.py:331
  9.1 9.0 %all_to_all.30.refs_1_.recv_ref = f32[4,8,128]{2,1,0:T(8,128)S(1)} all-to-all(f32[4,8,128]{2,1,0:T(8,128)S(1)} %get-tuple-element.21), channel_id=1, replica_groups=mesh['bg'=64,'type'=4] {'type'}, dimensions={0} | all-to-all | bytes 32768 | tf_op jit(solution)/shard_map/all_to_all | solution.py:349
  18.2 0.0 copy-done.5
  18.2 1.6 %county_sums_1.1 = (f32[8,2,40,128]{3,2,1,0:T(8,128)S(1)}, f32[64,80,128]{2,1,0:T(8,128)S(1)}, f32[128,128]{1,0:T(8,128)S(1)}) custom-call(s32[256]{0:T(256)S(1)} %get-tuple-element.20.refs_0_.seg_ref, f32[4,8,128]{2,1,0:T(8,128)S(1)} %all_to_all.30.refs_1_.recv_ref, s32[1,128]{1,0:T(1,128)S(1)} %bitcast.3, f32[128,9216]{1,0:T(8,128)S(1)} %copy-done.1, ...), custom_call_target="tpu_custom_call" | custom-call | tf_op jit(solution)/shard_map/county_sums_1/pallas_call | solution.py:378
  19.7 13.7 %all_to_all.31.got_ref = f32[8,2,40,128]{3,2,1,0:T(8,128)S(1)} all-to-all(f32[8,2,40,128]{3,2,1,0:T(8,128)S(1)} %get-tuple-element.25), channel_id=1, replica_groups={{0,4,8,12,16,20,24,28},{32,36,40,44,48,52,56,60},{64,68,72,76,80,84,88,..., dimensions={0} | all-to-all | bytes 655360 | tf_op jit(solution)/shard_map/all_to_all | solution.py:356
  33.4 0.1 plane_sums.2
  33.5 16.6 %all_to_all.32.far_ref = f32[8,40,128]{2,1,0:T(8,128)S(1)} all-to-all(f32[8,40,128]{2,1,0:T(8,128)S(1)} %plane_sums.2), channel_id=1, replica_groups={{0,32,64,96,128,160,192,224},{4,36,68,100,132,164,196,228},{8,40,72,104..., dimensions={0} | all-to-all | bytes 327680 | tf_op jit(solution)/shard_map/all_to_all | solution.py:365
  50.1 0.2 edge_sums.2
  50.3 2.7 %collective-permute-start = (f32[2,40,128]{2,1,0:T(8,128)S(1)}, f32[2,40,128]{2,1,0:T(8,128)S(1)}, u32[]{:S(2)}, u32[]{:S(2)}) collective-permute-start(f32[2,40,128]{2,1,0:T(8,128)S(1)} %get-tuple-element.27), channel_id=1, source_target_pairs={{0,4},{4,0},{8,12},{12,8},{16,20},{20,16},{24,28},{28,24},{32,36},... | collective-permute-start | bytes 122888 | tf_op jit(solution)/shard_map/ppermute | solution.py:374
  53.0 0.9 collective-permute-done.other_ref
  53.9 1.4 %row_sums_2.1 = (f32[64,72,128]{2,1,0:T(8,128)S(1)}, f32[4,8,128]{2,1,0:T(8,128)S(1)}) custom-call(s32[256]{0:T(256)S(1)} %get-tuple-element.20.refs_0_.seg_ref, f32[4,8,128]{2,1,0:T(8,128)S(1)} %all_to_all.30.refs_1_.recv_ref, f32[128,9216]{1,0:T(8,128)S(1)} %copy-done.1, f32[2,128,128]{2,1,0:T(8,128)S(1)} %get-tuple-element.22.refs_4_.cols_ref, ...), custom_call_target="tpu_custom_call" | custom-call | tf_op jit(solution)/shard_map/row_sums_2/pallas_call | solution.py:388
  55.3 6.6 %all_to_all.33.refs_1_ = f32[4,8,128]{2,1,0:T(8,128)S(1)} all-to-all(f32[4,8,128]{2,1,0:T(8,128)S(1)} %get-tuple-element.28), channel_id=1, replica_groups=mesh['bg'=64,'type'=4] {'type'}, dimensions={0} | all-to-all | bytes 32768 | tf_op jit(solution)/shard_map/all_to_all | solution.py:349
  61.8 2.0 %county_sums_2.1 = (f32[8,2,40,128]{3,2,1,0:T(8,128)S(1)}, f32[64,80,128]{2,1,0:T(8,128)S(1)}, f32[128,128]{1,0:T(8,128)S(1)}) custom-call(s32[256]{0:T(256)S(1)} %get-tuple-element.20.refs_0_.seg_ref, f32[4,8,128]{2,1,0:T(8,128)S(1)} %all_to_all.33.refs_1_, s32[1,128]{1,0:T(1,128)S(1)} %bitcast.4, f32[128,9216]{1,0:T(8,128)S(1)} %copy-done.1, ...), custom_call_target="tpu_custom_call" | custom-call | tf_op jit(solution)/shard_map/county_sums_2/pallas_call | solution.py:398
  63.9 11.4 %all_to_all.34.got_ref = f32[8,2,40,128]{3,2,1,0:T(8,128)S(1)} all-to-all(f32[8,2,40,128]{3,2,1,0:T(8,128)S(1)} %get-tuple-element.32), channel_id=1, replica_groups={{0,4,8,12,16,20,24,28},{32,36,40,44,48,52,56,60},{64,68,72,76,80,84,88,..., dimensions={0} | all-to-all | bytes 655360 | tf_op jit(solution)/shard_map/all_to_all | solution.py:356
  75.2 0.1 plane_sums.3
  75.3 10.7 %all_to_all.35.far_ref = f32[8,40,128]{2,1,0:T(8,128)S(1)} all-to-all(f32[8,40,128]{2,1,0:T(8,128)S(1)} %plane_sums.3), channel_id=1, replica_groups={{0,32,64,96,128,160,192,224},{4,36,68,100,132,164,196,228},{8,40,72,104..., dimensions={0} | all-to-all | bytes 327680 | tf_op jit(solution)/shard_map/all_to_all | solution.py:365
  86.1 0.2 edge_sums.3
  86.2 2.5 %collective-permute-start.1 = (f32[2,40,128]{2,1,0:T(8,128)S(1)}, f32[2,40,128]{2,1,0:T(8,128)S(1)}, u32[]{:S(2)}, u32[]{:S(2)}) collective-permute-start(f32[2,40,128]{2,1,0:T(8,128)S(1)} %get-tuple-element.34), channel_id=1, source_target_pairs={{0,4},{4,0},{8,12},{12,8},{16,20},{20,16},{24,28},{28,24},{32,36},... | collective-permute-start | bytes 122888 | tf_op jit(solution)/shard_map/ppermute | solution.py:374
  88.7 0.9 collective-permute-done.1.other_ref
  89.6 3.9 %fitted.1 = f32[128,9216]{1,0:T(8,128)} custom-call(s32[256]{0:T(256)S(1)} %get-tuple-element.20.refs_0_.seg_ref, f32[4,8,128]{2,1,0:T(8,128)S(1)} %all_to_all.30.refs_1_.recv_ref, f32[128,9216]{1,0:T(8,128)S(1)} %copy-done.1, f32[2,128,128]{2,1,0:T(8,128)S(1)} %get-tuple-element.22.refs_4_.cols_ref, f32[128,128]{1,0:T(8,128)S(1)} %get-tuple-element.23.r1_ref.refs_5_, ...), custom_call_target="tpu_custom_call" | custom-call | tf_op jit(solution)/shard_map/fitted/pallas_call | solution.py:407
  (9 shorter events, 0.0 us)
Async XLA Ops:
  0.0 2.3 %copy-start = (f32[128,9216]{1,0:T(8,128)S(1)}, f32[128,9216]{1,0:T(8,128)}, u32[]{:S(2)}) copy-start(f32[128,9216]{1,0:T(8,128)} %w_ref.5) | copy-start | bytes 14155780
  2.3 1.7 %copy-start.2 = (s32[64,9216]{1,0:T(8,128)S(1)}, s32[64,9216]{1,0:T(8,128)}, u32[]{:S(2)}) copy-start(s32[64,9216]{1,0:T(8,128)} %tgt_ref.5) | copy-start | bytes 7077892
  4.0 0.7 copy-start.4
  4.7 0.7 copy-start.6
  5.3 12.8 %copy-start.1 = (f32[128,9216]{1,0:T(8,128)S(1)}, f32[128,9216]{1,0:T(8,128)}, u32[]{:S(2)}) copy-start(f32[128,9216]{1,0:T(8,128)} %w_ref.5) | copy-start | bytes 14155780
  5.3 12.8 %copy-start.5 = (s32[128]{0:T(128)S(1)}, s32[128]{0:T(128)}, u32[]{:S(2)}) copy-start(s32[128]{0:T(128)} %param.5) | copy-start | bytes 1540
  18.2 35.7 %copy-start.3 = (s32[64,9216]{1,0:T(8,128)S(1)}, s32[64,9216]{1,0:T(8,128)}, u32[]{:S(2)}) copy-start(s32[64,9216]{1,0:T(8,128)} %tgt_ref.5) | copy-start | bytes 7077892
  50.3 3.6 %collective-permute-start = (f32[2,40,128]{2,1,0:T(8,128)S(1)}, f32[2,40,128]{2,1,0:T(8,128)S(1)}, u32[]{:S(2)}, u32[]{:S(2)}) collective-permute-start(f32[2,40,128]{2,1,0:T(8,128)S(1)} %get-tuple-element.27), channel_id=1, source_target_pairs={{0,4},{4,0},{8,12},{12,8},{16,20},{20,16},{24,28},{28,24},{32,36},... | collective-permute-start | bytes 122888 | tf_op jit(solution)/shard_map/ppermute | solution.py:374
  86.2 3.3 %collective-permute-start.1 = (f32[2,40,128]{2,1,0:T(8,128)S(1)}, f32[2,40,128]{2,1,0:T(8,128)S(1)}, u32[]{:S(2)}, u32[]{:S(2)}) collective-permute-start(f32[2,40,128]{2,1,0:T(8,128)S(1)} %get-tuple-element.34), channel_id=1, source_target_pairs={{0,4},{4,0},{8,12},{12,8},{16,20},{20,16},{24,28},{28,24},{32,36},... | collective-permute-start | bytes 122888 | tf_op jit(solution)/shard_map/ppermute | solution.py:374

commit v2 on v0

v2 whole, which is shorter than its diff:
```python
import functools

import jax
import jax.numpy as jnp
from jax import lax
from jax.experimental import pallas as pl
from jax.experimental.pallas import tpu as pltpu
from jax.sharding import PartitionSpec as P

LANES = 128
SUB = 8
PLANE = 8
COUNT = 255
NAMES = 128
VMEM = pl.BlockSpec(memory_space=pltpu.VMEM)
SMEM = pl.BlockSpec(memory_space=pltpu.SMEM)
HBM = pl.BlockSpec(memory_space=pltpu.HBM)
PARAMS = pltpu.CompilerParams(vmem_limit_bytes=32 * 1024 * 1024)


def f32(*shape):
    return jax.ShapeDtypeStruct(shape, jnp.float32)


def tile(t):
    return pl.ds(t * LANES, LANES)


def rows_of(b):
    return pl.ds(pl.multiple_of(b * SUB, SUB), SUB)


def column(row):
    return jnp.broadcast_to(row, (LANES, LANES)).T


def fold(parts):
    sub = lax.broadcasted_iota(jnp.int32, (SUB, LANES), 0)
    order, step = list(parts), 1
    while step < SUB:
        mask = (sub & step) == 0
        merged = []
        for a, b in zip(order[0::2], order[1::2]):
            merged.append(jnp.where(mask, a, b) + pltpu.roll(jnp.where(mask, b, a), SUB - step, 0))
        order, step = merged, 2 * step
    return order[0]


def seg_blocks(seg_ref, k):
    first = seg_ref[k]
    end = seg_ref[k + 1]
    return first >> 3, (end + 7) >> 3, seg_ref[NAMES + k]


def message(msg_ref, row_sum, share):
    sub = lax.broadcasted_iota(jnp.int32, (SUB, LANES), 0)
    msg_ref[...] = jnp.where(sub == 0, row_sum, jnp.where(sub == 1, share, 0.0))


def first_kernel(
    chunks, cid_hbm, cid_row_hbm, goal_row_hbm, w_hbm, tgt_hbm, msg_ref, seg_ref, cols_ref, w_ref, share_ref, cid_ref, cid_row, goal_row, tgt_ref, acc_w, acc_t, sems
):
    rows, width = w_ref.shape
    counties = tgt_ref.shape[0]
    tiles = width // LANES
    block = width // chunks
    small = [
        pltpu.make_async_copy(cid_hbm, cid_ref, sems.at[0]),
        pltpu.make_async_copy(cid_row_hbm, cid_row, sems.at[1]),
        pltpu.make_async_copy(goal_row_hbm, goal_row, sems.at[2]),
    ]
    targets = pltpu.make_async_copy(tgt_hbm, tgt_ref, sems.at[3])
    slabs = []
    for q in range(chunks):
        part = pl.ds(q * block, block)
        slabs.append(pltpu.make_async_copy(w_hbm.at[:, part], w_ref.at[:, part], sems.at[4 + q]))
    for copy in small + [targets] + slabs:
        copy.start()
    for copy in small:
        copy.wait()

    n = jnp.int32(0)
    seg_ref[0] = 0
    for g in range(rows):
        c = cid_ref[g]
        seg_ref[NAMES + n] = c
        seg_ref[n + 1] = g + 1
        if g + 1 < rows:
            n = n + (cid_ref[g + 1] != c).astype(jnp.int32)
    n = n + 1
    seg_ref[COUNT] = n
    cols_ref[0] = column(cid_row[...].astype(jnp.float32))
    cols_ref[1] = column(goal_row[...].astype(jnp.float32))
    acc_w[...] = jnp.zeros_like(acc_w)
    acc_t[...] = jnp.zeros_like(acc_t)

    targets.wait()

    @pl.loop(0, counties // SUB)
    def _(b):
        part = rows_of(b)
        accs = [jnp.zeros((SUB, LANES), jnp.float32)] * 4
        for t in range(tiles):
            accs[t % 4] = accs[t % 4] + tgt_ref[part, tile(t)].astype(jnp.float32)
        acc_t[part, :] = (accs[0] + accs[1]) + (accs[2] + accs[3])

    sub = lax.broadcasted_iota(jnp.int32, (SUB, LANES), 0)

    @pl.loop(0, n)
    def _(k):
        c = seg_ref[NAMES + k]
        part = rows_of(c >> 3)
        mask = sub == (c & 7)
        for t in range(0, tiles, SUB):
            parts = [jnp.where(mask, tgt_ref[part, tile(t + i)].astype(jnp.float32), 0.0) for i in range(SUB)]
            share_ref[k, t : t + SUB, :] = fold(parts)

    for q in range(chunks):
        slabs[q].wait()

        @pl.loop(0, rows // SUB)
        def _(b):
            part = rows_of(b)
            accs = [acc_w[part, :]] + [jnp.zeros((SUB, LANES), jnp.float32)] * 3
            for i in range(block // LANES):
                accs[i % 4] = accs[i % 4] + w_ref[part, tile(q * (block // LANES) + i)]
            acc_w[part, :] = (accs[0] + accs[1]) + (accs[2] + accs[3])

    row_sum = jnp.sum(acc_w[...].T, axis=0, keepdims=True)
    share = jnp.sum(acc_t[...].T, axis=0, keepdims=True)
    message(msg_ref, row_sum, share)


def sums_kernel(second, parts_n, *refs):
    seg_ref, refs = refs[0], refs[1:]
    msgs, refs = refs[:parts_n], refs[parts_n:]
    if second:
        w_ref, cols_ref, r1_ref, fac_ref, keep_ref, give_ref, sums_ref, rcol_ref, total_ref = refs
        chunks = 3
    else:
        w_ref, cols_ref, keep_ref, give_ref, sums_ref, rcol_ref, total_ref = refs
        chunks = 2
    tiles = w_ref.shape[1] // LANES
    half = tiles // 2
    width = tiles // chunks
    total = msgs[0][...]
    for m in msgs[1:]:
        total = total + m[...]
    total_ref[...] = total
    rcol_ref[...] = cols_ref[1] / column(total[0:1])
    n = seg_ref[COUNT]
    sub = lax.broadcasted_iota(jnp.int32, (SUB, LANES), 0)

    def county(k, carry):
        b0, b1, c = seg_blocks(seg_ref, k)
        name = c.astype(jnp.float32)
        if second:
            people = jnp.zeros((1, LANES), jnp.float32)
        else:

            def persons(b, acc):
                rows = rows_of(b)
                return acc + jnp.where(cols_ref[0, rows, :] == name, cols_ref[1, rows, :], 0.0)

            people = lax.fori_loop(b0, b1, persons, jnp.zeros((SUB, LANES), jnp.float32))
            people = jnp.sum(people, axis=0, keepdims=True)
        sums_ref[k, tiles : tiles + SUB, :] = jnp.where(sub == 0, people, jnp.where(sub == 1, name, 0.0))
        parts = []
        for q in range(chunks):
            own = range(q * width, (q + 1) * width)
            if second:
                factor = [jnp.broadcast_to(fac_ref[k, t : t + 1, :], (SUB, LANES)) for t in own]

            def block(b, accs):
                rows = rows_of(b)
                mask = cols_ref[0, rows, :] == name
                out = []
                if second:
                    r1 = jnp.where(mask, r1_ref[rows, :], 0.0)
                    r2 = rcol_ref[rows, :]
                    for i, t in enumerate(own):
                        out.append(accs[i] + w_ref[rows, tile(t)] * r1 * factor[i] * r2)
                else:
                    r1 = jnp.where(mask, rcol_ref[rows, :], 0.0)
                    for i, t in enumerate(own):
                        out.append(accs[i] + w_ref[rows, tile(t)] * r1)
                return tuple(out)

            parts.extend(lax.fori_loop(b0, b1, block, tuple(jnp.zeros((SUB, LANES), jnp.float32) for _ in own)))
            while len(parts) >= SUB:
                at = (q + 1) * width - len(parts)
                sums_ref[k, at : at + SUB, :] = fold(parts[:SUB])
                parts = parts[SUB:]
        return carry

    lax.fori_loop(0, n, county, 0)
    core = lax.axis_index("bg") % 2
    for mine in range(2):

        @pl.when(core == mine)
        def _():
            for out_ref, h in ((keep_ref, mine), (give_ref, 1 - mine)):
                for e, k in ((0, 0), (1, n - 1)):
                    out_ref[e, 0:half, :] = sums_ref[k, h * half : (h + 1) * half, :]
                    out_ref[e, half : half + 4, :] = sums_ref[k, tiles : tiles + 4, :]


def join(refs):
    rows = refs[0].shape[1]
    name = rows - 3
    sub = lax.broadcasted_iota(jnp.int32, (rows, LANES), 0)
    out = []
    for e, pick in ((0, jnp.minimum), (1, jnp.maximum)):
        names = [ref[e, name : name + 1, :] for ref in refs]
        edge = functools.reduce(pick, names)
        total = jnp.zeros((rows, LANES), jnp.float32)
        for ref, own in zip(refs, names):
            total = total + jnp.where(own == edge, ref[e], 0.0)
        out.append(jnp.where(sub == name, edge, total))
    return out


def chip_kernel(keep_ref, got_ref, chip_ref):
    head, tail = join([keep_ref, got_ref])
    chip_ref[0] = head
    chip_ref[1] = tail


def plane_kernel(*refs):
    send_ref = refs[-1]
    z = lax.axis_index("bg") // PLANE
    head, tail = join(refs[:-1])
    for j in range(send_ref.shape[0]):

        @pl.when(j > z)
        def _():
            send_ref[j] = tail

        @pl.when(j <= z)
        def _():
            send_ref[j] = head


def edge_kernel(keep_ref, got_ref, far_ref, *refs):
    chips, (own_ref, other_ref) = refs[:-2], refs[-2:]
    planes, rows = far_ref.shape[:2]
    me = lax.axis_index("bg")
    z = me // PLANE
    x = (me // 2) % (PLANE // 2)
    core = me % 2
    name = rows - 3
    sub = lax.broadcasted_iota(jnp.int32, (rows, LANES), 0)

    for mine_ref, near_ref, out_ref, side in ((keep_ref, got_ref, own_ref, core), (got_ref, keep_ref, other_ref, 1 - core)):
        for e in range(2):
            county = mine_ref[e, name : name + 1, :]
            total = mine_ref[e]

            def add(total, ref, county=county):
                return total + jnp.where(ref[name : name + 1, :] == county, ref[...], 0.0)

            total = add(total, near_ref.at[side])
            for m, chip_ref in enumerate(chips, 1):
                total = add(total, chip_ref.at[jnp.where((x ^ m) < x, 1, 0)])
            for j in range(planes):
                hit = jnp.logical_and(far_ref[j, name : name + 1, :] == county, j != z)
                total = total + jnp.where(hit, far_ref[j], 0.0)
            out_ref[e] = total


def edges_of(tiles, own_ref, other_ref, edge_ref):
    half = tiles // 2
    core = lax.axis_index("bg") % 2
    for mine, left_ref, right_ref in ((0, own_ref, other_ref), (1, other_ref, own_ref)):

        @pl.when(core == mine)
        def _():
            for e in range(2):
                edge_ref[e, 0:half, :] = left_ref[e, 0:half, :]
                edge_ref[e, half:tiles, :] = right_ref[e, 0:half, :]
                edge_ref[e, tiles : tiles + 4, :] = left_ref[e, half : half + 4, :]


def rows_kernel(
    seg_ref, total_ref, w_ref, cols_ref, r1_ref, sums_ref, own_ref, other_ref, share_ref, fac_ref, goal_ref, msg_ref, edge_ref, acc_ref
):
    tiles = w_ref.shape[1] // LANES
    n = seg_ref[COUNT]
    edges_of(tiles, own_ref, other_ref, edge_ref)
    share = total_ref[1:2, :]
    lane = lax.broadcasted_iota(jnp.int32, (1, LANES), 1)

    def factor(k, sum_ref):
        whole = jnp.sum(jnp.where(lane == seg_ref[NAMES + k], share, 0.0), axis=1, keepdims=True)
        goal = share_ref[k] * (sum_ref[tiles : tiles + 1, :] / whole)
        goal_ref[k] = goal
        fac_ref[k] = goal / sum_ref[0:tiles, :]

    factor(0, edge_ref.at[0])
    factor(n - 1, edge_ref.at[1])

    @pl.loop(1, n - 1)
    def _(k):
        factor(k, sums_ref.at[k])

    acc_ref[...] = jnp.zeros_like(acc_ref)

    def county(k, carry):
        b0, b1, c = seg_blocks(seg_ref, k)
        name = c.astype(jnp.float32)

        def block(b, inner):
            rows = rows_of(b)
            mask = cols_ref[0, rows, :] == name
            r1 = jnp.where(mask, r1_ref[rows, :], 0.0)
            sums = [None] * 4
            for t in range(tiles):
                x = w_ref[rows, tile(t)] * r1 * fac_ref[k, t : t + 1, :]
                sums[t % 4] = x if sums[t % 4] is None else sums[t % 4] + x
            acc_ref[rows, :] += (sums[0] + sums[1]) + (sums[2] + sums[3])
            return inner

        return lax.fori_loop(b0, b1, block, carry)

    lax.fori_loop(0, n, county, 0)
    message(msg_ref, jnp.sum(acc_ref[...].T, axis=0, keepdims=True), jnp.zeros((1, LANES), jnp.float32))


def last_kernel(
    chunks, seg_ref, w_ref, cols_ref, r1_ref, r2_ref, fac_ref, goal_ref, sums_ref, own_ref, other_ref, out_hbm, out_ref, fac2_ref, edge_ref, sems
):
    width = w_ref.shape[1]
    tiles = width // LANES
    here = tiles // chunks
    n = seg_ref[COUNT]
    edges_of(tiles, own_ref, other_ref, edge_ref)
    fac2_ref[0] = goal_ref[0] / edge_ref[0, 0:tiles, :]
    fac2_ref[n - 1] = goal_ref[n - 1] / edge_ref[1, 0:tiles, :]

    @pl.loop(1, n - 1)
    def _(k):
        fac2_ref[k] = goal_ref[k] / sums_ref[k, 0:tiles, :]

    copies = []
    for q in range(chunks):
        own = range(q * here, (q + 1) * here)

        def county(k, carry):
            b0, b1, c = seg_blocks(seg_ref, k)
            name = c.astype(jnp.float32)
            one = [jnp.broadcast_to(fac_ref[k, t : t + 1, :], (SUB, LANES)) for t in own]
            two = [jnp.broadcast_to(fac2_ref[k, t : t + 1, :], (SUB, LANES)) for t in own]

            def block(b, inner):
                rows = rows_of(b)
                mask = cols_ref[0, rows, :] == name
                r1 = r1_ref[rows, :]
                r2 = r2_ref[rows, :]
                for i, t in enumerate(own):
                    x = w_ref[rows, tile(t)] * r1 * one[i] * r2 * two[i] * 100.0
                    pltpu.store(out_ref.at[rows, tile(t)], x, mask=mask)
                return inner

            return lax.fori_loop(b0, b1, block, carry)

        lax.fori_loop(0, n, county, 0)
        part = pl.ds(q * here * LANES, here * LANES)
        copy = pltpu.make_async_copy(out_ref.at[:, part], out_hbm.at[:, part], sems.at[q])
        copy.start()
        copies.append(copy)
    for copy in copies:
        copy.wait()


def call(kernel, name, ins, in_specs, out_shape, out_specs=None, scratch=()):
    if out_specs is None:
        out_specs = jax.tree.map(lambda _: VMEM, out_shape)
    return pl.pallas_call(
        kernel, out_shape=out_shape, in_specs=in_specs, out_specs=out_specs, scratch_shapes=scratch, compiler_params=PARAMS, name=name
    )(*ins)


def local(planes, parts, seed_slab, row_target, county_id, county_target):
    rows, width = seed_slab.shape
    counties = county_target.shape[0]
    tiles = width // LANES
    half_rows = tiles // 2 + 4
    in_chunks, out_chunks = 8, 4
    device = planes * PLANE

    edge = f32(2, half_rows, LANES)
    table = f32(counties, tiles, LANES)
    column_of = f32(rows, LANES)
    small = f32(SUB, LANES)
    msg, seg, cols, slab, share = call(
        functools.partial(first_kernel, in_chunks),
        "row_sums_1",
        (county_id, county_id.reshape(1, rows), row_target.reshape(1, rows), seed_slab, county_target),
        [HBM] * 5,
        (small, jax.ShapeDtypeStruct((256,), jnp.int32), f32(2, rows, LANES), f32(rows, width), table),
        (VMEM, SMEM, VMEM, VMEM, VMEM),
        [
            pltpu.SMEM((rows,), jnp.int32),
            pltpu.VMEM((1, rows), jnp.int32),
            pltpu.VMEM((1, rows), jnp.int32),
            pltpu.VMEM((counties, width), jnp.int32),
            pltpu.VMEM((rows, LANES), jnp.float32),
            pltpu.VMEM((LANES, LANES), jnp.float32),
            pltpu.SemaphoreType.DMA((4 + in_chunks,)),
        ],
    )

    def swap(x, axis, size, mask):
        return lax.ppermute(x, axis, [(i, i ^ mask) for i in range(size)])

    def over_type(x):
        return [x] + [swap(x, "type", parts, m) for m in range(1, parts)]

    lines = [[PLANE * z + s for z in range(planes)] for s in range(PLANE)]

    def edges(keep, give):
        got = swap(give, "bg", device, 1)
        chip = call(chip_kernel, "chip_sums", (keep, got), [VMEM] * 2, edge)
        chips = [swap(chip, "bg", device, 2 * m) for m in range(1, PLANE // 2)]
        send = call(plane_kernel, "plane_sums", [chip] + chips, [VMEM] * (PLANE // 2), f32(planes, half_rows, LANES))
        far = lax.all_to_all(send, "bg", 0, 0, axis_index_groups=lines)
        own, other = call(edge_kernel, "edge_sums", [keep, got, far] + chips, [VMEM] * (2 + PLANE // 2), (edge, edge))
        return own, swap(other, "bg", device, 1)

    sums_shapes = (edge, edge, f32(counties, tiles + SUB, LANES), column_of, small)
    edge_scratch = pltpu.VMEM((2, tiles + SUB, LANES), jnp.float32)
    keep, give, sums, r1, total = call(
        functools.partial(sums_kernel, False, parts),
        "county_sums_1",
        [seg] + over_type(msg) + [slab, cols],
        [SMEM] + [VMEM] * (parts + 2),
        sums_shapes,
    )
    own, other = edges(keep, give)
    fac, goal, msg = call(
        rows_kernel,
        "row_sums_2",
        (seg, total, slab, cols, r1, sums, own, other, share),
        [SMEM] + [VMEM] * 8,
        (table, table, small),
        None,
        [edge_scratch, pltpu.VMEM((rows, LANES), jnp.float32)],
    )
    keep, give, sums, r2, _ = call(
        functools.partial(sums_kernel, True, parts),
        "county_sums_2",
        [seg] + over_type(msg) + [slab, cols, r1, fac],
        [SMEM] + [VMEM] * (parts + 4),
        sums_shapes,
    )
    own, other = edges(keep, give)
    return call(
        functools.partial(last_kernel, out_chunks),
        "fitted",
        (seg, slab, cols, r1, r2, fac, goal, sums, own, other),
        [SMEM] + [VMEM] * 9,
        f32(rows, width),
        HBM,
        [
            pltpu.VMEM((rows, width), jnp.float32),
            pltpu.VMEM((counties, tiles, LANES), jnp.float32),
            edge_scratch,
            pltpu.SemaphoreType.DMA((out_chunks,)),
        ],
    )


def solution(mesh):
    return jax.shard_map(
        functools.partial(local, mesh.shape["bg"] // PLANE, mesh.shape["type"]),
        mesh=mesh,
        in_specs=(P("bg", "type"), P("bg"), P("bg"), P(None, "type")),
        out_specs=P("bg", "type"),
        check_vma=False,
    )
```

time: 446 us -> 84.1 us (0.19)
  waiting for transfers between devices: 251 us -> 14.4 us
  blocking collectives: 147 us -> 27.1 us
  matrix products: 27.6 us -> 0 us
  starting transfers between devices: 0.04 us -> 24.9 us
  between operations: 13.4 us -> 0.07 us
  Pallas kernels: 0 us -> 12 us
  local copies, waits for them, and re-layouts: 0.02 us -> 5.31 us
  other arithmetic: 4.69 us -> 0 us
    psum x2 -> x0, waiting for transfers between devices: 251 us -> none  [local(): county_sum = lax.psum(partial_value, 'bg')]
    psum x3 -> x0, blocking collectives: 147 us -> none  [the longest x1 129 us: local(): people = lax.psum(jnp.sum(county_member * row_goal[:, None], axis=0), 'bg')]
    dot_general x4 -> x0, matrix products: 27.6 us -> none  [the longest x2 15.9 us: local(): jnp.dot(county_member, factor, precision=highest, preferred_element_type=...]
    all_to_all x0 -> x2, blocking collectives: none -> 27.1 us  [edges(): far = lax.all_to_all(send, 'bg', 0, 0, axis_index_groups=lines)]
    ppermute x0 -> x16, starting transfers between devices: none -> 24.9 us  [swap(): return lax.ppermute(x, axis, [(i, i ^ mask) for i in range(size)])]
    ppermute x0 -> x16, waiting for transfers between devices: none -> 14.4 us  [swap(): return lax.ppermute(x, axis, [(i, i ^ mask) for i in range(size)])]
    pallas_call x0 -> x11, Pallas kernels: none -> 12 us  [call(): pl.pallas_call(kernel, out_shape=out_shape, in_specs=in_specs, out_specs=...]
    unnamed x6 -> x8, local copies, waits for them, and re-layouts: 0.02 us -> 5.31 us
  transfers between devices with their start and end apart: 2 -> 16, of which waited for: 2 -> 12; matrix products, arithmetic and copies ran while one was open for 0% -> 0% of each run, Pallas kernels for 0% -> 0%
where the time goes in v2:
time: 84.1 us; the launch traced here: 83.8 us
  blocking collectives  27.1 us (32%)
  starting transfers between devices  24.9 us (30%)
  waiting for transfers between devices  14.4 us (17%)
  Pallas kernels  12 us (14%)
  local copies, waits for them, and re-layouts  5.31 us (6%)
    all_to_all x2, blocking collectives, edges(): far = lax.all_to_all(send, 'bg', 0, 0, axis_index_groups=lines)  27.1 us
    ppermute x16, starting transfers between devices, swap(): return lax.ppermute(x, axis, [(i, i ^ mask) for i in range(size)])  24.9 us
    ppermute x16, waiting for transfers between devices, swap(): return lax.ppermute(x, axis, [(i, i ^ mask) for i in range(size)])  14.4 us
    pallas_call x11, Pallas kernels, call(): pl.pallas_call(kernel, out_shape=out_shape, in_specs=in_specs, out_specs=...  12 us
    unnamed x8, local copies, waits for them, and re-layouts  5.31 us
  transfers between devices with their start and end apart: 16, of which 12 were waited for; matrix products, arithmetic and copies ran while one was open for 0% of the time, Pallas kernels for 0%

profile of v2, /device:TPU:1, one launch (start us, length us, event | category | flops | bytes accessed | tf_op | source)
XLA Modules:
  0.0 83.8 jit_solution(15436129157686614619)
XLA Ops:
  0.0 2.3 %copy-done = f32[128,9216]{1,0:T(8,128)S(1)} copy-done((f32[128,9216]{1,0:T(8,128)S(1)}, f32[128,9216]{1,0:T(8,128)}, u32[]{:S(2)}) %copy-start) | copy-done | bytes 4718616
  2.3 1.7 %copy-done.1 = s32[64,9216]{1,0:T(8,128)S(1)} copy-done((s32[64,9216]{1,0:T(8,128)S(1)}, s32[64,9216]{1,0:T(8,128)}, u32[]{:S(2)}) %copy-start.1) | copy-done | bytes 2359320
  5.3 3.0 %row_sums_1.1 = (f32[8,128]{1,0:T(8,128)S(1)}, s32[256]{0:T(256)S(1)}, f32[2,128,128]{2,1,0:T(8,128)S(1)}, f32[128,9216]{1,0:T(8,128)S(1)}, f32[64,72,128]{2,1,0:T(8,128)S(1)}) custom-call(s32[128]{0:T(128)S(1)} %copy-done.2, s32[1,128]{1,0:T(1,128)S(1)} %bitcast.2, s32[1,128]{1,0:T(1,128)S(1)} %bitcast.3, f32[128,9216]{1,0:T(8,128)S(1)} %copy-done, ...), custom_call_target="tpu_custom_call" | custom-call | tf_op jit(solution)/shard_map/row_sums_1/pallas_call | solution.py:378
  8.3 3.7 %collective-permute-start.2 = (f32[8,128]{1,0:T(8,128)S(1)}, f32[8,128]{1,0:T(8,128)S(1)}, u32[]{:S(2)}, u32[]{:S(2)}) collective-permute-start(f32[8,128]{1,0:T(8,128)S(1)} %get-tuple-element.29.refs_1_), channel_id=1, source_target_pairs={{0,3},{1,2},{2,1},{3,0},{4,7},{5,6},{6,5},{7,4},{8,11},{9,10},{10,... | collective-permute-start | bytes 12296 | tf_op jit(solution)/shard_map/ppermute | solution.py:414
  13.0 3.0 %collective-permute-done.1.refs_3_ = f32[8,128]{1,0:T(8,128)S(1)} collective-permute-done((f32[8,128]{1,0:T(8,128)S(1)}, f32[8,128]{1,0:T(8,128)S(1)}, u32[]{:S(2)}, u32[]{:S(2)}) %collective-permute-start.1) | collective-permute-done | bytes 4128 | tf_op jit(solution)/shard_map/ppermute | solution.py:414
  15.9 1.5 %county_sums_1.1 = (f32[2,40,128]{2,1,0:T(8,128)S(1)}, f32[2,40,128]{2,1,0:T(8,128)S(1)}, f32[64,80,128]{2,1,0:T(8,128)S(1)}, f32[128,128]{1,0:T(8,128)S(1)}, f32[8,128]{1,0:T(8,128)S(1)}) custom-call(s32[256]{0:T(256)S(1)} %get-tuple-element.26.refs_0_.seg_ref, f32[8,128]{1,0:T(8,128)S(1)} %get-tuple-element.29.refs_1_, ...), custom_call_target="tpu_custom_call" | custom-call | tf_op jit(solution)/shard_map/county_sums_1/pallas_call | solution.py:378
  17.4 2.2 %collective-permute-start.3 = (f32[2,40,128]{2,1,0:T(8,128)S(1)}, f32[2,40,128]{2,1,0:T(8,128)S(1)}, u32[]{:S(2)}, u32[]{:S(2)}) collective-permute-start(f32[2,40,128]{2,1,0:T(8,128)S(1)} %get-tuple-element.34), channel_id=1, source_target_pairs={{0,4},{4,0},{8,12},{12,8},{16,20},{20,16},{24,28},{28,24},{32,36},... | collective-permute-start | bytes 122888 | tf_op jit(solution)/shard_map/ppermute | solution.py:414
  19.6 0.9 %collective-permute-done.3.got_ref = f32[2,40,128]{2,1,0:T(8,128)S(1)} collective-permute-done((f32[2,40,128]{2,1,0:T(8,128)S(1)}, f32[2,40,128]{2,1,0:T(8,128)S(1)}, u32[]{:S(2)}, u32[]{:S(2)}) %collective-permute-start.3) | collective-permute-done | bytes 40992 | tf_op jit(solution)/shard_map/ppermute | solution.py:414
  20.5 2.6 %collective-permute-start.6 = (f32[2,40,128]{2,1,0:T(8,128)S(1)}, f32[2,40,128]{2,1,0:T(8,128)S(1)}, u32[]{:S(2)}, u32[]{:S(2)}) collective-permute-start(f32[2,40,128]{2,1,0:T(8,128)S(1)} %chip_sums.2.refs_0_), channel_id=1, source_target_pairs={{0,24},{4,28},{8,16},{12,20},{16,8},{20,12},{24,0},{28,4},{32,56},... | collective-permute-start | bytes 122888 | tf_op jit(solution)/shard_map/ppermute | solution.py:414
  24.7 2.8 %collective-permute-done.5.refs_2_.refs_1_ = f32[2,40,128]{2,1,0:T(8,128)S(1)} collective-permute-done((f32[2,40,128]{2,1,0:T(8,128)S(1)}, f32[2,40,128]{2,1,0:T(8,128)S(1)}, u32[]{:S(2)}, u32[]{:S(2)}) %collective-permute-start.5) | collective-permute-done | bytes 40992 | tf_op jit(solution)/shard_map/ppermute | solution.py:414
  27.5 16.4 %all_to_all.10.far_ref = f32[8,40,128]{2,1,0:T(8,128)S(1)} all-to-all(f32[8,40,128]{2,1,0:T(8,128)S(1)} %plane_sums.2), channel_id=1, replica_groups={{0,32,64,96,128,160,192,224},{4,36,68,100,132,164,196,228},{8,40,72,104..., dimensions={0} | all-to-all | bytes 327680 | tf_op jit(solution)/shard_map/all_to_all | solution.py:426
  44.0 3.6 %collective-permute-start.7 = (f32[2,40,128]{2,1,0:T(8,128)S(1)}, f32[2,40,128]{2,1,0:T(8,128)S(1)}, u32[]{:S(2)}, u32[]{:S(2)}) collective-permute-start(f32[2,40,128]{2,1,0:T(8,128)S(1)} %get-tuple-element.36), channel_id=1, source_target_pairs={{0,4},{4,0},{8,12},{12,8},{16,20},{20,16},{24,28},{28,24},{32,36},... | collective-permute-start | bytes 122888 | tf_op jit(solution)/shard_map/ppermute | solution.py:414
  48.5 1.5 %row_sums_2.1 = (f32[64,72,128]{2,1,0:T(8,128)S(1)}, f32[64,72,128]{2,1,0:T(8,128)S(1)}, f32[8,128]{1,0:T(8,128)S(1)}) custom-call(s32[256]{0:T(256)S(1)} %get-tuple-element.26.refs_0_.seg_ref, f32[8,128]{1,0:T(8,128)S(1)} %get-tuple-element.31.total_ref, f32[128,9216]{1,0:T(8,128)S(1)} %get-tuple-element.27.refs_5_.w_ref, ...), custom_call_target="tpu_custom_call" | custom-call | tf_op jit(solution)/shard_map/row_sums_2/pallas_call | solution.py:378
  50.1 1.1 %collective-permute-start.10 = (f32[8,128]{1,0:T(8,128)S(1)}, f32[8,128]{1,0:T(8,128)S(1)}, u32[]{:S(2)}, u32[]{:S(2)}) collective-permute-start(f32[8,128]{1,0:T(8,128)S(1)} %get-tuple-element.38.refs_1_), channel_id=1, source_target_pairs={{0,3},{1,2},{2,1},{3,0},{4,7},{5,6},{6,5},{7,4},{8,11},{9,10},{10,... | collective-permute-start | bytes 12296 | tf_op jit(solution)/shard_map/ppermute | solution.py:414
  52.0 1.4 %collective-permute-start.8 = (f32[8,128]{1,0:T(8,128)S(1)}, f32[8,128]{1,0:T(8,128)S(1)}, u32[]{:S(2)}, u32[]{:S(2)}) collective-permute-start(f32[8,128]{1,0:T(8,128)S(1)} %get-tuple-element.38.refs_1_), channel_id=1, source_target_pairs={{0,1},{1,0},{2,3},{3,2},{4,5},{5,4},{6,7},{7,6},{8,9},{9,8},{10,11... | collective-permute-start | bytes 12296 | tf_op jit(solution)/shard_map/ppermute | solution.py:414
  53.8 1.3 %collective-permute-done.9.refs_3_ = f32[8,128]{1,0:T(8,128)S(1)} collective-permute-done((f32[8,128]{1,0:T(8,128)S(1)}, f32[8,128]{1,0:T(8,128)S(1)}, u32[]{:S(2)}, u32[]{:S(2)}) %collective-permute-start.9) | collective-permute-done | bytes 4128 | tf_op jit(solution)/shard_map/ppermute | solution.py:414
  55.1 2.4 %county_sums_2.1 = (f32[2,40,128]{2,1,0:T(8,128)S(1)}, f32[2,40,128]{2,1,0:T(8,128)S(1)}, f32[64,80,128]{2,1,0:T(8,128)S(1)}, f32[128,128]{1,0:T(8,128)S(1)}, f32[8,128]{1,0:T(8,128)}) custom-call(s32[256]{0:T(256)S(1)} %get-tuple-element.26.refs_0_.seg_ref, f32[8,128]{1,0:T(8,128)S(1)} %get-tuple-element.38.refs_1_, ...), custom_call_target="tpu_custom_call" | custom-call | tf_op jit(solution)/shard_map/county_sums_2/pallas_call | solution.py:378
  57.6 1.8 %collective-permute-start.11 = (f32[2,40,128]{2,1,0:T(8,128)S(1)}, f32[2,40,128]{2,1,0:T(8,128)S(1)}, u32[]{:S(2)}, u32[]{:S(2)}) collective-permute-start(f32[2,40,128]{2,1,0:T(8,128)S(1)} %get-tuple-element.44), channel_id=1, source_target_pairs={{0,4},{4,0},{8,12},{12,8},{16,20},{20,16},{24,28},{28,24},{32,36},... | collective-permute-start | bytes 122888 | tf_op jit(solution)/shard_map/ppermute | solution.py:414
  60.2 1.3 %collective-permute-start.14 = (f32[2,40,128]{2,1,0:T(8,128)S(1)}, f32[2,40,128]{2,1,0:T(8,128)S(1)}, u32[]{:S(2)}, u32[]{:S(2)}) collective-permute-start(f32[2,40,128]{2,1,0:T(8,128)S(1)} %chip_sums.3.refs_0_), channel_id=1, source_target_pairs={{0,24},{4,28},{8,16},{12,20},{16,8},{20,12},{24,0},{28,4},{32,56},... | collective-permute-start | bytes 122888 | tf_op jit(solution)/shard_map/ppermute | solution.py:414
  62.2 1.4 %collective-permute-start.12 = (f32[2,40,128]{2,1,0:T(8,128)S(1)}, f32[2,40,128]{2,1,0:T(8,128)S(1)}, u32[]{:S(2)}, u32[]{:S(2)}) collective-permute-start(f32[2,40,128]{2,1,0:T(8,128)S(1)} %chip_sums.3.refs_0_), channel_id=1, source_target_pairs={{0,8},{4,12},{8,0},{12,4},{16,24},{20,28},{24,16},{28,20},{32,40},... | collective-permute-start | bytes 122888 | tf_op jit(solution)/shard_map/ppermute | solution.py:414
  64.4 1.5 %collective-permute-done.13.refs_2_.refs_1_ = f32[2,40,128]{2,1,0:T(8,128)S(1)} collective-permute-done((f32[2,40,128]{2,1,0:T(8,128)S(1)}, f32[2,40,128]{2,1,0:T(8,128)S(1)}, u32[]{:S(2)}, u32[]{:S(2)}) %collective-permute-start.13) | collective-permute-done | bytes 40992 | tf_op jit(solution)/shard_map/ppermute | solution.py:414
  66.0 10.7 %all_to_all.11.far_ref = f32[8,40,128]{2,1,0:T(8,128)S(1)} all-to-all(f32[8,40,128]{2,1,0:T(8,128)S(1)} %plane_sums.3), channel_id=1, replica_groups={{0,32,64,96,128,160,192,224},{4,36,68,100,132,164,196,228},{8,40,72,104..., dimensions={0} | all-to-all | bytes 327680 | tf_op jit(solution)/shard_map/all_to_all | solution.py:426
  76.8 3.0 %collective-permute-start.15 = (f32[2,40,128]{2,1,0:T(8,128)S(1)}, f32[2,40,128]{2,1,0:T(8,128)S(1)}, u32[]{:S(2)}, u32[]{:S(2)}) collective-permute-start(f32[2,40,128]{2,1,0:T(8,128)S(1)} %get-tuple-element.46), channel_id=1, source_target_pairs={{0,4},{4,0},{8,12},{12,8},{16,20},{20,16},{24,28},{28,24},{32,36},... | collective-permute-start | bytes 122888 | tf_op jit(solution)/shard_map/ppermute | solution.py:414
  80.7 3.1 %fitted.1 = f32[128,9216]{1,0:T(8,128)} custom-call(s32[256]{0:T(256)S(1)} %get-tuple-element.26.refs_0_.seg_ref, f32[128,9216]{1,0:T(8,128)S(1)} %get-tuple-element.27.refs_5_.w_ref, f32[2,128,128]{2,1,0:T(8,128)S(1)} %get-tuple-element.28.refs_6_.cols_ref, f32[128,128]{1,0:T(8,128)S(1)} %get-tuple-element.30.r1_ref.refs_7_, ...), custom_call_target="tpu_custom_call" | custom-call | tf_op jit(solution)/shard_map/fitted/pallas_call | solution.py:378
  (29 shorter events, 9.6 us)
Async XLA Ops:
  0.0 2.3 %copy-start = (f32[128,9216]{1,0:T(8,128)S(1)}, f32[128,9216]{1,0:T(8,128)}, u32[]{:S(2)}) copy-start(f32[128,9216]{1,0:T(8,128)} %w_hbm.1) | copy-start | bytes 14155780
  2.3 1.7 %copy-start.1 = (s32[64,9216]{1,0:T(8,128)S(1)}, s32[64,9216]{1,0:T(8,128)}, u32[]{:S(2)}) copy-start(s32[64,9216]{1,0:T(8,128)} %tgt_hbm.1) | copy-start | bytes 7077892
  4.0 0.7 copy-start.2
  4.7 0.7 copy-start.3
  8.3 4.6 %collective-permute-start.2 = (f32[8,128]{1,0:T(8,128)S(1)}, f32[8,128]{1,0:T(8,128)S(1)}, u32[]{:S(2)}, u32[]{:S(2)}) collective-permute-start(f32[8,128]{1,0:T(8,128)S(1)} %get-tuple-element.29.refs_1_), channel_id=1, source_target_pairs={{0,3},{1,2},{2,1},{3,0},{4,7},{5,6},{6,5},{7,4},{8,11},{9,10},{10,... | collective-permute-start | bytes 12296 | tf_op jit(solution)/shard_map/ppermute | solution.py:414
  12.0 4.0 %collective-permute-start.1 = (f32[8,128]{1,0:T(8,128)S(1)}, f32[8,128]{1,0:T(8,128)S(1)}, u32[]{:S(2)}, u32[]{:S(2)}) collective-permute-start(f32[8,128]{1,0:T(8,128)S(1)} %get-tuple-element.29.refs_1_), channel_id=1, source_target_pairs={{0,2},{1,3},{2,0},{3,1},{4,6},{5,7},{6,4},{7,5},{8,10},{9,11},{10,... | collective-permute-start | bytes 12296 | tf_op jit(solution)/shard_map/ppermute | solution.py:414
  12.3 3.6 %collective-permute-start = (f32[8,128]{1,0:T(8,128)S(1)}, f32[8,128]{1,0:T(8,128)S(1)}, u32[]{:S(2)}, u32[]{:S(2)}) collective-permute-start(f32[8,128]{1,0:T(8,128)S(1)} %get-tuple-element.29.refs_1_), channel_id=1, source_target_pairs={{0,1},{1,0},{2,3},{3,2},{4,5},{5,4},{6,7},{7,6},{8,9},{9,8},{10,11... | collective-permute-start | bytes 12296 | tf_op jit(solution)/shard_map/ppermute | solution.py:414
  17.4 3.1 %collective-permute-start.3 = (f32[2,40,128]{2,1,0:T(8,128)S(1)}, f32[2,40,128]{2,1,0:T(8,128)S(1)}, u32[]{:S(2)}, u32[]{:S(2)}) collective-permute-start(f32[2,40,128]{2,1,0:T(8,128)S(1)} %get-tuple-element.34), channel_id=1, source_target_pairs={{0,4},{4,0},{8,12},{12,8},{16,20},{20,16},{24,28},{28,24},{32,36},... | collective-permute-start | bytes 122888 | tf_op jit(solution)/shard_map/ppermute | solution.py:414
  20.5 4.2 %collective-permute-start.6 = (f32[2,40,128]{2,1,0:T(8,128)S(1)}, f32[2,40,128]{2,1,0:T(8,128)S(1)}, u32[]{:S(2)}, u32[]{:S(2)}) collective-permute-start(f32[2,40,128]{2,1,0:T(8,128)S(1)} %chip_sums.2.refs_0_), channel_id=1, source_target_pairs={{0,24},{4,28},{8,16},{12,20},{16,8},{20,12},{24,0},{28,4},{32,56},... | collective-permute-start | bytes 122888 | tf_op jit(solution)/shard_map/ppermute | solution.py:414
  23.1 4.4 %collective-permute-start.5 = (f32[2,40,128]{2,1,0:T(8,128)S(1)}, f32[2,40,128]{2,1,0:T(8,128)S(1)}, u32[]{:S(2)}, u32[]{:S(2)}) collective-permute-start(f32[2,40,128]{2,1,0:T(8,128)S(1)} %chip_sums.2.refs_0_), channel_id=1, source_target_pairs={{0,16},{4,20},{8,24},{12,28},{16,0},{20,4},{24,8},{28,12},{32,48},... | collective-permute-start | bytes 122888 | tf_op jit(solution)/shard_map/ppermute | solution.py:414
  23.6 3.8 %collective-permute-start.4 = (f32[2,40,128]{2,1,0:T(8,128)S(1)}, f32[2,40,128]{2,1,0:T(8,128)S(1)}, u32[]{:S(2)}, u32[]{:S(2)}) collective-permute-start(f32[2,40,128]{2,1,0:T(8,128)S(1)} %chip_sums.2.refs_0_), channel_id=1, source_target_pairs={{0,8},{4,12},{8,0},{12,4},{16,24},{20,28},{24,16},{28,20},{32,40},... | collective-permute-start | bytes 122888 | tf_op jit(solution)/shard_map/ppermute | solution.py:414
  44.0 4.5 %collective-permute-start.7 = (f32[2,40,128]{2,1,0:T(8,128)S(1)}, f32[2,40,128]{2,1,0:T(8,128)S(1)}, u32[]{:S(2)}, u32[]{:S(2)}) collective-permute-start(f32[2,40,128]{2,1,0:T(8,128)S(1)} %get-tuple-element.36), channel_id=1, source_target_pairs={{0,4},{4,0},{8,12},{12,8},{16,20},{20,16},{24,28},{28,24},{32,36},... | collective-permute-start | bytes 122888 | tf_op jit(solution)/shard_map/ppermute | solution.py:414
  50.1 3.8 %collective-permute-start.10 = (f32[8,128]{1,0:T(8,128)S(1)}, f32[8,128]{1,0:T(8,128)S(1)}, u32[]{:S(2)}, u32[]{:S(2)}) collective-permute-start(f32[8,128]{1,0:T(8,128)S(1)} %get-tuple-element.38.refs_1_), channel_id=1, source_target_pairs={{0,3},{1,2},{2,1},{3,0},{4,7},{5,6},{6,5},{7,4},{8,11},{9,10},{10,... | collective-permute-start | bytes 12296 | tf_op jit(solution)/shard_map/ppermute | solution.py:414
  51.2 4.0 %collective-permute-start.9 = (f32[8,128]{1,0:T(8,128)S(1)}, f32[8,128]{1,0:T(8,128)S(1)}, u32[]{:S(2)}, u32[]{:S(2)}) collective-permute-start(f32[8,128]{1,0:T(8,128)S(1)} %get-tuple-element.38.refs_1_), channel_id=1, source_target_pairs={{0,2},{1,3},{2,0},{3,1},{4,6},{5,7},{6,4},{7,5},{8,10},{9,11},{10,... | collective-permute-start | bytes 12296 | tf_op jit(solution)/shard_map/ppermute | solution.py:414
  52.0 3.1 %collective-permute-start.8 = (f32[8,128]{1,0:T(8,128)S(1)}, f32[8,128]{1,0:T(8,128)S(1)}, u32[]{:S(2)}, u32[]{:S(2)}) collective-permute-start(f32[8,128]{1,0:T(8,128)S(1)} %get-tuple-element.38.refs_1_), channel_id=1, source_target_pairs={{0,1},{1,0},{2,3},{3,2},{4,5},{5,4},{6,7},{7,6},{8,9},{9,8},{10,11... | collective-permute-start | bytes 12296 | tf_op jit(solution)/shard_map/ppermute | solution.py:414
  57.6 2.6 %collective-permute-start.11 = (f32[2,40,128]{2,1,0:T(8,128)S(1)}, f32[2,40,128]{2,1,0:T(8,128)S(1)}, u32[]{:S(2)}, u32[]{:S(2)}) collective-permute-start(f32[2,40,128]{2,1,0:T(8,128)S(1)} %get-tuple-element.44), channel_id=1, source_target_pairs={{0,4},{4,0},{8,12},{12,8},{16,20},{20,16},{24,28},{28,24},{32,36},... | collective-permute-start | bytes 122888 | tf_op jit(solution)/shard_map/ppermute | solution.py:414
  60.2 4.2 %collective-permute-start.14 = (f32[2,40,128]{2,1,0:T(8,128)S(1)}, f32[2,40,128]{2,1,0:T(8,128)S(1)}, u32[]{:S(2)}, u32[]{:S(2)}) collective-permute-start(f32[2,40,128]{2,1,0:T(8,128)S(1)} %chip_sums.3.refs_0_), channel_id=1, source_target_pairs={{0,24},{4,28},{8,16},{12,20},{16,8},{20,12},{24,0},{28,4},{32,56},... | collective-permute-start | bytes 122888 | tf_op jit(solution)/shard_map/ppermute | solution.py:414
  61.6 4.4 %collective-permute-start.13 = (f32[2,40,128]{2,1,0:T(8,128)S(1)}, f32[2,40,128]{2,1,0:T(8,128)S(1)}, u32[]{:S(2)}, u32[]{:S(2)}) collective-permute-start(f32[2,40,128]{2,1,0:T(8,128)S(1)} %chip_sums.3.refs_0_), channel_id=1, source_target_pairs={{0,16},{4,20},{8,24},{12,28},{16,0},{20,4},{24,8},{28,12},{32,48},... | collective-permute-start | bytes 122888 | tf_op jit(solution)/shard_map/ppermute | solution.py:414
  62.2 3.7 %collective-permute-start.12 = (f32[2,40,128]{2,1,0:T(8,128)S(1)}, f32[2,40,128]{2,1,0:T(8,128)S(1)}, u32[]{:S(2)}, u32[]{:S(2)}) collective-permute-start(f32[2,40,128]{2,1,0:T(8,128)S(1)} %chip_sums.3.refs_0_), channel_id=1, source_target_pairs={{0,8},{4,12},{8,0},{12,4},{16,24},{20,28},{24,16},{28,20},{32,40},... | collective-permute-start | bytes 122888 | tf_op jit(solution)/shard_map/ppermute | solution.py:414
  76.8 3.8 %collective-permute-start.15 = (f32[2,40,128]{2,1,0:T(8,128)S(1)}, f32[2,40,128]{2,1,0:T(8,128)S(1)}, u32[]{:S(2)}, u32[]{:S(2)}) collective-permute-start(f32[2,40,128]{2,1,0:T(8,128)S(1)} %get-tuple-element.46), channel_id=1, source_target_pairs={{0,4},{4,0},{8,12},{12,8},{16,20},{20,16},{24,28},{28,24},{32,36},... | collective-permute-start | bytes 122888 | tf_op jit(solution)/shard_map/ppermute | solution.py:414

commit v3 on v2

--- a/solution.py
+++ b/solution.py
@@ -136,7 +136,7 @@
     msgs, refs = refs[:parts_n], refs[parts_n:]
     if second:
         w_ref, cols_ref, r1_ref, fac_ref, keep_ref, give_ref, sums_ref, rcol_ref, total_ref = refs
-        chunks = 3
+        chunks = 4
     else:
         w_ref, cols_ref, keep_ref, give_ref, sums_ref, rcol_ref, total_ref = refs
         chunks = 2
@@ -395,7 +395,10 @@
     msg, seg, cols, slab, share = call(
         functools.partial(first_kernel, in_chunks),
         "row_sums_1",
-        (county_id, county_id.reshape(1, rows), row_target.reshape(1, rows), seed_slab, county_target),
+        [
+            pltpu.with_memory_space_constraint(x, pltpu.HBM)
+            for x in (county_id, county_id.reshape(1, rows), row_target.reshape(1, rows), seed_slab, county_target)
+        ],
         [HBM] * 5,
         (small, jax.ShapeDtypeStruct((256,), jnp.int32), f32(2, rows, LANES), f32(rows, width), table),
         (VMEM, SMEM, VMEM, VMEM, VMEM),

time: 84.1 us -> 79.4 us (0.944)
  local copies, waits for them, and re-layouts: 5.31 us -> 0 us
  Pallas kernels: 12 us -> 13 us
    unnamed x8 -> x0, local copies, waits for them, and re-layouts: 5.31 us -> none
    pallas_call x11, Pallas kernels: 12 us -> 13 us  [call(): pl.pallas_call(kernel, out_shape=out_shape, in_specs=in_specs, out_specs=...]
  transfers between devices with their start and end apart: 16 -> 16, of which waited for: 12 -> 13; matrix products, arithmetic and copies ran while one was open for 0% -> 0% of each run, Pallas kernels for 0% -> 0%
where the time goes in v3:
time: 79.4 us; the launch traced here: 79.3 us
  blocking collectives  27.4 us (35%)
  starting transfers between devices  24.6 us (31%)
  waiting for transfers between devices  14.2 us (18%)
  Pallas kernels  13 us (16%)
    all_to_all x2, blocking collectives, edges(): far = lax.all_to_all(send, 'bg', 0, 0, axis_index_groups=lines)  27.4 us
    ppermute x16, starting transfers between devices, swap(): return lax.ppermute(x, axis, [(i, i ^ mask) for i in range(size)])  24.6 us
    ppermute x16, waiting for transfers between devices, swap(): return lax.ppermute(x, axis, [(i, i ^ mask) for i in range(size)])  14.2 us
    pallas_call x11, Pallas kernels, call(): pl.pallas_call(kernel, out_shape=out_shape, in_specs=in_specs, out_specs=...  13 us
  transfers between devices with their start and end apart: 16, of which 13 were waited for; matrix products, arithmetic and copies ran while one was open for 0% of the time, Pallas kernels for 0%

profile of v3, /device:TPU:1, one launch (start us, length us, event | category | flops | bytes accessed | tf_op | source)
XLA Modules:
  0.0 79.3 jit_solution(10377292895472709530)
XLA Ops:
  0.0 3.9 %row_sums_1.1 = (f32[8,128]{1,0:T(8,128)S(1)}, s32[256]{0:T(256)S(1)}, f32[2,128,128]{2,1,0:T(8,128)S(1)}, f32[128,9216]{1,0:T(8,128)S(1)}, f32[64,72,128]{2,1,0:T(8,128)S(1)}) custom-call(s32[128]{0:T(128)} %cid_hbm.1, s32[1,128]{1,0:T(1,128)} %bitcast.2, s32[1,128]{1,0:T(1,128)} %bitcast.3, f32[128,9216]{1,0:T(8,128)} %w_hbm.1, s32[64,9216]{1,0:T(8,128)} %tgt_hbm.1), custom_call_target="tpu_custom_call" | custom-call | tf_op jit(solution)/shard_map/row_sums_1/pallas_call | solution.py:378
  3.9 3.7 %collective-permute-start.2 = (f32[8,128]{1,0:T(8,128)S(1)}, f32[8,128]{1,0:T(8,128)S(1)}, u32[]{:S(2)}, u32[]{:S(2)}) collective-permute-start(f32[8,128]{1,0:T(8,128)S(1)} %get-tuple-element.29.refs_1_), channel_id=1, source_target_pairs={{0,3},{1,2},{2,1},{3,0},{4,7},{5,6},{6,5},{7,4},{8,11},{9,10},{10,... | collective-permute-start | bytes 12296 | tf_op jit(solution)/shard_map/ppermute | solution.py:417
  8.5 3.0 %collective-permute-done.1.refs_3_ = f32[8,128]{1,0:T(8,128)S(1)} collective-permute-done((f32[8,128]{1,0:T(8,128)S(1)}, f32[8,128]{1,0:T(8,128)S(1)}, u32[]{:S(2)}, u32[]{:S(2)}) %collective-permute-start.1) | collective-permute-done | bytes 4128 | tf_op jit(solution)/shard_map/ppermute | solution.py:417
  11.5 1.5 %county_sums_1.1 = (f32[2,40,128]{2,1,0:T(8,128)S(1)}, f32[2,40,128]{2,1,0:T(8,128)S(1)}, f32[64,80,128]{2,1,0:T(8,128)S(1)}, f32[128,128]{1,0:T(8,128)S(1)}, f32[8,128]{1,0:T(8,128)S(1)}) custom-call(s32[256]{0:T(256)S(1)} %get-tuple-element.26.refs_0_.seg_ref, f32[8,128]{1,0:T(8,128)S(1)} %get-tuple-element.29.refs_1_, ...), custom_call_target="tpu_custom_call" | custom-call | tf_op jit(solution)/shard_map/county_sums_1/pallas_call | solution.py:378
  13.0 2.2 %collective-permute-start.3 = (f32[2,40,128]{2,1,0:T(8,128)S(1)}, f32[2,40,128]{2,1,0:T(8,128)S(1)}, u32[]{:S(2)}, u32[]{:S(2)}) collective-permute-start(f32[2,40,128]{2,1,0:T(8,128)S(1)} %get-tuple-element.34), channel_id=1, source_target_pairs={{0,4},{4,0},{8,12},{12,8},{16,20},{20,16},{24,28},{28,24},{32,36},... | collective-permute-start | bytes 122888 | tf_op jit(solution)/shard_map/ppermute | solution.py:417
  15.2 0.9 %collective-permute-done.3.got_ref = f32[2,40,128]{2,1,0:T(8,128)S(1)} collective-permute-done((f32[2,40,128]{2,1,0:T(8,128)S(1)}, f32[2,40,128]{2,1,0:T(8,128)S(1)}, u32[]{:S(2)}, u32[]{:S(2)}) %collective-permute-start.3) | collective-permute-done | bytes 40992 | tf_op jit(solution)/shard_map/ppermute | solution.py:417
  16.1 2.6 %collective-permute-start.6 = (f32[2,40,128]{2,1,0:T(8,128)S(1)}, f32[2,40,128]{2,1,0:T(8,128)S(1)}, u32[]{:S(2)}, u32[]{:S(2)}) collective-permute-start(f32[2,40,128]{2,1,0:T(8,128)S(1)} %chip_sums.2.refs_0_), channel_id=1, source_target_pairs={{0,24},{4,28},{8,16},{12,20},{16,8},{20,12},{24,0},{28,4},{32,56},... | collective-permute-start | bytes 122888 | tf_op jit(solution)/shard_map/ppermute | solution.py:417
  20.2 2.8 %collective-permute-done.5.refs_2_.refs_1_ = f32[2,40,128]{2,1,0:T(8,128)S(1)} collective-permute-done((f32[2,40,128]{2,1,0:T(8,128)S(1)}, f32[2,40,128]{2,1,0:T(8,128)S(1)}, u32[]{:S(2)}, u32[]{:S(2)}) %collective-permute-start.5) | collective-permute-done | bytes 40992 | tf_op jit(solution)/shard_map/ppermute | solution.py:417
  23.1 16.7 %all_to_all.10.far_ref = f32[8,40,128]{2,1,0:T(8,128)S(1)} all-to-all(f32[8,40,128]{2,1,0:T(8,128)S(1)} %plane_sums.2), channel_id=1, replica_groups={{0,32,64,96,128,160,192,224},{4,36,68,100,132,164,196,228},{8,40,72,104..., dimensions={0} | all-to-all | bytes 327680 | tf_op jit(solution)/shard_map/all_to_all | solution.py:429
  39.9 3.2 %collective-permute-start.7 = (f32[2,40,128]{2,1,0:T(8,128)S(1)}, f32[2,40,128]{2,1,0:T(8,128)S(1)}, u32[]{:S(2)}, u32[]{:S(2)}) collective-permute-start(f32[2,40,128]{2,1,0:T(8,128)S(1)} %get-tuple-element.36), channel_id=1, source_target_pairs={{0,4},{4,0},{8,12},{12,8},{16,20},{20,16},{24,28},{28,24},{32,36},... | collective-permute-start | bytes 122888 | tf_op jit(solution)/shard_map/ppermute | solution.py:417
  43.2 0.9 %collective-permute-done.7.other_ref = f32[2,40,128]{2,1,0:T(8,128)S(1)} collective-permute-done((f32[2,40,128]{2,1,0:T(8,128)S(1)}, f32[2,40,128]{2,1,0:T(8,128)S(1)}, u32[]{:S(2)}, u32[]{:S(2)}) %collective-permute-start.7) | collective-permute-done | bytes 40992 | tf_op jit(solution)/shard_map/ppermute | solution.py:417
  44.0 1.5 %row_sums_2.1 = (f32[64,72,128]{2,1,0:T(8,128)S(1)}, f32[64,72,128]{2,1,0:T(8,128)S(1)}, f32[8,128]{1,0:T(8,128)S(1)}) custom-call(s32[256]{0:T(256)S(1)} %get-tuple-element.26.refs_0_.seg_ref, f32[8,128]{1,0:T(8,128)S(1)} %get-tuple-element.31.total_ref, f32[128,9216]{1,0:T(8,128)S(1)} %get-tuple-element.27.refs_5_.w_ref, ...), custom_call_target="tpu_custom_call" | custom-call | tf_op jit(solution)/shard_map/row_sums_2/pallas_call | solution.py:378
  45.6 1.1 %collective-permute-start.10 = (f32[8,128]{1,0:T(8,128)S(1)}, f32[8,128]{1,0:T(8,128)S(1)}, u32[]{:S(2)}, u32[]{:S(2)}) collective-permute-start(f32[8,128]{1,0:T(8,128)S(1)} %get-tuple-element.38.refs_1_), channel_id=1, source_target_pairs={{0,3},{1,2},{2,1},{3,0},{4,7},{5,6},{6,5},{7,4},{8,11},{9,10},{10,... | collective-permute-start | bytes 12296 | tf_op jit(solution)/shard_map/ppermute | solution.py:417
  47.5 1.4 %collective-permute-start.8 = (f32[8,128]{1,0:T(8,128)S(1)}, f32[8,128]{1,0:T(8,128)S(1)}, u32[]{:S(2)}, u32[]{:S(2)}) collective-permute-start(f32[8,128]{1,0:T(8,128)S(1)} %get-tuple-element.38.refs_1_), channel_id=1, source_target_pairs={{0,1},{1,0},{2,3},{3,2},{4,5},{5,4},{6,7},{7,6},{8,9},{9,8},{10,11... | collective-permute-start | bytes 12296 | tf_op jit(solution)/shard_map/ppermute | solution.py:417
  49.4 1.3 %collective-permute-done.9.refs_3_ = f32[8,128]{1,0:T(8,128)S(1)} collective-permute-done((f32[8,128]{1,0:T(8,128)S(1)}, f32[8,128]{1,0:T(8,128)S(1)}, u32[]{:S(2)}, u32[]{:S(2)}) %collective-permute-start.9) | collective-permute-done | bytes 4128 | tf_op jit(solution)/shard_map/ppermute | solution.py:417
  50.7 2.5 %county_sums_2.1 = (f32[2,40,128]{2,1,0:T(8,128)S(1)}, f32[2,40,128]{2,1,0:T(8,128)S(1)}, f32[64,80,128]{2,1,0:T(8,128)S(1)}, f32[128,128]{1,0:T(8,128)S(1)}, f32[8,128]{1,0:T(8,128)}) custom-call(s32[256]{0:T(256)S(1)} %get-tuple-element.26.refs_0_.seg_ref, f32[8,128]{1,0:T(8,128)S(1)} %get-tuple-element.38.refs_1_, ...), custom_call_target="tpu_custom_call" | custom-call | tf_op jit(solution)/shard_map/county_sums_2/pallas_call | solution.py:378
  53.2 1.8 %collective-permute-start.11 = (f32[2,40,128]{2,1,0:T(8,128)S(1)}, f32[2,40,128]{2,1,0:T(8,128)S(1)}, u32[]{:S(2)}, u32[]{:S(2)}) collective-permute-start(f32[2,40,128]{2,1,0:T(8,128)S(1)} %get-tuple-element.44), channel_id=1, source_target_pairs={{0,4},{4,0},{8,12},{12,8},{16,20},{20,16},{24,28},{28,24},{32,36},... | collective-permute-start | bytes 122888 | tf_op jit(solution)/shard_map/ppermute | solution.py:417
  55.0 0.9 %collective-permute-done.11.got_ref = f32[2,40,128]{2,1,0:T(8,128)S(1)} collective-permute-done((f32[2,40,128]{2,1,0:T(8,128)S(1)}, f32[2,40,128]{2,1,0:T(8,128)S(1)}, u32[]{:S(2)}, u32[]{:S(2)}) %collective-permute-start.11) | collective-permute-done | bytes 40992 | tf_op jit(solution)/shard_map/ppermute | solution.py:417
  56.7 1.1 %collective-permute-start.13 = (f32[2,40,128]{2,1,0:T(8,128)S(1)}, f32[2,40,128]{2,1,0:T(8,128)S(1)}, u32[]{:S(2)}, u32[]{:S(2)}) collective-permute-start(f32[2,40,128]{2,1,0:T(8,128)S(1)} %chip_sums.3.refs_0_), channel_id=1, source_target_pairs={{0,16},{4,20},{8,24},{12,28},{16,0},{20,4},{24,8},{28,12},{32,48},... | collective-permute-start | bytes 122888 | tf_op jit(solution)/shard_map/ppermute | solution.py:417
  57.8 1.4 %collective-permute-start.12 = (f32[2,40,128]{2,1,0:T(8,128)S(1)}, f32[2,40,128]{2,1,0:T(8,128)S(1)}, u32[]{:S(2)}, u32[]{:S(2)}) collective-permute-start(f32[2,40,128]{2,1,0:T(8,128)S(1)} %chip_sums.3.refs_0_), channel_id=1, source_target_pairs={{0,8},{4,12},{8,0},{12,4},{16,24},{20,28},{24,16},{28,20},{32,40},... | collective-permute-start | bytes 122888 | tf_op jit(solution)/shard_map/ppermute | solution.py:417
  60.0 1.2 %collective-permute-done.13.refs_2_.refs_1_ = f32[2,40,128]{2,1,0:T(8,128)S(1)} collective-permute-done((f32[2,40,128]{2,1,0:T(8,128)S(1)}, f32[2,40,128]{2,1,0:T(8,128)S(1)}, u32[]{:S(2)}, u32[]{:S(2)}) %collective-permute-start.13) | collective-permute-done | bytes 40992 | tf_op jit(solution)/shard_map/ppermute | solution.py:417
  61.4 10.7 %all_to_all.11.far_ref = f32[8,40,128]{2,1,0:T(8,128)S(1)} all-to-all(f32[8,40,128]{2,1,0:T(8,128)S(1)} %plane_sums.3), channel_id=1, replica_groups={{0,32,64,96,128,160,192,224},{4,36,68,100,132,164,196,228},{8,40,72,104..., dimensions={0} | all-to-all | bytes 327680 | tf_op jit(solution)/shard_map/all_to_all | solution.py:429
  72.2 3.0 %collective-permute-start.15 = (f32[2,40,128]{2,1,0:T(8,128)S(1)}, f32[2,40,128]{2,1,0:T(8,128)S(1)}, u32[]{:S(2)}, u32[]{:S(2)}) collective-permute-start(f32[2,40,128]{2,1,0:T(8,128)S(1)} %get-tuple-element.46), channel_id=1, source_target_pairs={{0,4},{4,0},{8,12},{12,8},{16,20},{20,16},{24,28},{28,24},{32,36},... | collective-permute-start | bytes 122888 | tf_op jit(solution)/shard_map/ppermute | solution.py:417
  76.1 3.1 %fitted.1 = f32[128,9216]{1,0:T(8,128)} custom-call(s32[256]{0:T(256)S(1)} %get-tuple-element.26.refs_0_.seg_ref, f32[128,9216]{1,0:T(8,128)S(1)} %get-tuple-element.27.refs_5_.w_ref, f32[2,128,128]{2,1,0:T(8,128)S(1)} %get-tuple-element.28.refs_6_.cols_ref, f32[128,128]{1,0:T(8,128)S(1)} %get-tuple-element.30.r1_ref.refs_7_, ...), custom_call_target="tpu_custom_call" | custom-call | tf_op jit(solution)/shard_map/fitted/pallas_call | solution.py:378
  (21 shorter events, 6.9 us)
Async XLA Ops:
  3.9 4.6 %collective-permute-start.2 = (f32[8,128]{1,0:T(8,128)S(1)}, f32[8,128]{1,0:T(8,128)S(1)}, u32[]{:S(2)}, u32[]{:S(2)}) collective-permute-start(f32[8,128]{1,0:T(8,128)S(1)} %get-tuple-element.29.refs_1_), channel_id=1, source_target_pairs={{0,3},{1,2},{2,1},{3,0},{4,7},{5,6},{6,5},{7,4},{8,11},{9,10},{10,... | collective-permute-start | bytes 12296 | tf_op jit(solution)/shard_map/ppermute | solution.py:417
  7.5 4.0 %collective-permute-start.1 = (f32[8,128]{1,0:T(8,128)S(1)}, f32[8,128]{1,0:T(8,128)S(1)}, u32[]{:S(2)}, u32[]{:S(2)}) collective-permute-start(f32[8,128]{1,0:T(8,128)S(1)} %get-tuple-element.29.refs_1_), channel_id=1, source_target_pairs={{0,2},{1,3},{2,0},{3,1},{4,6},{5,7},{6,4},{7,5},{8,10},{9,11},{10,... | collective-permute-start | bytes 12296 | tf_op jit(solution)/shard_map/ppermute | solution.py:417
  7.9 3.6 %collective-permute-start = (f32[8,128]{1,0:T(8,128)S(1)}, f32[8,128]{1,0:T(8,128)S(1)}, u32[]{:S(2)}, u32[]{:S(2)}) collective-permute-start(f32[8,128]{1,0:T(8,128)S(1)} %get-tuple-element.29.refs_1_), channel_id=1, source_target_pairs={{0,1},{1,0},{2,3},{3,2},{4,5},{5,4},{6,7},{7,6},{8,9},{9,8},{10,11... | collective-permute-start | bytes 12296 | tf_op jit(solution)/shard_map/ppermute | solution.py:417
  13.0 3.1 %collective-permute-start.3 = (f32[2,40,128]{2,1,0:T(8,128)S(1)}, f32[2,40,128]{2,1,0:T(8,128)S(1)}, u32[]{:S(2)}, u32[]{:S(2)}) collective-permute-start(f32[2,40,128]{2,1,0:T(8,128)S(1)} %get-tuple-element.34), channel_id=1, source_target_pairs={{0,4},{4,0},{8,12},{12,8},{16,20},{20,16},{24,28},{28,24},{32,36},... | collective-permute-start | bytes 122888 | tf_op jit(solution)/shard_map/ppermute | solution.py:417
  16.1 4.2 %collective-permute-start.6 = (f32[2,40,128]{2,1,0:T(8,128)S(1)}, f32[2,40,128]{2,1,0:T(8,128)S(1)}, u32[]{:S(2)}, u32[]{:S(2)}) collective-permute-start(f32[2,40,128]{2,1,0:T(8,128)S(1)} %chip_sums.2.refs_0_), channel_id=1, source_target_pairs={{0,24},{4,28},{8,16},{12,20},{16,8},{20,12},{24,0},{28,4},{32,56},... | collective-permute-start | bytes 122888 | tf_op jit(solution)/shard_map/ppermute | solution.py:417
  18.6 4.4 %collective-permute-start.5 = (f32[2,40,128]{2,1,0:T(8,128)S(1)}, f32[2,40,128]{2,1,0:T(8,128)S(1)}, u32[]{:S(2)}, u32[]{:S(2)}) collective-permute-start(f32[2,40,128]{2,1,0:T(8,128)S(1)} %chip_sums.2.refs_0_), channel_id=1, source_target_pairs={{0,16},{4,20},{8,24},{12,28},{16,0},{20,4},{24,8},{28,12},{32,48},... | collective-permute-start | bytes 122888 | tf_op jit(solution)/shard_map/ppermute | solution.py:417
  19.2 3.8 %collective-permute-start.4 = (f32[2,40,128]{2,1,0:T(8,128)S(1)}, f32[2,40,128]{2,1,0:T(8,128)S(1)}, u32[]{:S(2)}, u32[]{:S(2)}) collective-permute-start(f32[2,40,128]{2,1,0:T(8,128)S(1)} %chip_sums.2.refs_0_), channel_id=1, source_target_pairs={{0,8},{4,12},{8,0},{12,4},{16,24},{20,28},{24,16},{28,20},{32,40},... | collective-permute-start | bytes 122888 | tf_op jit(solution)/shard_map/ppermute | solution.py:417
  39.9 4.1 %collective-permute-start.7 = (f32[2,40,128]{2,1,0:T(8,128)S(1)}, f32[2,40,128]{2,1,0:T(8,128)S(1)}, u32[]{:S(2)}, u32[]{:S(2)}) collective-permute-start(f32[2,40,128]{2,1,0:T(8,128)S(1)} %get-tuple-element.36), channel_id=1, source_target_pairs={{0,4},{4,0},{8,12},{12,8},{16,20},{20,16},{24,28},{28,24},{32,36},... | collective-permute-start | bytes 122888 | tf_op jit(solution)/shard_map/ppermute | solution.py:417
  45.6 3.8 %collective-permute-start.10 = (f32[8,128]{1,0:T(8,128)S(1)}, f32[8,128]{1,0:T(8,128)S(1)}, u32[]{:S(2)}, u32[]{:S(2)}) collective-permute-start(f32[8,128]{1,0:T(8,128)S(1)} %get-tuple-element.38.refs_1_), channel_id=1, source_target_pairs={{0,3},{1,2},{2,1},{3,0},{4,7},{5,6},{6,5},{7,4},{8,11},{9,10},{10,... | collective-permute-start | bytes 12296 | tf_op jit(solution)/shard_map/ppermute | solution.py:417
  46.7 4.0 %collective-permute-start.9 = (f32[8,128]{1,0:T(8,128)S(1)}, f32[8,128]{1,0:T(8,128)S(1)}, u32[]{:S(2)}, u32[]{:S(2)}) collective-permute-start(f32[8,128]{1,0:T(8,128)S(1)} %get-tuple-element.38.refs_1_), channel_id=1, source_target_pairs={{0,2},{1,3},{2,0},{3,1},{4,6},{5,7},{6,4},{7,5},{8,10},{9,11},{10,... | collective-permute-start | bytes 12296 | tf_op jit(solution)/shard_map/ppermute | solution.py:417
  47.5 3.1 %collective-permute-start.8 = (f32[8,128]{1,0:T(8,128)S(1)}, f32[8,128]{1,0:T(8,128)S(1)}, u32[]{:S(2)}, u32[]{:S(2)}) collective-permute-start(f32[8,128]{1,0:T(8,128)S(1)} %get-tuple-element.38.refs_1_), channel_id=1, source_target_pairs={{0,1},{1,0},{2,3},{3,2},{4,5},{5,4},{6,7},{7,6},{8,9},{9,8},{10,11... | collective-permute-start | bytes 12296 | tf_op jit(solution)/shard_map/ppermute | solution.py:417
  53.2 2.6 %collective-permute-start.11 = (f32[2,40,128]{2,1,0:T(8,128)S(1)}, f32[2,40,128]{2,1,0:T(8,128)S(1)}, u32[]{:S(2)}, u32[]{:S(2)}) collective-permute-start(f32[2,40,128]{2,1,0:T(8,128)S(1)} %get-tuple-element.44), channel_id=1, source_target_pairs={{0,4},{4,0},{8,12},{12,8},{16,20},{20,16},{24,28},{28,24},{32,36},... | collective-permute-start | bytes 122888 | tf_op jit(solution)/shard_map/ppermute | solution.py:417
  55.9 4.2 %collective-permute-start.14 = (f32[2,40,128]{2,1,0:T(8,128)S(1)}, f32[2,40,128]{2,1,0:T(8,128)S(1)}, u32[]{:S(2)}, u32[]{:S(2)}) collective-permute-start(f32[2,40,128]{2,1,0:T(8,128)S(1)} %chip_sums.3.refs_0_), channel_id=1, source_target_pairs={{0,24},{4,28},{8,16},{12,20},{16,8},{20,12},{24,0},{28,4},{32,56},... | collective-permute-start | bytes 122888 | tf_op jit(solution)/shard_map/ppermute | solution.py:417
  56.7 4.5 %collective-permute-start.13 = (f32[2,40,128]{2,1,0:T(8,128)S(1)}, f32[2,40,128]{2,1,0:T(8,128)S(1)}, u32[]{:S(2)}, u32[]{:S(2)}) collective-permute-start(f32[2,40,128]{2,1,0:T(8,128)S(1)} %chip_sums.3.refs_0_), channel_id=1, source_target_pairs={{0,16},{4,20},{8,24},{12,28},{16,0},{20,4},{24,8},{28,12},{32,48},... | collective-permute-start | bytes 122888 | tf_op jit(solution)/shard_map/ppermute | solution.py:417
  57.8 3.5 %collective-permute-start.12 = (f32[2,40,128]{2,1,0:T(8,128)S(1)}, f32[2,40,128]{2,1,0:T(8,128)S(1)}, u32[]{:S(2)}, u32[]{:S(2)}) collective-permute-start(f32[2,40,128]{2,1,0:T(8,128)S(1)} %chip_sums.3.refs_0_), channel_id=1, source_target_pairs={{0,8},{4,12},{8,0},{12,4},{16,24},{20,28},{24,16},{28,20},{32,40},... | collective-permute-start | bytes 122888 | tf_op jit(solution)/shard_map/ppermute | solution.py:417
  72.2 3.9 %collective-permute-start.15 = (f32[2,40,128]{2,1,0:T(8,128)S(1)}, f32[2,40,128]{2,1,0:T(8,128)S(1)}, u32[]{:S(2)}, u32[]{:S(2)}) collective-permute-start(f32[2,40,128]{2,1,0:T(8,128)S(1)} %get-tuple-element.46), channel_id=1, source_target_pairs={{0,4},{4,0},{8,12},{12,8},{16,20},{20,16},{24,28},{28,24},{32,36},... | collective-permute-start | bytes 122888 | tf_op jit(solution)/shard_map/ppermute | solution.py:417

commit v4 on v3

v4 whole, which is shorter than its diff:
```python
import functools

import jax
import jax.numpy as jnp
from jax import lax
from jax.experimental import pallas as pl
from jax.experimental.pallas import tpu as pltpu
from jax.sharding import PartitionSpec as P

LANES = 128
SUB = 8
PLANE = 8
SCALE = 2.0**40
VMEM = pl.BlockSpec(memory_space=pltpu.VMEM)
HBM = pl.BlockSpec(memory_space=pltpu.HBM)
PARAMS = pltpu.CompilerParams(vmem_limit_bytes=32 * 1024 * 1024)


def f32(*shape):
    return jax.ShapeDtypeStruct(shape, jnp.float32)


def tile(t):
    return pl.ds(t * LANES, LANES)


def rows_of(b):
    return pl.ds(pl.multiple_of(b * SUB, SUB), SUB)


def column(row):
    return jnp.broadcast_to(row, (LANES, LANES)).T


def fold(parts):
    sub = lax.broadcasted_iota(jnp.int32, (SUB, LANES), 0)
    order, step = list(parts), 1
    while step < SUB:
        mask = (sub & step) == 0
        merged = []
        for a, b in zip(order[0::2], order[1::2]):
            merged.append(jnp.where(mask, a, b) + pltpu.roll(jnp.where(mask, b, a), SUB - step, 0))
        order, step = merged, 2 * step
    return order[0]


def table_rows(counties):
    return 2 * counties + SUB


def seg_count(seg_ref):
    last = seg_ref.shape[0] - SUB
    return seg_ref[last : last + 1, :][0, 0]


def seg_range(seg_ref, k):
    row = seg_ref[pl.ds(k, 1), :]
    return row[0, 0], row[0, 1]


def seg_name(seg_ref, k):
    return seg_ref[pl.ds((seg_ref.shape[0] - SUB) // 2 + k, 1), :]


def message(msg_ref, row_sum, share):
    sub = lax.broadcasted_iota(jnp.int32, (SUB, LANES), 0)
    msg_ref[...] = jnp.where(sub == 0, row_sum, jnp.where(sub == 1, share, 0.0))


def first_kernel(
    chunks, cid_hbm, cid_row_hbm, goal_row_hbm, w_hbm, tgt_hbm, msg_ref, seg_ref, cols_ref, w_ref, tgt_ref, cid_ref, cid_row, goal_row, acc_w, acc_t, sems
):
    rows = w_ref.shape[1]
    counties, width = tgt_ref.shape
    tiles = width // LANES
    block = width // chunks
    wide = chunks // 2
    small = [
        pltpu.make_async_copy(cid_hbm, cid_ref, sems.at[0]),
        pltpu.make_async_copy(cid_row_hbm, cid_row, sems.at[1]),
        pltpu.make_async_copy(goal_row_hbm, goal_row, sems.at[2]),
    ]
    slabs = []
    for q in range(chunks):
        place = w_ref.at[q // wide, :, pl.ds(q % wide * block, block)]
        slabs.append(pltpu.make_async_copy(w_hbm.at[:, pl.ds(q * block, block)], place, sems.at[3 + q]))
    for copy in small + slabs:
        copy.start()
    acc_w[...] = jnp.zeros_like(acc_w)
    acc_t[...] = jnp.zeros_like(acc_t)
    for copy in small:
        copy.wait()

    low = cid_ref[0] >> 3
    high = (cid_ref[rows - 1] >> 3) + 1

    def targets(b):
        return pltpu.make_async_copy(tgt_hbm.at[rows_of(b)], tgt_ref.at[rows_of(b)], sems.at[3 + chunks + b])

    @pl.loop(low, high)
    def _(b):
        targets(b).start()

    lane = lax.broadcasted_iota(jnp.int32, (1, LANES), 1)
    n = 0
    first = 0
    for g in range(rows):
        c = cid_ref[g]
        seg_ref[pl.ds(n, 1), :] = jnp.where(lane == 0, first, (g + SUB) // SUB)
        seg_ref[pl.ds(counties + n, 1), :] = jnp.full((1, LANES), c)
        if g + 1 < rows:
            new = cid_ref[g + 1] != c
            n = n + new.astype(jnp.int32)
            first = jnp.where(new, (g + 1) // SUB, first)
    seg_ref[2 * counties : 2 * counties + SUB, :] = jnp.full((SUB, LANES), n + 1)
    cols_ref[0] = column(cid_row[...].astype(jnp.float32))
    cols_ref[1] = column(goal_row[...].astype(jnp.float32))

    for q in range(chunks):
        slabs[q].wait()

        @pl.loop(0, rows // SUB)
        def _(b):
            part = rows_of(b)
            accs = [acc_w[part, :]] + [jnp.zeros((SUB, LANES), jnp.float32)] * 3
            for i in range(block // LANES):
                accs[i % 4] = accs[i % 4] + w_ref[q // wide, part, tile(q % wide * (block // LANES) + i)]
            acc_w[part, :] = (accs[0] + accs[1]) + (accs[2] + accs[3])

    @pl.loop(low, high)
    def _(b):
        targets(b).wait()
        part = rows_of(b)
        accs = [jnp.zeros((SUB, LANES), jnp.float32)] * 4
        for t in range(tiles):
            accs[t % 4] = accs[t % 4] + tgt_ref[part, tile(t)].astype(jnp.float32)
        acc_t[part, :] = (accs[0] + accs[1]) + (accs[2] + accs[3])

    row_sum = jnp.sum(acc_w[...].T, axis=0, keepdims=True)
    share = jnp.sum(acc_t[...].T, axis=0, keepdims=True)
    message(msg_ref, row_sum, share)


def share_kernel(seg_ref, tgt_ref, share_ref):
    tiles = tgt_ref.shape[1] // LANES
    half = tiles // 2
    sub = lax.broadcasted_iota(jnp.int32, (SUB, LANES), 0)
    none = jnp.zeros((SUB, LANES), jnp.float32)

    @pl.loop(0, seg_count(seg_ref))
    def _(k):
        c = seg_name(seg_ref, k)[0, 0]
        part = rows_of(c >> 3)
        mask = sub == (c & 7)
        for h in range(2):
            own = [jnp.where(mask, tgt_ref[part, tile(h * half + t)].astype(jnp.float32), 0.0) for t in range(half)]
            own += [none] * (-half % SUB)
            for t in range(0, len(own), SUB):
                share_ref[k, h, t : t + SUB, :] = fold(own[t : t + SUB])


def side_of(mine):
    core = lax.axis_index("bg") % 2
    return core if mine else 1 - core


def sums_body(second, mine, seg_ref, w_ref, cols_ref, r1_ref, r2_ref, edge_ref, sums_ref):
    w_ref = w_ref.at[side_of(mine)]
    half = w_ref.shape[1] // LANES
    n = seg_count(seg_ref)
    sub = lax.broadcasted_iota(jnp.int32, (SUB, LANES), 0)
    none = jnp.zeros((SUB, LANES), jnp.float32)

    @pl.loop(0, n)
    def _(k):
        b0, b1 = seg_range(seg_ref, k)
        name = seg_name(seg_ref, k).astype(jnp.float32)

        def block(b, accs):
            rows = rows_of(b)
            mask = cols_ref[0, rows, :] == name
            r1 = jnp.where(mask, r1_ref[rows, :], 0.0)
            out = []
            if second:
                r2 = r2_ref[rows, :]
                for t in range(half):
                    out.append(accs[t] + w_ref[rows, tile(t)] * r1 * r2)
            else:
                for t in range(half):
                    out.append(accs[t] + w_ref[rows, tile(t)] * r1)
                out.append(accs[half] + jnp.where(mask, cols_ref[1, rows, :], 0.0))
            return tuple(out)

        parts = list(lax.fori_loop(b0, b1, block, (none,) * (half if second else half + 1)))
        if second:
            parts.append(none)
        parts.append(jnp.where(sub == 0, name, 0.0))
        parts += [none] * (-len(parts) % SUB)
        for t in range(0, len(parts), SUB):
            sums_ref[k, t : t + SUB, :] = fold(parts[t : t + SUB])

    edge_ref[0] = sums_ref[0]
    edge_ref[1] = sums_ref[n - 1]


def give_kernel(second, parts_n, *refs):
    seg_ref, refs = refs[0], refs[1:]
    msgs, refs = refs[:parts_n], refs[parts_n:]
    if second:
        w_ref, cols_ref, r1_ref, edge_ref, sums_ref, rcol_ref = refs
    else:
        _, w_ref, cols_ref, edge_ref, sums_ref, rcol_ref, total_ref = refs
        r1_ref = rcol_ref
    total = msgs[0][...]
    for m in msgs[1:]:
        total = total + m[...]
    if not second:
        total_ref[...] = total
    rcol = cols_ref[1] / column(total[0:1])
    rcol_ref[...] = rcol * SCALE if second else rcol
    sums_body(second, False, seg_ref, w_ref, cols_ref, r1_ref, rcol_ref, edge_ref, sums_ref)


def keep_kernel(second, seg_ref, w_ref, cols_ref, r1_ref, *refs):
    r2_ref = refs[0] if second else None
    edge_ref, sums_ref = refs[-2:]
    sums_body(second, True, seg_ref, w_ref, cols_ref, r1_ref, r2_ref, edge_ref, sums_ref)


def join(refs):
    rows = refs[0].shape[1]
    name = rows - 3
    sub = lax.broadcasted_iota(jnp.int32, (rows, LANES), 0)
    out = []
    for e, pick in ((0, jnp.minimum), (1, jnp.maximum)):
        names = [ref[e, name : name + 1, :] for ref in refs]
        edge = functools.reduce(pick, names)
        total = jnp.zeros((rows, LANES), jnp.float32)
        for ref, own in zip(refs, names):
            total = total + jnp.where(own == edge, ref[e], 0.0)
        out.append(jnp.where(sub == name, edge, total))
    return out


def chip_kernel(keep_ref, got_ref, chip_ref):
    head, tail = join([keep_ref, got_ref])
    chip_ref[0] = head
    chip_ref[1] = tail


def plane_kernel(*refs):
    send_ref = refs[-1]
    z = lax.axis_index("bg") // PLANE
    head, tail = join(refs[:-1])
    for j in range(send_ref.shape[0]):

        @pl.when(j > z)
        def _():
            send_ref[j] = tail

        @pl.when(j <= z)
        def _():
            send_ref[j] = head


def edge_kernel(keep_ref, got_ref, far_ref, *refs):
    chips, (own_ref, other_ref) = refs[:-2], refs[-2:]
    planes, rows = far_ref.shape[:2]
    me = lax.axis_index("bg")
    z = me // PLANE
    x = (me // 2) % (PLANE // 2)
    core = me % 2
    name = rows - 3
    sub = lax.broadcasted_iota(jnp.int32, (rows, LANES), 0)

    for mine_ref, near_ref, out_ref, side in ((keep_ref, got_ref, own_ref, core), (got_ref, keep_ref, other_ref, 1 - core)):
        for e in range(2):
            county = mine_ref[e, name : name + 1, :]
            total = mine_ref[e]

            def add(total, ref, county=county):
                return total + jnp.where(ref[name : name + 1, :] == county, ref[...], 0.0)

            total = add(total, near_ref.at[side])
            for m, chip_ref in enumerate(chips, 1):
                total = add(total, chip_ref.at[jnp.where((x ^ m) < x, 1, 0)])
            for j in range(planes):
                hit = jnp.logical_and(far_ref[j, name : name + 1, :] == county, j != z)
                total = total + jnp.where(hit, far_ref[j], 0.0)
            out_ref[e] = total


def each_sum(n, edge_ref, sums_ref, body):
    body(0, edge_ref.at[0])
    body(n - 1, edge_ref.at[1])

    @pl.loop(1, n - 1)
    def _(k):
        body(k, sums_ref.at[k])


def rows_kernel(mine, seg_ref, total_ref, w_ref, cols_ref, r1_ref, sums_ref, edge_ref, share_ref, *refs):
    if mine:
        goal_ref, acc_ref, fac_ref = refs
    else:
        part_ref, goal_ref, msg_ref, fac_ref, acc_ref = refs
    w_ref = w_ref.at[side_of(mine)]
    half = w_ref.shape[1] // LANES
    side = side_of(mine)
    n = seg_count(seg_ref)
    share = total_ref[1:2, :]
    lane = lax.broadcasted_iota(jnp.int32, (1, LANES), 1)

    def factor(k, sum_ref):
        whole = jnp.sum(jnp.where(lane == seg_name(seg_ref, k), share, 0.0), axis=1, keepdims=True)
        goal = share_ref[k, side] * (sum_ref[half : half + 1, :] / whole)
        goal_ref[k] = goal
        fac_ref[k] = goal / sum_ref[...]

    each_sum(n, edge_ref, sums_ref, factor)
    acc_ref[...] = jnp.zeros_like(acc_ref) if mine else part_ref[...]

    @pl.loop(0, n)
    def _(k):
        b0, b1 = seg_range(seg_ref, k)
        name = seg_name(seg_ref, k).astype(jnp.float32)

        @pl.loop(b0, b1)
        def _(b):
            rows = rows_of(b)
            mask = cols_ref[0, rows, :] == name
            r1 = jnp.where(mask, r1_ref[rows, :], 0.0)
            sums = [None] * 4
            for t in range(half):
                x = w_ref[rows, tile(t)] * r1 * fac_ref[k, t : t + 1, :]
                sums[t % 4] = x if sums[t % 4] is None else sums[t % 4] + x
            acc_ref[rows, :] += (sums[0] + sums[1]) + (sums[2] + sums[3])

    if not mine:
        message(msg_ref, jnp.sum(acc_ref[...].T, axis=0, keepdims=True), jnp.zeros((1, LANES), jnp.float32))


def fitted(mine, chunks, done, seg_ref, w_ref, cols_ref, r1_ref, r2_ref, goal_ref, sums_ref, edge_ref, out_ref, fac_ref):
    w_ref = w_ref.at[side_of(mine)]
    half = w_ref.shape[1] // LANES
    n = seg_count(seg_ref)

    def factor(k, sum_ref):
        fac_ref[k] = 100.0 * (goal_ref[k] / sum_ref[...])

    each_sum(n, edge_ref, sums_ref, factor)
    for q in range(chunks):
        own = range(q * half // chunks, (q + 1) * half // chunks)

        @pl.loop(0, n)
        def _(k):
            b0, b1 = seg_range(seg_ref, k)
            name = seg_name(seg_ref, k).astype(jnp.float32)
            fac = [jnp.broadcast_to(fac_ref[k, t : t + 1, :], (SUB, LANES)) for t in own]

            @pl.loop(b0, b1)
            def _(b):
                rows = rows_of(b)
                mask = cols_ref[0, rows, :] == name
                r1 = r1_ref[rows, :]
                r2 = r2_ref[rows, :]
                for i, t in enumerate(own):
                    x = w_ref[rows, tile(t)] * r1 * r2 * fac[i]
                    pltpu.store(out_ref.at[rows, tile(t)], x, mask=mask)

        done(q)


def last_own_kernel(seg_ref, w_ref, cols_ref, r1_ref, r2_ref, goal_ref, sums_ref, edge_ref, out_ref, fac_ref):
    fitted(True, 1, lambda q: None, seg_ref, w_ref, cols_ref, r1_ref, r2_ref, goal_ref, sums_ref, edge_ref, out_ref, fac_ref)


def last_kernel(
    chunks, seg_ref, w_ref, cols_ref, r1_ref, r2_ref, goal_ref, sums_ref, edge_ref, own_ref, out_hbm, out_ref, fac_ref, sems
):
    width = w_ref.shape[2]
    block = width // chunks

    def place(mine, at, size):
        start = side_of(mine) * width + at
        return out_hbm.at[:, pl.ds(pl.multiple_of(start, LANES), size)]

    copies = []
    for q in range(chunks):
        part = pl.ds(q * block, block)
        copies.append(pltpu.make_async_copy(own_ref.at[:, part], place(True, q * block, block), sems.at[chunks + q]))
        copies[q].start()

    def done(q):
        copy = pltpu.make_async_copy(out_ref.at[:, pl.ds(q * block, block)], place(False, q * block, block), sems.at[q])
        copy.start()
        copies.append(copy)

    fitted(False, chunks, done, seg_ref, w_ref, cols_ref, r1_ref, r2_ref, goal_ref, sums_ref, edge_ref, out_ref, fac_ref)
    for copy in copies:
        copy.wait()


def call(kernel, name, ins, in_specs, out_shape, out_specs=None, scratch=()):
    if out_specs is None:
        out_specs = jax.tree.map(lambda _: VMEM, out_shape)
    return pl.pallas_call(
        kernel,
        out_shape=out_shape,
        in_specs=in_specs,
        out_specs=out_specs,
        scratch_shapes=scratch,
        compiler_params=PARAMS,
        cost_estimate=pl.CostEstimate(flops=4 << 20, bytes_accessed=4 << 20, transcendentals=0),
        name=name,
    )(*ins)


def local(planes, parts, seed_slab, row_target, county_id, county_target):
    rows, width = seed_slab.shape
    counties = county_target.shape[0]
    half = width // LANES // 2
    half_rows = half + 4
    in_chunks, out_chunks = 8, 2
    device = planes * PLANE

    edge = f32(2, half_rows, LANES)
    table = f32(counties, half_rows, LANES)
    column_of = f32(rows, LANES)
    small = f32(SUB, LANES)
    msg, seg, cols, slab, targets = call(
        functools.partial(first_kernel, in_chunks),
        "row_sums_1",
        [
            pltpu.with_memory_space_constraint(x, pltpu.HBM)
            for x in (county_id, county_id.reshape(1, rows), row_target.reshape(1, rows), seed_slab, county_target)
        ],
        [HBM] * 5,
        (small, jax.ShapeDtypeStruct((table_rows(counties), LANES), jnp.int32), f32(2, rows, LANES), f32(2, rows, width // 2), jax.ShapeDtypeStruct((counties, width), jnp.int32)),
        (VMEM, VMEM, VMEM, VMEM, VMEM),
        [
            pltpu.SMEM((rows,), jnp.int32),
            pltpu.VMEM((1, rows), jnp.int32),
            pltpu.VMEM((1, rows), jnp.int32),
            pltpu.VMEM((rows, LANES), jnp.float32),
            pltpu.VMEM((LANES, LANES), jnp.float32),
            pltpu.SemaphoreType.DMA((3 + in_chunks + counties // SUB,)),
        ],
    )

    def swap(x, axis, size, mask):
        return lax.ppermute(x, axis, [(i, i ^ mask) for i in range(size)])

    def over_type(x):
        return [x] + [swap(x, "type", parts, m) for m in range(1, parts)]

    lines = [[PLANE * z + s for z in range(planes)] for s in range(PLANE)]

    def edges(give, keep):
        got = swap(give, "bg", device, 1)
        keep = keep()
        chip = call(chip_kernel, "chip_sums", (keep[0], got), [VMEM] * 2, edge)
        chips = [swap(chip, "bg", device, 2 * m) for m in range(1, PLANE // 2)]
        send = call(plane_kernel, "plane_sums", [chip] + chips, [VMEM] * (PLANE // 2), f32(planes, half_rows, LANES))
        far = lax.all_to_all(send, "bg", 0, 0, axis_index_groups=lines)
        own, other = call(edge_kernel, "edge_sums", [keep[0], got, far] + chips, [VMEM] * (2 + PLANE // 2), (edge, edge))
        return own, swap(other, "bg", device, 1), keep[1]

    msgs = over_type(msg)
    share = call(share_kernel, "shares", (seg, targets), [VMEM, VMEM], f32(counties, 2, half_rows, LANES))
    give, sums_give, r1, total = call(
        functools.partial(give_kernel, False, parts),
        "county_sums_1a",
        [seg] + msgs + [share, slab, cols],
        [VMEM] * (parts + 4),
        (edge, table, column_of, small),
    )
    own, other, sums_keep = edges(
        give,
        lambda: call(functools.partial(keep_kernel, False), "county_sums_1b", (seg, slab, cols, r1), [VMEM] * 4, (edge, table)),
    )
    fac = pltpu.VMEM((counties, half_rows, LANES), jnp.float32)
    goal_keep, part = call(
        functools.partial(rows_kernel, True),
        "row_sums_2a",
        (seg, total, slab, cols, r1, sums_keep, own, share),
        [VMEM] * 8,
        (table, column_of),
        None,
        [fac],
    )
    goal_give, msg = call(
        functools.partial(rows_kernel, False),
        "row_sums_2b",
        (seg, total, slab, cols, r1, sums_give, other, share, part),
        [VMEM] * 9,
        (table, small),
        None,
        [fac, pltpu.VMEM((rows, LANES), jnp.float32)],
    )
    give, sums_give, r2 = call(
        functools.partial(give_kernel, True, parts),
        "county_sums_2a",
        [seg] + over_type(msg) + [slab, cols, r1],
        [VMEM] * (parts + 4),
        (edge, table, column_of),
    )
    own, other, sums_keep = edges(
        give,
        lambda: call(functools.partial(keep_kernel, True), "county_sums_2b", (seg, slab, cols, r1, r2), [VMEM] * 5, (edge, table)),
    )
    mine = call(
        last_own_kernel,
        "fitted_a",
        (seg, slab, cols, r1, r2, goal_keep, sums_keep, own),
        [VMEM] * 8,
        f32(rows, width // 2),
        None,
        [fac],
    )
    return call(
        functools.partial(last_kernel, out_chunks),
        "fitted_b",
        (seg, slab, cols, r1, r2, goal_give, sums_give, other, mine),
        [VMEM] * 9,
        f32(rows, width),
        HBM,
        [pltpu.VMEM((rows, width // 2), jnp.float32), fac, pltpu.SemaphoreType.DMA((2 * out_chunks,))],
    )


def solution(mesh):
    return jax.shard_map(
        functools.partial(local, mesh.shape["bg"] // PLANE, mesh.shape["type"]),
        mesh=mesh,
        in_specs=(P("bg", "type"), P("bg"), P("bg"), P(None, "type")),
        out_specs=P("bg", "type"),
        check_vma=False,
    )
```

time: 79.4 us -> 74.6 us (0.940)
  Pallas kernels: 13 us -> 9.99 us
  waiting for transfers between devices: 14.2 us -> 11.7 us
    pallas_call x11 -> x16, Pallas kernels: 13 us -> 9.99 us  [call(): pl.pallas_call(kernel, out_shape=out_shape, in_specs=in_specs, out_specs=...]
    ppermute x16, waiting for transfers between devices: 14.2 us -> 11.7 us  [swap(): return lax.ppermute(x, axis, [(i, i ^ mask) for i in range(size)])]
  transfers between devices with their start and end apart: 16 -> 16, of which waited for: 13 -> 13; matrix products, arithmetic and copies ran while one was open for 0% -> 0% of each run, Pallas kernels for 0% -> 3%
where the time goes in v4:
time: 74.6 us; the launch traced here: 73.9 us
  blocking collectives  27.6 us (37%)
  starting transfers between devices  24.5 us (33%)
  waiting for transfers between devices  11.7 us (16%)
  Pallas kernels  9.99 us (13%)
    all_to_all x2, blocking collectives, edges(): far = lax.all_to_all(send, 'bg', 0, 0, axis_index_groups=lines)  27.6 us
    ppermute x16, starting transfers between devices, swap(): return lax.ppermute(x, axis, [(i, i ^ mask) for i in range(size)])  24.5 us
    ppermute x16, waiting for transfers between devices, swap(): return lax.ppermute(x, axis, [(i, i ^ mask) for i in range(size)])  11.7 us
    pallas_call x16, Pallas kernels, call(): pl.pallas_call(kernel, out_shape=out_shape, in_specs=in_specs, out_specs=...  9.99 us
  transfers between devices with their start and end apart: 16, of which 13 were waited for; matrix products, arithmetic and copies ran while one was open for 0% of the time, Pallas kernels for 3%

profile of v4, /device:TPU:1, one launch (start us, length us, event | category | flops | bytes accessed | tf_op | source)
XLA Modules:
  0.0 73.9 jit_solution(10897105040849620199)
XLA Ops:
  0.0 2.9 %row_sums_1.1 = (f32[8,128]{1,0:T(8,128)S(1)}, s32[136,128]{1,0:T(8,128)S(1)}, f32[2,128,128]{2,1,0:T(8,128)S(1)}, f32[2,128,4608]{2,1,0:T(8,128)S(1)}, s32[64,9216]{1,0:T(8,128)S(1)}) custom-call(s32[128]{0:T(128)} %cid_hbm.1, s32[1,128]{1,0:T(1,128)} %bitcast.2, s32[1,128]{1,0:T(1,128)} %bitcast.3, f32[128,9216]{1,0:T(8,128)} %w_hbm.1, s32[64,9216]{1,0:T(8,128)} %tgt_hbm.1), custom_call_target="tpu_custom_call" | custom-call | flops 4194304 | bytes 4194304 | tf_op jit(solution)/shard_map/row_sums_1/pallas_call | solution.py:407
  2.9 3.7 %collective-permute-start.2 = (f32[8,128]{1,0:T(8,128)S(1)}, f32[8,128]{1,0:T(8,128)S(1)}, u32[]{:S(2)}, u32[]{:S(2)}) collective-permute-start(f32[8,128]{1,0:T(8,128)S(1)} %get-tuple-element.32.refs_1_), channel_id=1, source_target_pairs={{0,3},{1,2},{2,1},{3,0},{4,7},{5,6},{6,5},{7,4},{8,11},{9,10},{10,... | collective-permute-start | bytes 12296 | tf_op jit(solution)/shard_map/ppermute | solution.py:452
  7.5 3.0 %collective-permute-done.1.refs_3_ = f32[8,128]{1,0:T(8,128)S(1)} collective-permute-done((f32[8,128]{1,0:T(8,128)S(1)}, f32[8,128]{1,0:T(8,128)S(1)}, u32[]{:S(2)}, u32[]{:S(2)}) %collective-permute-start.1) | collective-permute-done | bytes 4128 | tf_op jit(solution)/shard_map/ppermute | solution.py:452
  11.1 2.2 %collective-permute-start.3 = (f32[2,40,128]{2,1,0:T(8,128)S(1)}, f32[2,40,128]{2,1,0:T(8,128)S(1)}, u32[]{:S(2)}, u32[]{:S(2)}) collective-permute-start(f32[2,40,128]{2,1,0:T(8,128)S(1)} %get-tuple-element.38), channel_id=1, source_target_pairs={{0,4},{4,0},{8,12},{12,8},{16,20},{20,16},{24,28},{28,24},{32,36},... | collective-permute-start | bytes 122888 | tf_op jit(solution)/shard_map/ppermute | solution.py:452
  14.2 2.6 %collective-permute-start.6 = (f32[2,40,128]{2,1,0:T(8,128)S(1)}, f32[2,40,128]{2,1,0:T(8,128)S(1)}, u32[]{:S(2)}, u32[]{:S(2)}) collective-permute-start(f32[2,40,128]{2,1,0:T(8,128)S(1)} %chip_sums.2.refs_0_), channel_id=1, source_target_pairs={{0,24},{4,28},{8,16},{12,20},{16,8},{20,12},{24,0},{28,4},{32,56},... | collective-permute-start | bytes 122888 | tf_op jit(solution)/shard_map/ppermute | solution.py:452
  17.5 0.8 %collective-permute-done.6.refs_3_.refs_2_ = f32[2,40,128]{2,1,0:T(8,128)S(1)} collective-permute-done((f32[2,40,128]{2,1,0:T(8,128)S(1)}, f32[2,40,128]{2,1,0:T(8,128)S(1)}, u32[]{:S(2)}, u32[]{:S(2)}) %collective-permute-start.6) | collective-permute-done | bytes 40992 | tf_op jit(solution)/shard_map/ppermute | solution.py:452
  18.3 2.8 %collective-permute-done.5.refs_2_.refs_1_ = f32[2,40,128]{2,1,0:T(8,128)S(1)} collective-permute-done((f32[2,40,128]{2,1,0:T(8,128)S(1)}, f32[2,40,128]{2,1,0:T(8,128)S(1)}, u32[]{:S(2)}, u32[]{:S(2)}) %collective-permute-start.5) | collective-permute-done | bytes 40992 | tf_op jit(solution)/shard_map/ppermute | solution.py:452
  21.2 16.6 %all_to_all.10.far_ref = f32[8,40,128]{2,1,0:T(8,128)S(1)} all-to-all(f32[8,40,128]{2,1,0:T(8,128)S(1)} %plane_sums.2), channel_id=1, replica_groups={{0,32,64,96,128,160,192,224},{4,36,68,100,132,164,196,228},{8,40,72,104..., dimensions={0} | all-to-all | bytes 327680 | tf_op jit(solution)/shard_map/all_to_all | solution.py:465
  37.9 3.2 %collective-permute-start.7 = (f32[2,40,128]{2,1,0:T(8,128)S(1)}, f32[2,40,128]{2,1,0:T(8,128)S(1)}, u32[]{:S(2)}, u32[]{:S(2)}) collective-permute-start(f32[2,40,128]{2,1,0:T(8,128)S(1)} %get-tuple-element.39), channel_id=1, source_target_pairs={{0,4},{4,0},{8,12},{12,8},{16,20},{20,16},{24,28},{28,24},{32,36},... | collective-permute-start | bytes 122888 | tf_op jit(solution)/shard_map/ppermute | solution.py:452
  42.0 0.8 %row_sums_2b.1 = (f32[64,40,128]{2,1,0:T(8,128)S(1)}, f32[8,128]{1,0:T(8,128)S(1)}) custom-call(s32[136,128]{1,0:T(8,128)S(1)} %get-tuple-element.29.seg_ref.refs_0_, f32[8,128]{1,0:T(8,128)S(1)} %get-tuple-element.35.total_ref, f32[2,128,4608]{2,1,0:T(8,128)S(1)} %get-tuple-element.30.refs_6_.w_ref.refs_5_, ...), custom_call_target="tpu_custom_call" | custom-call | flops 4194304 | bytes 4194304 | tf_op jit(solution)/shard_map/row_sums_2b/pallas_call | solution.py:407
  42.8 1.1 %collective-permute-start.10 = (f32[8,128]{1,0:T(8,128)S(1)}, f32[8,128]{1,0:T(8,128)S(1)}, u32[]{:S(2)}, u32[]{:S(2)}) collective-permute-start(f32[8,128]{1,0:T(8,128)S(1)} %get-tuple-element.43.refs_1_), channel_id=1, source_target_pairs={{0,3},{1,2},{2,1},{3,0},{4,7},{5,6},{6,5},{7,4},{8,11},{9,10},{10,... | collective-permute-start | bytes 12296 | tf_op jit(solution)/shard_map/ppermute | solution.py:452
  43.9 0.8 %collective-permute-start.9 = (f32[8,128]{1,0:T(8,128)S(1)}, f32[8,128]{1,0:T(8,128)S(1)}, u32[]{:S(2)}, u32[]{:S(2)}) collective-permute-start(f32[8,128]{1,0:T(8,128)S(1)} %get-tuple-element.43.refs_1_), channel_id=1, source_target_pairs={{0,2},{1,3},{2,0},{3,1},{4,6},{5,7},{6,4},{7,5},{8,10},{9,11},{10,... | collective-permute-start | bytes 12296 | tf_op jit(solution)/shard_map/ppermute | solution.py:452
  44.7 1.4 %collective-permute-start.8 = (f32[8,128]{1,0:T(8,128)S(1)}, f32[8,128]{1,0:T(8,128)S(1)}, u32[]{:S(2)}, u32[]{:S(2)}) collective-permute-start(f32[8,128]{1,0:T(8,128)S(1)} %get-tuple-element.43.refs_1_), channel_id=1, source_target_pairs={{0,1},{1,0},{2,3},{3,2},{4,5},{5,4},{6,7},{7,6},{8,9},{9,8},{10,11... | collective-permute-start | bytes 12296 | tf_op jit(solution)/shard_map/ppermute | solution.py:452
  46.6 1.3 %collective-permute-done.9.refs_3_ = f32[8,128]{1,0:T(8,128)S(1)} collective-permute-done((f32[8,128]{1,0:T(8,128)S(1)}, f32[8,128]{1,0:T(8,128)S(1)}, u32[]{:S(2)}, u32[]{:S(2)}) %collective-permute-start.9) | collective-permute-done | bytes 4128 | tf_op jit(solution)/shard_map/ppermute | solution.py:452
  47.9 0.7 county_sums_2a.1
  48.6 1.9 %collective-permute-start.11 = (f32[2,40,128]{2,1,0:T(8,128)S(1)}, f32[2,40,128]{2,1,0:T(8,128)S(1)}, u32[]{:S(2)}, u32[]{:S(2)}) collective-permute-start(f32[2,40,128]{2,1,0:T(8,128)S(1)} %get-tuple-element.48), channel_id=1, source_target_pairs={{0,4},{4,0},{8,12},{12,8},{16,20},{20,16},{24,28},{28,24},{32,36},... | collective-permute-start | bytes 122888 | tf_op jit(solution)/shard_map/ppermute | solution.py:452
  51.3 0.9 %collective-permute-start.14 = (f32[2,40,128]{2,1,0:T(8,128)S(1)}, f32[2,40,128]{2,1,0:T(8,128)S(1)}, u32[]{:S(2)}, u32[]{:S(2)}) collective-permute-start(f32[2,40,128]{2,1,0:T(8,128)S(1)} %chip_sums.3.refs_0_), channel_id=1, source_target_pairs={{0,24},{4,28},{8,16},{12,20},{16,8},{20,12},{24,0},{28,4},{32,56},... | collective-permute-start | bytes 122888 | tf_op jit(solution)/shard_map/ppermute | solution.py:452
  52.2 1.0 %collective-permute-start.13 = (f32[2,40,128]{2,1,0:T(8,128)S(1)}, f32[2,40,128]{2,1,0:T(8,128)S(1)}, u32[]{:S(2)}, u32[]{:S(2)}) collective-permute-start(f32[2,40,128]{2,1,0:T(8,128)S(1)} %chip_sums.3.refs_0_), channel_id=1, source_target_pairs={{0,16},{4,20},{8,24},{12,28},{16,0},{20,4},{24,8},{28,12},{32,48},... | collective-permute-start | bytes 122888 | tf_op jit(solution)/shard_map/ppermute | solution.py:452
  53.3 1.4 %collective-permute-start.12 = (f32[2,40,128]{2,1,0:T(8,128)S(1)}, f32[2,40,128]{2,1,0:T(8,128)S(1)}, u32[]{:S(2)}, u32[]{:S(2)}) collective-permute-start(f32[2,40,128]{2,1,0:T(8,128)S(1)} %chip_sums.3.refs_0_), channel_id=1, source_target_pairs={{0,8},{4,12},{8,0},{12,4},{16,24},{20,28},{24,16},{28,20},{32,40},... | collective-permute-start | bytes 122888 | tf_op jit(solution)/shard_map/ppermute | solution.py:452
  54.7 0.8 %collective-permute-done.14.refs_3_.refs_2_ = f32[2,40,128]{2,1,0:T(8,128)S(1)} collective-permute-done((f32[2,40,128]{2,1,0:T(8,128)S(1)}, f32[2,40,128]{2,1,0:T(8,128)S(1)}, u32[]{:S(2)}, u32[]{:S(2)}) %collective-permute-start.14) | collective-permute-done | bytes 40992 | tf_op jit(solution)/shard_map/ppermute | solution.py:452
  55.5 1.2 %collective-permute-done.13.refs_2_.refs_1_ = f32[2,40,128]{2,1,0:T(8,128)S(1)} collective-permute-done((f32[2,40,128]{2,1,0:T(8,128)S(1)}, f32[2,40,128]{2,1,0:T(8,128)S(1)}, u32[]{:S(2)}, u32[]{:S(2)}) %collective-permute-start.13) | collective-permute-done | bytes 40992 | tf_op jit(solution)/shard_map/ppermute | solution.py:452
  56.9 10.9 %all_to_all.11.far_ref = f32[8,40,128]{2,1,0:T(8,128)S(1)} all-to-all(f32[8,40,128]{2,1,0:T(8,128)S(1)} %plane_sums.3), channel_id=1, replica_groups={{0,32,64,96,128,160,192,224},{4,36,68,100,132,164,196,228},{8,40,72,104..., dimensions={0} | all-to-all | bytes 327680 | tf_op jit(solution)/shard_map/all_to_all | solution.py:465
  67.9 2.8 %collective-permute-start.15 = (f32[2,40,128]{2,1,0:T(8,128)S(1)}, f32[2,40,128]{2,1,0:T(8,128)S(1)}, u32[]{:S(2)}, u32[]{:S(2)}) collective-permute-start(f32[2,40,128]{2,1,0:T(8,128)S(1)} %get-tuple-element.49), channel_id=1, source_target_pairs={{0,4},{4,0},{8,12},{12,8},{16,20},{20,16},{24,28},{28,24},{32,36},... | collective-permute-start | bytes 122888 | tf_op jit(solution)/shard_map/ppermute | solution.py:452
  71.7 2.2 %fitted_b.1 = f32[128,9216]{1,0:T(8,128)} custom-call(s32[136,128]{1,0:T(8,128)S(1)} %get-tuple-element.29.seg_ref.refs_0_, f32[2,128,4608]{2,1,0:T(8,128)S(1)} %get-tuple-element.30.refs_6_.w_ref.refs_5_, f32[2,128,128]{2,1,0:T(8,128)S(1)} %get-tuple-element.31.refs_7_.cols_ref.refs_6_, f32[128,128]{1,0:T(8,128)S(1)} %get-tuple-element.34.r1_ref.refs_7_, ...), custom_call_target="tpu_custom_call" | custom-call | flops 4194304 | bytes 4194304 | tf_op jit(solution)/shard_map/fitted_b/pallas_call | solution.py:407
  (26 shorter events, 6.8 us)
Async XLA Ops:
  2.9 4.6 %collective-permute-start.2 = (f32[8,128]{1,0:T(8,128)S(1)}, f32[8,128]{1,0:T(8,128)S(1)}, u32[]{:S(2)}, u32[]{:S(2)}) collective-permute-start(f32[8,128]{1,0:T(8,128)S(1)} %get-tuple-element.32.refs_1_), channel_id=1, source_target_pairs={{0,3},{1,2},{2,1},{3,0},{4,7},{5,6},{6,5},{7,4},{8,11},{9,10},{10,... | collective-permute-start | bytes 12296 | tf_op jit(solution)/shard_map/ppermute | solution.py:452
  6.5 4.0 %collective-permute-start.1 = (f32[8,128]{1,0:T(8,128)S(1)}, f32[8,128]{1,0:T(8,128)S(1)}, u32[]{:S(2)}, u32[]{:S(2)}) collective-permute-start(f32[8,128]{1,0:T(8,128)S(1)} %get-tuple-element.32.refs_1_), channel_id=1, source_target_pairs={{0,2},{1,3},{2,0},{3,1},{4,6},{5,7},{6,4},{7,5},{8,10},{9,11},{10,... | collective-permute-start | bytes 12296 | tf_op jit(solution)/shard_map/ppermute | solution.py:452
  6.9 3.6 %collective-permute-start = (f32[8,128]{1,0:T(8,128)S(1)}, f32[8,128]{1,0:T(8,128)S(1)}, u32[]{:S(2)}, u32[]{:S(2)}) collective-permute-start(f32[8,128]{1,0:T(8,128)S(1)} %get-tuple-element.32.refs_1_), channel_id=1, source_target_pairs={{0,1},{1,0},{2,3},{3,2},{4,5},{5,4},{6,7},{7,6},{8,9},{9,8},{10,11... | collective-permute-start | bytes 12296 | tf_op jit(solution)/shard_map/ppermute | solution.py:452
  11.1 3.1 %collective-permute-start.3 = (f32[2,40,128]{2,1,0:T(8,128)S(1)}, f32[2,40,128]{2,1,0:T(8,128)S(1)}, u32[]{:S(2)}, u32[]{:S(2)}) collective-permute-start(f32[2,40,128]{2,1,0:T(8,128)S(1)} %get-tuple-element.38), channel_id=1, source_target_pairs={{0,4},{4,0},{8,12},{12,8},{16,20},{20,16},{24,28},{28,24},{32,36},... | collective-permute-start | bytes 122888 | tf_op jit(solution)/shard_map/ppermute | solution.py:452
  14.2 4.2 %collective-permute-start.6 = (f32[2,40,128]{2,1,0:T(8,128)S(1)}, f32[2,40,128]{2,1,0:T(8,128)S(1)}, u32[]{:S(2)}, u32[]{:S(2)}) collective-permute-start(f32[2,40,128]{2,1,0:T(8,128)S(1)} %chip_sums.2.refs_0_), channel_id=1, source_target_pairs={{0,24},{4,28},{8,16},{12,20},{16,8},{20,12},{24,0},{28,4},{32,56},... | collective-permute-start | bytes 122888 | tf_op jit(solution)/shard_map/ppermute | solution.py:452
  16.7 4.4 %collective-permute-start.5 = (f32[2,40,128]{2,1,0:T(8,128)S(1)}, f32[2,40,128]{2,1,0:T(8,128)S(1)}, u32[]{:S(2)}, u32[]{:S(2)}) collective-permute-start(f32[2,40,128]{2,1,0:T(8,128)S(1)} %chip_sums.2.refs_0_), channel_id=1, source_target_pairs={{0,16},{4,20},{8,24},{12,28},{16,0},{20,4},{24,8},{28,12},{32,48},... | collective-permute-start | bytes 122888 | tf_op jit(solution)/shard_map/ppermute | solution.py:452
  17.3 3.8 %collective-permute-start.4 = (f32[2,40,128]{2,1,0:T(8,128)S(1)}, f32[2,40,128]{2,1,0:T(8,128)S(1)}, u32[]{:S(2)}, u32[]{:S(2)}) collective-permute-start(f32[2,40,128]{2,1,0:T(8,128)S(1)} %chip_sums.2.refs_0_), channel_id=1, source_target_pairs={{0,8},{4,12},{8,0},{12,4},{16,24},{20,28},{24,16},{28,20},{32,40},... | collective-permute-start | bytes 122888 | tf_op jit(solution)/shard_map/ppermute | solution.py:452
  37.9 4.1 %collective-permute-start.7 = (f32[2,40,128]{2,1,0:T(8,128)S(1)}, f32[2,40,128]{2,1,0:T(8,128)S(1)}, u32[]{:S(2)}, u32[]{:S(2)}) collective-permute-start(f32[2,40,128]{2,1,0:T(8,128)S(1)} %get-tuple-element.39), channel_id=1, source_target_pairs={{0,4},{4,0},{8,12},{12,8},{16,20},{20,16},{24,28},{28,24},{32,36},... | collective-permute-start | bytes 122888 | tf_op jit(solution)/shard_map/ppermute | solution.py:452
  42.8 3.8 %collective-permute-start.10 = (f32[8,128]{1,0:T(8,128)S(1)}, f32[8,128]{1,0:T(8,128)S(1)}, u32[]{:S(2)}, u32[]{:S(2)}) collective-permute-start(f32[8,128]{1,0:T(8,128)S(1)} %get-tuple-element.43.refs_1_), channel_id=1, source_target_pairs={{0,3},{1,2},{2,1},{3,0},{4,7},{5,6},{6,5},{7,4},{8,11},{9,10},{10,... | collective-permute-start | bytes 12296 | tf_op jit(solution)/shard_map/ppermute | solution.py:452
  43.9 4.0 %collective-permute-start.9 = (f32[8,128]{1,0:T(8,128)S(1)}, f32[8,128]{1,0:T(8,128)S(1)}, u32[]{:S(2)}, u32[]{:S(2)}) collective-permute-start(f32[8,128]{1,0:T(8,128)S(1)} %get-tuple-element.43.refs_1_), channel_id=1, source_target_pairs={{0,2},{1,3},{2,0},{3,1},{4,6},{5,7},{6,4},{7,5},{8,10},{9,11},{10,... | collective-permute-start | bytes 12296 | tf_op jit(solution)/shard_map/ppermute | solution.py:452
  44.7 3.1 %collective-permute-start.8 = (f32[8,128]{1,0:T(8,128)S(1)}, f32[8,128]{1,0:T(8,128)S(1)}, u32[]{:S(2)}, u32[]{:S(2)}) collective-permute-start(f32[8,128]{1,0:T(8,128)S(1)} %get-tuple-element.43.refs_1_), channel_id=1, source_target_pairs={{0,1},{1,0},{2,3},{3,2},{4,5},{5,4},{6,7},{7,6},{8,9},{9,8},{10,11... | collective-permute-start | bytes 12296 | tf_op jit(solution)/shard_map/ppermute | solution.py:452
  48.6 2.7 %collective-permute-start.11 = (f32[2,40,128]{2,1,0:T(8,128)S(1)}, f32[2,40,128]{2,1,0:T(8,128)S(1)}, u32[]{:S(2)}, u32[]{:S(2)}) collective-permute-start(f32[2,40,128]{2,1,0:T(8,128)S(1)} %get-tuple-element.48), channel_id=1, source_target_pairs={{0,4},{4,0},{8,12},{12,8},{16,20},{20,16},{24,28},{28,24},{32,36},... | collective-permute-start | bytes 122888 | tf_op jit(solution)/shard_map/ppermute | solution.py:452
  51.3 4.2 %collective-permute-start.14 = (f32[2,40,128]{2,1,0:T(8,128)S(1)}, f32[2,40,128]{2,1,0:T(8,128)S(1)}, u32[]{:S(2)}, u32[]{:S(2)}) collective-permute-start(f32[2,40,128]{2,1,0:T(8,128)S(1)} %chip_sums.3.refs_0_), channel_id=1, source_target_pairs={{0,24},{4,28},{8,16},{12,20},{16,8},{20,12},{24,0},{28,4},{32,56},... | collective-permute-start | bytes 122888 | tf_op jit(solution)/shard_map/ppermute | solution.py:452
  52.2 4.5 %collective-permute-start.13 = (f32[2,40,128]{2,1,0:T(8,128)S(1)}, f32[2,40,128]{2,1,0:T(8,128)S(1)}, u32[]{:S(2)}, u32[]{:S(2)}) collective-permute-start(f32[2,40,128]{2,1,0:T(8,128)S(1)} %chip_sums.3.refs_0_), channel_id=1, source_target_pairs={{0,16},{4,20},{8,24},{12,28},{16,0},{20,4},{24,8},{28,12},{32,48},... | collective-permute-start | bytes 122888 | tf_op jit(solution)/shard_map/ppermute | solution.py:452
  53.3 3.5 %collective-permute-start.12 = (f32[2,40,128]{2,1,0:T(8,128)S(1)}, f32[2,40,128]{2,1,0:T(8,128)S(1)}, u32[]{:S(2)}, u32[]{:S(2)}) collective-permute-start(f32[2,40,128]{2,1,0:T(8,128)S(1)} %chip_sums.3.refs_0_), channel_id=1, source_target_pairs={{0,8},{4,12},{8,0},{12,4},{16,24},{20,28},{24,16},{28,20},{32,40},... | collective-permute-start | bytes 122888 | tf_op jit(solution)/shard_map/ppermute | solution.py:452
  67.9 3.7 %collective-permute-start.15 = (f32[2,40,128]{2,1,0:T(8,128)S(1)}, f32[2,40,128]{2,1,0:T(8,128)S(1)}, u32[]{:S(2)}, u32[]{:S(2)}) collective-permute-start(f32[2,40,128]{2,1,0:T(8,128)S(1)} %get-tuple-element.49), channel_id=1, source_target_pairs={{0,4},{4,0},{8,12},{12,8},{16,20},{20,16},{24,28},{28,24},{32,36},... | collective-permute-start | bytes 122888 | tf_op jit(solution)/shard_map/ppermute | solution.py:452

commit v5 on v4

--- a/solution.py
+++ b/solution.py
@@ -9,6 +9,7 @@
 
 LANES = 128
 SUB = 8
+CHUNKS = 4
 PLANE = 8
 SCALE = 2.0**40
 VMEM = pl.BlockSpec(memory_space=pltpu.VMEM)
@@ -44,22 +45,42 @@
     return order[0]
 
 
+PAIRS = 80
+
+
 def table_rows(counties):
-    return 2 * counties + SUB
-
-
-def seg_count(seg_ref):
-    last = seg_ref.shape[0] - SUB
-    return seg_ref[last : last + 1, :][0, 0]
-
-
-def seg_range(seg_ref, k):
-    row = seg_ref[pl.ds(k, 1), :]
-    return row[0, 0], row[0, 1]
+    return 2 * counties + PAIRS + SUB
+
+
+def seg_number(seg_ref, row):
+    return seg_ref[pl.ds(row, 1), :][0, 0]
+
+
+def seg_counties(seg_ref):
+    return (seg_ref.shape[0] - SUB - PAIRS) // 2
+
+
+def seg_counts(seg_ref):
+    both = seg_number(seg_ref, seg_ref.shape[0] - SUB)
+    return both & 255, both >> 8
 
 
 def seg_name(seg_ref, k):
-    return seg_ref[pl.ds((seg_ref.shape[0] - SUB) // 2 + k, 1), :]
+    return seg_ref[pl.ds(seg_counties(seg_ref) + k, 1), :]
+
+
+def each_pair(seg_ref, cols_ref, body):
+    at = 2 * seg_counties(seg_ref)
+
+    def step(p, pair):
+        following = seg_number(seg_ref, at + p + 1)
+        k = pair >> 8
+        rows = rows_of(pair & 255)
+        mask = cols_ref[0, rows, :] == seg_name(seg_ref, k).astype(jnp.float32)
+        body(k, rows, mask)
+        return following
+
+    lax.fori_loop(0, seg_counts(seg_ref)[1], step, seg_number(seg_ref, at))
 
 
 def message(msg_ref, row_sum, share):
@@ -67,54 +88,33 @@
     msg_ref[...] = jnp.where(sub == 0, row_sum, jnp.where(sub == 1, share, 0.0))
 
 
-def first_kernel(
-    chunks, cid_hbm, cid_row_hbm, goal_row_hbm, w_hbm, tgt_hbm, msg_ref, seg_ref, cols_ref, w_ref, tgt_ref, cid_ref, cid_row, goal_row, acc_w, acc_t, sems
-):
+def first_kernel(cid_hbm, w_hbm, tgt_hbm, msg_ref, w_ref, tgt_ref, cid_ref, acc_w, acc_t, sems):
     rows = w_ref.shape[1]
     counties, width = tgt_ref.shape
     tiles = width // LANES
+    chunks = CHUNKS
     block = width // chunks
     wide = chunks // 2
-    small = [
-        pltpu.make_async_copy(cid_hbm, cid_ref, sems.at[0]),
-        pltpu.make_async_copy(cid_row_hbm, cid_row, sems.at[1]),
-        pltpu.make_async_copy(goal_row_hbm, goal_row, sems.at[2]),
-    ]
+    county_ids = pltpu.make_async_copy(cid_hbm, cid_ref, sems.at[0])
+    county_ids.start()
     slabs = []
     for q in range(chunks):
         place = w_ref.at[q // wide, :, pl.ds(q % wide * block, block)]
-        slabs.append(pltpu.make_async_copy(w_hbm.at[:, pl.ds(q * block, block)], place, sems.at[3 + q]))
-    for copy in small + slabs:
-        copy.start()
+        slabs.append(pltpu.make_async_copy(w_hbm.at[:, pl.ds(q * block, block)], place, sems.at[1 + q]))
+        slabs[q].start()
     acc_w[...] = jnp.zeros_like(acc_w)
     acc_t[...] = jnp.zeros_like(acc_t)
-    for copy in small:
-        copy.wait()
+    county_ids.wait()
 
     low = cid_ref[0] >> 3
     high = (cid_ref[rows - 1] >> 3) + 1
 
     def targets(b):
-        return pltpu.make_async_copy(tgt_hbm.at[rows_of(b)], tgt_ref.at[rows_of(b)], sems.at[3 + chunks + b])
+        return pltpu.make_async_copy(tgt_hbm.at[rows_of(b)], tgt_ref.at[rows_of(b)], sems.at[1 + chunks + b])
 
     @pl.loop(low, high)
     def _(b):
         targets(b).start()
-
-    lane = lax.broadcasted_iota(jnp.int32, (1, LANES), 1)
-    n = 0
-    first = 0
-    for g in range(rows):
-        c = cid_ref[g]
-        seg_ref[pl.ds(n, 1), :] = jnp.where(lane == 0, first, (g + SUB) // SUB)
-        seg_ref[pl.ds(counties + n, 1), :] = jnp.full((1, LANES), c)
-        if g + 1 < rows:
-            new = cid_ref[g + 1] != c
-            n = n + new.astype(jnp.int32)
-            first = jnp.where(new, (g + 1) // SUB, first)
-    seg_ref[2 * counties : 2 * counties + SUB, :] = jnp.full((SUB, LANES), n + 1)
-    cols_ref[0] = column(cid_row[...].astype(jnp.float32))
-    cols_ref[1] = column(goal_row[...].astype(jnp.float32))
 
     for q in range(chunks):
         slabs[q].wait()
@@ -141,13 +141,44 @@
     message(msg_ref, row_sum, share)
 
 
-def share_kernel(seg_ref, tgt_ref, share_ref):
-    tiles = tgt_ref.shape[1] // LANES
-    half = tiles // 2
+def prepare_kernel(cid_hbm, cid_row_hbm, goal_row_hbm, tgt_ref, seg_ref, cols_ref, share_ref, cid_ref, cid_row, goal_row, sems):
+    copies = [
+        pltpu.make_async_copy(cid_hbm, cid_ref, sems.at[0]),
+        pltpu.make_async_copy(cid_row_hbm, cid_row, sems.at[1]),
+        pltpu.make_async_copy(goal_row_hbm, goal_row, sems.at[2]),
+    ]
+    for copy in copies:
+        copy.start()
+    for copy in copies:
+        copy.wait()
+    rows = cid_ref.shape[0]
+    counties, width = tgt_ref.shape
+    half = width // LANES // 2
+    n, p, first = 0, 0, 0
+    for g in range(rows):
+        c = cid_ref[g]
+        b = g // SUB
+        if g and g % SUB == 0:
+            p = p + 1
+        seg_ref[pl.ds(n, 1), :] = jnp.full((1, LANES), first + 256 * (b + 1))
+        seg_ref[pl.ds(counties + n, 1), :] = jnp.full((1, LANES), c)
+        seg_ref[pl.ds(2 * counties + p, 1), :] = jnp.full((1, LANES), b + 256 * n)
+        if g + 1 < rows:
+            new = cid_ref[g + 1] != c
+            step = new.astype(jnp.int32)
+            n = n + step
+            first = jnp.where(new, (g + 1) // SUB, first)
+            if (g + 1) % SUB:
+                p = p + step
+    last = 2 * counties + PAIRS
+    seg_ref[last : last + SUB, :] = jnp.full((SUB, LANES), n + 1 + 256 * (p + 1))
+    cols_ref[0] = column(cid_row[...].astype(jnp.float32))
+    cols_ref[1] = column(goal_row[...].astype(jnp.float32))
+
     sub = lax.broadcasted_iota(jnp.int32, (SUB, LANES), 0)
     none = jnp.zeros((SUB, LANES), jnp.float32)
 
-    @pl.loop(0, seg_count(seg_ref))
+    @pl.loop(0, n + 1)
     def _(k):
         c = seg_name(seg_ref, k)[0, 0]
         part = rows_of(c >> 3)
@@ -164,16 +195,14 @@
     return core if mine else 1 - core
 
 
-def sums_body(second, mine, seg_ref, w_ref, cols_ref, r1_ref, r2_ref, edge_ref, sums_ref):
+def sums_body(second, mine, seg_ref, w_ref, cols_ref, r1_ref, r2_ref, edge_ref, sums_ref, parts_ref):
     w_ref = w_ref.at[side_of(mine)]
     half = w_ref.shape[1] // LANES
-    n = seg_count(seg_ref)
+    n = seg_counts(seg_ref)[0]
     sub = lax.broadcasted_iota(jnp.int32, (SUB, LANES), 0)
     none = jnp.zeros((SUB, LANES), jnp.float32)
 
-    @pl.loop(0, n)
-    def _(k):
-        b0, b1 = seg_range(seg_ref, k)
+    def county(k, place):
         name = seg_name(seg_ref, k).astype(jnp.float32)
 
         def block(b, accs):
@@ -191,21 +220,29 @@
                 out.append(accs[half] + jnp.where(mask, cols_ref[1, rows, :], 0.0))
             return tuple(out)
 
-        parts = list(lax.fori_loop(b0, b1, block, (none,) * (half if second else half + 1)))
+        parts = list(lax.fori_loop(place & 255, place >> 8, block, (none,) * (half if second else half + 1)))
+        following = seg_number(seg_ref, k + 1)
         if second:
             parts.append(none)
         parts.append(jnp.where(sub == 0, name, 0.0))
         parts += [none] * (-len(parts) % SUB)
+        for i, part in enumerate(parts):
+            parts_ref[i * SUB : (i + 1) * SUB, :] = part
         for t in range(0, len(parts), SUB):
-            sums_ref[k, t : t + SUB, :] = fold(parts[t : t + SUB])
-
+            folded = [parts_ref[pl.ds(t * SUB + i, SUB, stride=SUB), :] for i in range(SUB)]
+            while len(folded) > 1:
+                folded = [x + y for x, y in zip(folded[0::2], folded[1::2])]
+            sums_ref[k, t : t + SUB, :] = folded[0]
+        return following
+
+    lax.fori_loop(0, n, county, seg_number(seg_ref, 0))
     edge_ref[0] = sums_ref[0]
     edge_ref[1] = sums_ref[n - 1]
 
 
 def give_kernel(second, parts_n, *refs):
     seg_ref, refs = refs[0], refs[1:]
-    msgs, refs = refs[:parts_n], refs[parts_n:]
+    msgs, refs, parts_ref = refs[:parts_n], refs[parts_n:-1], refs[-1]
     if second:
         w_ref, cols_ref, r1_ref, edge_ref, sums_ref, rcol_ref = refs
     else:
@@ -218,13 +255,12 @@
         total_ref[...] = total
     rcol = cols_ref[1] / column(total[0:1])
     rcol_ref[...] = rcol * SCALE if second else rcol
-    sums_body(second, False, seg_ref, w_ref, cols_ref, r1_ref, rcol_ref, edge_ref, sums_ref)
+    sums_body(second, False, seg_ref, w_ref, cols_ref, r1_ref, rcol_ref, edge_ref, sums_ref, parts_ref)
 
 
 def keep_kernel(second, seg_ref, w_ref, cols_ref, r1_ref, *refs):
     r2_ref = refs[0] if second else None
-    edge_ref, sums_ref = refs[-2:]
-    sums_body(second, True, seg_ref, w_ref, cols_ref, r1_ref, r2_ref, edge_ref, sums_ref)
+    sums_body(second, True, seg_ref, w_ref, cols_ref, r1_ref, r2_ref, *refs[-3:])
 
 
 def join(refs):
@@ -291,12 +327,17 @@
 
 
 def each_sum(n, edge_ref, sums_ref, body):
+    group = 4
+
+    @pl.when(n > 2)
+    def _():
+        @pl.loop(0, (n + group - 1) // group)
+        def _(g):
+            for i in range(group):
+                body(g * group + i, sums_ref.at[g * group + i])
+
     body(0, edge_ref.at[0])
     body(n - 1, edge_ref.at[1])
-
-    @pl.loop(1, n - 1)
-    def _(k):
-        body(k, sums_ref.at[k])
 
 
 def rows_kernel(mine, seg_ref, total_ref, w_ref, cols_ref, r1_ref, sums_ref, edge_ref, share_ref, *refs):
@@ -307,7 +348,7 @@
     w_ref = w_ref.at[side_of(mine)]
     half = w_ref.shape[1] // LANES
     side = side_of(mine)
-    n = seg_count(seg_ref)
+    n = seg_counts(seg_ref)[0]
     share = total_ref[1:2, :]
     lane = lax.broadcasted_iota(jnp.int32, (1, LANES), 1)
 
@@ -320,22 +361,15 @@
     each_sum(n, edge_ref, sums_ref, factor)
     acc_ref[...] = jnp.zeros_like(acc_ref) if mine else part_ref[...]
 
-    @pl.loop(0, n)
-    def _(k):
-        b0, b1 = seg_range(seg_ref, k)
-        name = seg_name(seg_ref, k).astype(jnp.float32)
-
-        @pl.loop(b0, b1)
-        def _(b):
-            rows = rows_of(b)
-            mask = cols_ref[0, rows, :] == name
-            r1 = jnp.where(mask, r1_ref[rows, :], 0.0)
-            sums = [None] * 4
-            for t in range(half):
-                x = w_ref[rows, tile(t)] * r1 * fac_ref[k, t : t + 1, :]
-                sums[t % 4] = x if sums[t % 4] is None else sums[t % 4] + x
-            acc_ref[rows, :] += (sums[0] + sums[1]) + (sums[2] + sums[3])
-
+    def pair(k, rows, mask):
+        r1 = jnp.where(mask, r1_ref[rows, :], 0.0)
+        sums = [None] * 4
+        for t in range(half):
+            x = w_ref[rows, tile(t)] * r1 * fac_ref[k, t : t + 1, :]
+            sums[t % 4] = x if sums[t % 4] is None else sums[t % 4] + x
+        acc_ref[rows, :] += (sums[0] + sums[1]) + (sums[2] + sums[3])
+
+    each_pair(seg_ref, cols_ref, pair)
     if not mine:
         message(msg_ref, jnp.sum(acc_ref[...].T, axis=0, keepdims=True), jnp.zeros((1, LANES), jnp.float32))
 
@@ -343,7 +377,7 @@
 def fitted(mine, chunks, done, seg_ref, w_ref, cols_ref, r1_ref, r2_ref, goal_ref, sums_ref, edge_ref, out_ref, fac_ref):
     w_ref = w_ref.at[side_of(mine)]
     half = w_ref.shape[1] // LANES
-    n = seg_count(seg_ref)
+    n = seg_counts(seg_ref)[0]
 
     def factor(k, sum_ref):
         fac_ref[k] = 100.0 * (goal_ref[k] / sum_ref[...])
@@ -352,22 +386,14 @@
     for q in range(chunks):
         own = range(q * half // chunks, (q + 1) * half // chunks)
 
-        @pl.loop(0, n)
-        def _(k):
-            b0, b1 = seg_range(seg_ref, k)
-            name = seg_name(seg_ref, k).astype(jnp.float32)
-            fac = [jnp.broadcast_to(fac_ref[k, t : t + 1, :], (SUB, LANES)) for t in own]
-
-            @pl.loop(b0, b1)
-            def _(b):
-                rows = rows_of(b)
-                mask = cols_ref[0, rows, :] == name
-                r1 = r1_ref[rows, :]
-                r2 = r2_ref[rows, :]
-                for i, t in enumerate(own):
-                    x = w_ref[rows, tile(t)] * r1 * r2 * fac[i]
-                    pltpu.store(out_ref.at[rows, tile(t)], x, mask=mask)
-
+        def pair(k, rows, mask):
+            r1 = r1_ref[rows, :]
+            r2 = r2_ref[rows, :]
+            for t in own:
+                x = w_ref[rows, tile(t)] * r1 * r2 * fac_ref[k, t : t + 1, :]
+                pltpu.store(out_ref.at[rows, tile(t)], x, mask=mask)
+
+        each_pair(seg_ref, cols_ref, pair)
         done(q)
 
 
@@ -421,30 +447,27 @@
     counties = county_target.shape[0]
     half = width // LANES // 2
     half_rows = half + 4
-    in_chunks, out_chunks = 8, 2
+    out_chunks = 1
     device = planes * PLANE
 
     edge = f32(2, half_rows, LANES)
     table = f32(counties, half_rows, LANES)
     column_of = f32(rows, LANES)
     small = f32(SUB, LANES)
-    msg, seg, cols, slab, targets = call(
-        functools.partial(first_kernel, in_chunks),
+    parts_scratch = [pltpu.VMEM((half_rows * SUB, LANES), jnp.float32)]
+    hbm = [pltpu.with_memory_space_constraint(x, pltpu.HBM) for x in (county_id, county_id.reshape(1, rows), row_target.reshape(1, rows))]
+    msg, slab, targets = call(
+        first_kernel,
         "row_sums_1",
-        [
-            pltpu.with_memory_space_constraint(x, pltpu.HBM)
-            for x in (county_id, county_id.reshape(1, rows), row_target.reshape(1, rows), seed_slab, county_target)
-        ],
-        [HBM] * 5,
-        (small, jax.ShapeDtypeStruct((table_rows(counties), LANES), jnp.int32), f32(2, rows, LANES), f32(2, rows, width // 2), jax.ShapeDtypeStruct((counties, width), jnp.int32)),
-        (VMEM, VMEM, VMEM, VMEM, VMEM),
+        [hbm[0]] + [pltpu.with_memory_space_constraint(x, pltpu.HBM) for x in (seed_slab, county_target)],
+        [HBM] * 3,
+        (small, f32(2, rows, width // 2), jax.ShapeDtypeStruct((counties, width), jnp.int32)),
+        None,
         [
             pltpu.SMEM((rows,), jnp.int32),
-            pltpu.VMEM((1, rows), jnp.int32),
-            pltpu.VMEM((1, rows), jnp.int32),
             pltpu.VMEM((rows, LANES), jnp.float32),
             pltpu.VMEM((LANES, LANES), jnp.float32),
-            pltpu.SemaphoreType.DMA((3 + in_chunks + counties // SUB,)),
+            pltpu.SemaphoreType.DMA((1 + CHUNKS + counties // SUB,)),
         ],
     )
 
@@ -467,17 +490,32 @@
         return own, swap(other, "bg", device, 1), keep[1]
 
     msgs = over_type(msg)
-    share = call(share_kernel, "shares", (seg, targets), [VMEM, VMEM], f32(counties, 2, half_rows, LANES))
+    seg, cols, share = call(
+        prepare_kernel,
+        "prepare",
+        hbm + [targets],
+        [HBM] * 3 + [VMEM],
+        (jax.ShapeDtypeStruct((table_rows(counties), LANES), jnp.int32), f32(2, rows, LANES), f32(counties, 2, half_rows, LANES)),
+        None,
+        [
+            pltpu.SMEM((rows,), jnp.int32),
+            pltpu.VMEM((1, rows), jnp.int32),
+            pltpu.VMEM((1, rows), jnp.int32),
+            pltpu.SemaphoreType.DMA((3,)),
+        ],
+    )
     give, sums_give, r1, total = call(
         functools.partial(give_kernel, False, parts),
         "county_sums_1a",
         [seg] + msgs + [share, slab, cols],
         [VMEM] * (parts + 4),
         (edge, table, column_of, small),
+        None,
+        parts_scratch,
     )
     own, other, sums_keep = edges(
         give,
-        lambda: call(functools.partial(keep_kernel, False), "county_sums_1b", (seg, slab, cols, r1), [VMEM] * 4, (edge, table)),
+        lambda: call(functools.partial(keep_kernel, False), "county_sums_1b", (seg, slab, cols, r1), [VMEM] * 4, (edge, table), None, parts_scratch),
     )
     fac = pltpu.VMEM((counties, half_rows, LANES), jnp.float32)
     goal_keep, part = call(
@@ -504,10 +542,12 @@
         [seg] + over_type(msg) + [slab, cols, r1],
         [VMEM] * (parts + 4),
         (edge, table, column_of),
+        None,
+        parts_scratch,
     )
     own, other, sums_keep = edges(
         give,
-        lambda: call(functools.partial(keep_kernel, True), "county_sums_2b", (seg, slab, cols, r1, r2), [VMEM] * 5, (edge, table)),
+        lambda: call(functools.partial(keep_kernel, True), "county_sums_2b", (seg, slab, cols, r1, r2), [VMEM] * 5, (edge, table), None, parts_scratch),
     )
     mine = call(
         last_own_kernel,

time: 74.6 us -> 73.8 us (0.989)
  waiting for transfers between devices: 11.7 us -> 10.8 us
  Pallas kernels: 9.99 us -> 10.8 us
    ppermute x16, waiting for transfers between devices: 11.7 us -> 10.8 us  [swap(): return lax.ppermute(x, axis, [(i, i ^ mask) for i in range(size)])]
    pallas_call x16, Pallas kernels: 9.99 us -> 10.8 us  [call(): pl.pallas_call(kernel, out_shape=out_shape, in_specs=in_specs, out_specs=...]
  transfers between devices with their start and end apart: 16 -> 16, of which waited for: 13 -> 11; matrix products, arithmetic and copies ran while one was open for 0% -> 0% of each run, Pallas kernels for 3% -> 5%
where the time goes in v5:
time: 73.8 us; the launch traced here: 73.6 us
  blocking collectives  27 us (37%)
  starting transfers between devices  24.8 us (34%)
  Pallas kernels  10.8 us (15%)
  waiting for transfers between devices  10.8 us (15%)
    all_to_all x2, blocking collectives, edges(): far = lax.all_to_all(send, 'bg', 0, 0, axis_index_groups=lines)  27 us
    ppermute x16, starting transfers between devices, swap(): return lax.ppermute(x, axis, [(i, i ^ mask) for i in range(size)])  24.8 us
    ppermute x16, waiting for transfers between devices, swap(): return lax.ppermute(x, axis, [(i, i ^ mask) for i in range(size)])  10.8 us
    pallas_call x16, Pallas kernels, call(): pl.pallas_call(kernel, out_shape=out_shape, in_specs=in_specs, out_specs=...  10.8 us
  transfers between devices with their start and end apart: 16, of which 11 were waited for; matrix products, arithmetic and copies ran while one was open for 0% of the time, Pallas kernels for 5%

profile of v5, /device:TPU:1, one launch (start us, length us, event | category | flops | bytes accessed | tf_op | source)
XLA Modules:
  0.0 73.6 jit_solution(1181920380879622106)
XLA Ops:
  0.0 2.8 %row_sums_1.1 = (f32[8,128]{1,0:T(8,128)S(1)}, f32[2,128,4608]{2,1,0:T(8,128)S(1)}, s32[64,9216]{1,0:T(8,128)S(1)}) custom-call(s32[128]{0:T(128)} %cid_hbm.3, f32[128,9216]{1,0:T(8,128)} %w_hbm.1, s32[64,9216]{1,0:T(8,128)} %tgt_hbm.1), custom_call_target="tpu_custom_call" | custom-call | flops 4194304 | bytes 4194304 | tf_op jit(solution)/shard_map/row_sums_1/pallas_call | solution.py:433
  2.8 3.7 %collective-permute-start.2 = (f32[8,128]{1,0:T(8,128)S(1)}, f32[8,128]{1,0:T(8,128)S(1)}, u32[]{:S(2)}, u32[]{:S(2)}) collective-permute-start(f32[8,128]{1,0:T(8,128)S(1)} %get-tuple-element.34.refs_1_), channel_id=1, source_target_pairs={{0,3},{1,2},{2,1},{3,0},{4,7},{5,6},{6,5},{7,4},{8,11},{9,10},{10,... | collective-permute-start | bytes 12296 | tf_op jit(solution)/shard_map/ppermute | solution.py:475
  7.1 1.2 %prepare.1 = (s32[216,128]{1,0:T(8,128)S(1)}, f32[2,128,128]{2,1,0:T(8,128)S(1)}, f32[64,2,40,128]{3,2,1,0:T(8,128)S(1)}) custom-call(s32[128]{0:T(128)} %cid_hbm.3, s32[1,128]{1,0:T(1,128)} %bitcast.2, s32[1,128]{1,0:T(1,128)} %bitcast.3, s32[64,9216]{1,0:T(8,128)S(1)} %get-tuple-element.30.tgt_ref), custom_call_target="tpu_custom_call" | custom-call | flops 4194304 | bytes 4194304 | tf_op jit(solution)/shard_map/prepare/pallas_call | solution.py:433
  8.4 2.0 %collective-permute-done.1.refs_3_ = f32[8,128]{1,0:T(8,128)S(1)} collective-permute-done((f32[8,128]{1,0:T(8,128)S(1)}, f32[8,128]{1,0:T(8,128)S(1)}, u32[]{:S(2)}, u32[]{:S(2)}) %collective-permute-start.1) | collective-permute-done | bytes 4128 | tf_op jit(solution)/shard_map/ppermute | solution.py:475
  10.9 2.2 %collective-permute-start.3 = (f32[2,40,128]{2,1,0:T(8,128)S(1)}, f32[2,40,128]{2,1,0:T(8,128)S(1)}, u32[]{:S(2)}, u32[]{:S(2)}) collective-permute-start(f32[2,40,128]{2,1,0:T(8,128)S(1)} %get-tuple-element.40), channel_id=1, source_target_pairs={{0,4},{4,0},{8,12},{12,8},{16,20},{20,16},{24,28},{28,24},{32,36},... | collective-permute-start | bytes 122888 | tf_op jit(solution)/shard_map/ppermute | solution.py:475
  14.0 2.6 %collective-permute-start.6 = (f32[2,40,128]{2,1,0:T(8,128)S(1)}, f32[2,40,128]{2,1,0:T(8,128)S(1)}, u32[]{:S(2)}, u32[]{:S(2)}) collective-permute-start(f32[2,40,128]{2,1,0:T(8,128)S(1)} %chip_sums.2.refs_0_), channel_id=1, source_target_pairs={{0,24},{4,28},{8,16},{12,20},{16,8},{20,12},{24,0},{28,4},{32,56},... | collective-permute-start | bytes 122888 | tf_op jit(solution)/shard_map/ppermute | solution.py:475
  17.4 0.8 %collective-permute-done.6.refs_3_.refs_2_ = f32[2,40,128]{2,1,0:T(8,128)S(1)} collective-permute-done((f32[2,40,128]{2,1,0:T(8,128)S(1)}, f32[2,40,128]{2,1,0:T(8,128)S(1)}, u32[]{:S(2)}, u32[]{:S(2)}) %collective-permute-start.6) | collective-permute-done | bytes 40992 | tf_op jit(solution)/shard_map/ppermute | solution.py:475
  18.2 2.8 %collective-permute-done.5.refs_2_.refs_1_ = f32[2,40,128]{2,1,0:T(8,128)S(1)} collective-permute-done((f32[2,40,128]{2,1,0:T(8,128)S(1)}, f32[2,40,128]{2,1,0:T(8,128)S(1)}, u32[]{:S(2)}, u32[]{:S(2)}) %collective-permute-start.5) | collective-permute-done | bytes 40992 | tf_op jit(solution)/shard_map/ppermute | solution.py:475
  21.0 16.3 %all_to_all.10.far_ref = f32[8,40,128]{2,1,0:T(8,128)S(1)} all-to-all(f32[8,40,128]{2,1,0:T(8,128)S(1)} %plane_sums.2), channel_id=1, replica_groups={{0,32,64,96,128,160,192,224},{4,36,68,100,132,164,196,228},{8,40,72,104..., dimensions={0} | all-to-all | bytes 327680 | tf_op jit(solution)/shard_map/all_to_all | solution.py:488
  37.5 3.2 %collective-permute-start.7 = (f32[2,40,128]{2,1,0:T(8,128)S(1)}, f32[2,40,128]{2,1,0:T(8,128)S(1)}, u32[]{:S(2)}, u32[]{:S(2)}) collective-permute-start(f32[2,40,128]{2,1,0:T(8,128)S(1)} %get-tuple-element.41), channel_id=1, source_target_pairs={{0,4},{4,0},{8,12},{12,8},{16,20},{20,16},{24,28},{28,24},{32,36},... | collective-permute-start | bytes 122888 | tf_op jit(solution)/shard_map/ppermute | solution.py:475
  41.6 0.8 %row_sums_2b.1 = (f32[64,40,128]{2,1,0:T(8,128)S(1)}, f32[8,128]{1,0:T(8,128)S(1)}) custom-call(s32[216,128]{1,0:T(8,128)S(1)} %get-tuple-element.31.refs_0_.seg_ref, f32[8,128]{1,0:T(8,128)S(1)} %get-tuple-element.37.total_ref, f32[2,128,4608]{2,1,0:T(8,128)S(1)} %get-tuple-element.32.refs_6_.w_ref.refs_5_, ...), custom_call_target="tpu_custom_call" | custom-call | flops 4194304 | bytes 4194304 | tf_op jit(solution)/shard_map/row_sums_2b/pallas_call | solution.py:433
  42.4 1.1 %collective-permute-start.10 = (f32[8,128]{1,0:T(8,128)S(1)}, f32[8,128]{1,0:T(8,128)S(1)}, u32[]{:S(2)}, u32[]{:S(2)}) collective-permute-start(f32[8,128]{1,0:T(8,128)S(1)} %get-tuple-element.45.refs_1_), channel_id=1, source_target_pairs={{0,3},{1,2},{2,1},{3,0},{4,7},{5,6},{6,5},{7,4},{8,11},{9,10},{10,... | collective-permute-start | bytes 12296 | tf_op jit(solution)/shard_map/ppermute | solution.py:475
  43.5 0.8 %collective-permute-start.9 = (f32[8,128]{1,0:T(8,128)S(1)}, f32[8,128]{1,0:T(8,128)S(1)}, u32[]{:S(2)}, u32[]{:S(2)}) collective-permute-start(f32[8,128]{1,0:T(8,128)S(1)} %get-tuple-element.45.refs_1_), channel_id=1, source_target_pairs={{0,2},{1,3},{2,0},{3,1},{4,6},{5,7},{6,4},{7,5},{8,10},{9,11},{10,... | collective-permute-start | bytes 12296 | tf_op jit(solution)/shard_map/ppermute | solution.py:475
  44.3 1.4 %collective-permute-start.8 = (f32[8,128]{1,0:T(8,128)S(1)}, f32[8,128]{1,0:T(8,128)S(1)}, u32[]{:S(2)}, u32[]{:S(2)}) collective-permute-start(f32[8,128]{1,0:T(8,128)S(1)} %get-tuple-element.45.refs_1_), channel_id=1, source_target_pairs={{0,1},{1,0},{2,3},{3,2},{4,5},{5,4},{6,7},{7,6},{8,9},{9,8},{10,11... | collective-permute-start | bytes 12296 | tf_op jit(solution)/shard_map/ppermute | solution.py:475
  46.1 1.3 %collective-permute-done.9.refs_3_ = f32[8,128]{1,0:T(8,128)S(1)} collective-permute-done((f32[8,128]{1,0:T(8,128)S(1)}, f32[8,128]{1,0:T(8,128)S(1)}, u32[]{:S(2)}, u32[]{:S(2)}) %collective-permute-start.9) | collective-permute-done | bytes 4128 | tf_op jit(solution)/shard_map/ppermute | solution.py:475
  48.0 1.9 %collective-permute-start.11 = (f32[2,40,128]{2,1,0:T(8,128)S(1)}, f32[2,40,128]{2,1,0:T(8,128)S(1)}, u32[]{:S(2)}, u32[]{:S(2)}) collective-permute-start(f32[2,40,128]{2,1,0:T(8,128)S(1)} %get-tuple-element.50), channel_id=1, source_target_pairs={{0,4},{4,0},{8,12},{12,8},{16,20},{20,16},{24,28},{28,24},{32,36},... | collective-permute-start | bytes 122888 | tf_op jit(solution)/shard_map/ppermute | solution.py:475
  50.8 1.3 %collective-permute-start.14 = (f32[2,40,128]{2,1,0:T(8,128)S(1)}, f32[2,40,128]{2,1,0:T(8,128)S(1)}, u32[]{:S(2)}, u32[]{:S(2)}) collective-permute-start(f32[2,40,128]{2,1,0:T(8,128)S(1)} %chip_sums.3.refs_0_), channel_id=1, source_target_pairs={{0,24},{4,28},{8,16},{12,20},{16,8},{20,12},{24,0},{28,4},{32,56},... | collective-permute-start | bytes 122888 | tf_op jit(solution)/shard_map/ppermute | solution.py:475
  52.0 0.8 %collective-permute-start.13 = (f32[2,40,128]{2,1,0:T(8,128)S(1)}, f32[2,40,128]{2,1,0:T(8,128)S(1)}, u32[]{:S(2)}, u32[]{:S(2)}) collective-permute-start(f32[2,40,128]{2,1,0:T(8,128)S(1)} %chip_sums.3.refs_0_), channel_id=1, source_target_pairs={{0,16},{4,20},{8,24},{12,28},{16,0},{20,4},{24,8},{28,12},{32,48},... | collective-permute-start | bytes 122888 | tf_op jit(solution)/shard_map/ppermute | solution.py:475
  52.9 1.3 %collective-permute-start.12 = (f32[2,40,128]{2,1,0:T(8,128)S(1)}, f32[2,40,128]{2,1,0:T(8,128)S(1)}, u32[]{:S(2)}, u32[]{:S(2)}) collective-permute-start(f32[2,40,128]{2,1,0:T(8,128)S(1)} %chip_sums.3.refs_0_), channel_id=1, source_target_pairs={{0,8},{4,12},{8,0},{12,4},{16,24},{20,28},{24,16},{28,20},{32,40},... | collective-permute-start | bytes 122888 | tf_op jit(solution)/shard_map/ppermute | solution.py:475
  54.1 0.8 %collective-permute-done.14.refs_3_.refs_2_ = f32[2,40,128]{2,1,0:T(8,128)S(1)} collective-permute-done((f32[2,40,128]{2,1,0:T(8,128)S(1)}, f32[2,40,128]{2,1,0:T(8,128)S(1)}, u32[]{:S(2)}, u32[]{:S(2)}) %collective-permute-start.14) | collective-permute-done | bytes 40992 | tf_op jit(solution)/shard_map/ppermute | solution.py:475
  54.9 1.5 %collective-permute-done.13.refs_2_.refs_1_ = f32[2,40,128]{2,1,0:T(8,128)S(1)} collective-permute-done((f32[2,40,128]{2,1,0:T(8,128)S(1)}, f32[2,40,128]{2,1,0:T(8,128)S(1)}, u32[]{:S(2)}, u32[]{:S(2)}) %collective-permute-start.13) | collective-permute-done | bytes 40992 | tf_op jit(solution)/shard_map/ppermute | solution.py:475
  56.5 10.7 %all_to_all.11.far_ref = f32[8,40,128]{2,1,0:T(8,128)S(1)} all-to-all(f32[8,40,128]{2,1,0:T(8,128)S(1)} %plane_sums.3), channel_id=1, replica_groups={{0,32,64,96,128,160,192,224},{4,36,68,100,132,164,196,228},{8,40,72,104..., dimensions={0} | all-to-all | bytes 327680 | tf_op jit(solution)/shard_map/all_to_all | solution.py:488
  67.3 3.2 %collective-permute-start.15 = (f32[2,40,128]{2,1,0:T(8,128)S(1)}, f32[2,40,128]{2,1,0:T(8,128)S(1)}, u32[]{:S(2)}, u32[]{:S(2)}) collective-permute-start(f32[2,40,128]{2,1,0:T(8,128)S(1)} %get-tuple-element.51), channel_id=1, source_target_pairs={{0,4},{4,0},{8,12},{12,8},{16,20},{20,16},{24,28},{28,24},{32,36},... | collective-permute-start | bytes 122888 | tf_op jit(solution)/shard_map/ppermute | solution.py:475
  71.4 2.2 %fitted_b.1 = f32[128,9216]{1,0:T(8,128)} custom-call(s32[216,128]{1,0:T(8,128)S(1)} %get-tuple-element.31.refs_0_.seg_ref, f32[2,128,4608]{2,1,0:T(8,128)S(1)} %get-tuple-element.32.refs_6_.w_ref.refs_5_, f32[2,128,128]{2,1,0:T(8,128)S(1)} %get-tuple-element.33.refs_7_.cols_ref.refs_6_, f32[128,128]{1,0:T(8,128)S(1)} %get-tuple-element.36.r1_ref.refs_7_, ...), custom_call_target="tpu_custom_call" | custom-call | flops 4194304 | bytes 4194304 | tf_op jit(solution)/shard_map/fitted_b/pallas_call | solution.py:433
  (26 shorter events, 6.9 us)
Async XLA Ops:
  2.8 5.6 %collective-permute-start.2 = (f32[8,128]{1,0:T(8,128)S(1)}, f32[8,128]{1,0:T(8,128)S(1)}, u32[]{:S(2)}, u32[]{:S(2)}) collective-permute-start(f32[8,128]{1,0:T(8,128)S(1)} %get-tuple-element.34.refs_1_), channel_id=1, source_target_pairs={{0,3},{1,2},{2,1},{3,0},{4,7},{5,6},{6,5},{7,4},{8,11},{9,10},{10,... | collective-permute-start | bytes 12296 | tf_op jit(solution)/shard_map/ppermute | solution.py:475
  6.4 4.0 %collective-permute-start.1 = (f32[8,128]{1,0:T(8,128)S(1)}, f32[8,128]{1,0:T(8,128)S(1)}, u32[]{:S(2)}, u32[]{:S(2)}) collective-permute-start(f32[8,128]{1,0:T(8,128)S(1)} %get-tuple-element.34.refs_1_), channel_id=1, source_target_pairs={{0,2},{1,3},{2,0},{3,1},{4,6},{5,7},{6,4},{7,5},{8,10},{9,11},{10,... | collective-permute-start | bytes 12296 | tf_op jit(solution)/shard_map/ppermute | solution.py:475
  6.8 3.6 %collective-permute-start = (f32[8,128]{1,0:T(8,128)S(1)}, f32[8,128]{1,0:T(8,128)S(1)}, u32[]{:S(2)}, u32[]{:S(2)}) collective-permute-start(f32[8,128]{1,0:T(8,128)S(1)} %get-tuple-element.34.refs_1_), channel_id=1, source_target_pairs={{0,1},{1,0},{2,3},{3,2},{4,5},{5,4},{6,7},{7,6},{8,9},{9,8},{10,11... | collective-permute-start | bytes 12296 | tf_op jit(solution)/shard_map/ppermute | solution.py:475
  10.9 3.1 %collective-permute-start.3 = (f32[2,40,128]{2,1,0:T(8,128)S(1)}, f32[2,40,128]{2,1,0:T(8,128)S(1)}, u32[]{:S(2)}, u32[]{:S(2)}) collective-permute-start(f32[2,40,128]{2,1,0:T(8,128)S(1)} %get-tuple-element.40), channel_id=1, source_target_pairs={{0,4},{4,0},{8,12},{12,8},{16,20},{20,16},{24,28},{28,24},{32,36},... | collective-permute-start | bytes 122888 | tf_op jit(solution)/shard_map/ppermute | solution.py:475
  14.0 4.2 %collective-permute-start.6 = (f32[2,40,128]{2,1,0:T(8,128)S(1)}, f32[2,40,128]{2,1,0:T(8,128)S(1)}, u32[]{:S(2)}, u32[]{:S(2)}) collective-permute-start(f32[2,40,128]{2,1,0:T(8,128)S(1)} %chip_sums.2.refs_0_), channel_id=1, source_target_pairs={{0,24},{4,28},{8,16},{12,20},{16,8},{20,12},{24,0},{28,4},{32,56},... | collective-permute-start | bytes 122888 | tf_op jit(solution)/shard_map/ppermute | solution.py:475
  16.6 4.4 %collective-permute-start.5 = (f32[2,40,128]{2,1,0:T(8,128)S(1)}, f32[2,40,128]{2,1,0:T(8,128)S(1)}, u32[]{:S(2)}, u32[]{:S(2)}) collective-permute-start(f32[2,40,128]{2,1,0:T(8,128)S(1)} %chip_sums.2.refs_0_), channel_id=1, source_target_pairs={{0,16},{4,20},{8,24},{12,28},{16,0},{20,4},{24,8},{28,12},{32,48},... | collective-permute-start | bytes 122888 | tf_op jit(solution)/shard_map/ppermute | solution.py:475
  17.1 3.8 %collective-permute-start.4 = (f32[2,40,128]{2,1,0:T(8,128)S(1)}, f32[2,40,128]{2,1,0:T(8,128)S(1)}, u32[]{:S(2)}, u32[]{:S(2)}) collective-permute-start(f32[2,40,128]{2,1,0:T(8,128)S(1)} %chip_sums.2.refs_0_), channel_id=1, source_target_pairs={{0,8},{4,12},{8,0},{12,4},{16,24},{20,28},{24,16},{28,20},{32,40},... | collective-permute-start | bytes 122888 | tf_op jit(solution)/shard_map/ppermute | solution.py:475
  37.5 4.1 %collective-permute-start.7 = (f32[2,40,128]{2,1,0:T(8,128)S(1)}, f32[2,40,128]{2,1,0:T(8,128)S(1)}, u32[]{:S(2)}, u32[]{:S(2)}) collective-permute-start(f32[2,40,128]{2,1,0:T(8,128)S(1)} %get-tuple-element.41), channel_id=1, source_target_pairs={{0,4},{4,0},{8,12},{12,8},{16,20},{20,16},{24,28},{28,24},{32,36},... | collective-permute-start | bytes 122888 | tf_op jit(solution)/shard_map/ppermute | solution.py:475
  42.4 3.8 %collective-permute-start.10 = (f32[8,128]{1,0:T(8,128)S(1)}, f32[8,128]{1,0:T(8,128)S(1)}, u32[]{:S(2)}, u32[]{:S(2)}) collective-permute-start(f32[8,128]{1,0:T(8,128)S(1)} %get-tuple-element.45.refs_1_), channel_id=1, source_target_pairs={{0,3},{1,2},{2,1},{3,0},{4,7},{5,6},{6,5},{7,4},{8,11},{9,10},{10,... | collective-permute-start | bytes 12296 | tf_op jit(solution)/shard_map/ppermute | solution.py:475
  43.5 4.0 %collective-permute-start.9 = (f32[8,128]{1,0:T(8,128)S(1)}, f32[8,128]{1,0:T(8,128)S(1)}, u32[]{:S(2)}, u32[]{:S(2)}) collective-permute-start(f32[8,128]{1,0:T(8,128)S(1)} %get-tuple-element.45.refs_1_), channel_id=1, source_target_pairs={{0,2},{1,3},{2,0},{3,1},{4,6},{5,7},{6,4},{7,5},{8,10},{9,11},{10,... | collective-permute-start | bytes 12296 | tf_op jit(solution)/shard_map/ppermute | solution.py:475
  44.3 3.1 %collective-permute-start.8 = (f32[8,128]{1,0:T(8,128)S(1)}, f32[8,128]{1,0:T(8,128)S(1)}, u32[]{:S(2)}, u32[]{:S(2)}) collective-permute-start(f32[8,128]{1,0:T(8,128)S(1)} %get-tuple-element.45.refs_1_), channel_id=1, source_target_pairs={{0,1},{1,0},{2,3},{3,2},{4,5},{5,4},{6,7},{7,6},{8,9},{9,8},{10,11... | collective-permute-start | bytes 12296 | tf_op jit(solution)/shard_map/ppermute | solution.py:475
  48.0 2.7 %collective-permute-start.11 = (f32[2,40,128]{2,1,0:T(8,128)S(1)}, f32[2,40,128]{2,1,0:T(8,128)S(1)}, u32[]{:S(2)}, u32[]{:S(2)}) collective-permute-start(f32[2,40,128]{2,1,0:T(8,128)S(1)} %get-tuple-element.50), channel_id=1, source_target_pairs={{0,4},{4,0},{8,12},{12,8},{16,20},{20,16},{24,28},{28,24},{32,36},... | collective-permute-start | bytes 122888 | tf_op jit(solution)/shard_map/ppermute | solution.py:475
  50.8 4.2 %collective-permute-start.14 = (f32[2,40,128]{2,1,0:T(8,128)S(1)}, f32[2,40,128]{2,1,0:T(8,128)S(1)}, u32[]{:S(2)}, u32[]{:S(2)}) collective-permute-start(f32[2,40,128]{2,1,0:T(8,128)S(1)} %chip_sums.3.refs_0_), channel_id=1, source_target_pairs={{0,24},{4,28},{8,16},{12,20},{16,8},{20,12},{24,0},{28,4},{32,56},... | collective-permute-start | bytes 122888 | tf_op jit(solution)/shard_map/ppermute | solution.py:475
  52.0 4.4 %collective-permute-start.13 = (f32[2,40,128]{2,1,0:T(8,128)S(1)}, f32[2,40,128]{2,1,0:T(8,128)S(1)}, u32[]{:S(2)}, u32[]{:S(2)}) collective-permute-start(f32[2,40,128]{2,1,0:T(8,128)S(1)} %chip_sums.3.refs_0_), channel_id=1, source_target_pairs={{0,16},{4,20},{8,24},{12,28},{16,0},{20,4},{24,8},{28,12},{32,48},... | collective-permute-start | bytes 122888 | tf_op jit(solution)/shard_map/ppermute | solution.py:475
  52.9 3.5 %collective-permute-start.12 = (f32[2,40,128]{2,1,0:T(8,128)S(1)}, f32[2,40,128]{2,1,0:T(8,128)S(1)}, u32[]{:S(2)}, u32[]{:S(2)}) collective-permute-start(f32[2,40,128]{2,1,0:T(8,128)S(1)} %chip_sums.3.refs_0_), channel_id=1, source_target_pairs={{0,8},{4,12},{8,0},{12,4},{16,24},{20,28},{24,16},{28,20},{32,40},... | collective-permute-start | bytes 122888 | tf_op jit(solution)/shard_map/ppermute | solution.py:475
  67.3 4.1 %collective-permute-start.15 = (f32[2,40,128]{2,1,0:T(8,128)S(1)}, f32[2,40,128]{2,1,0:T(8,128)S(1)}, u32[]{:S(2)}, u32[]{:S(2)}) collective-permute-start(f32[2,40,128]{2,1,0:T(8,128)S(1)} %get-tuple-element.51), channel_id=1, source_target_pairs={{0,4},{4,0},{8,12},{12,8},{16,20},{20,16},{24,28},{28,24},{32,36},... | collective-permute-start | bytes 122888 | tf_op jit(solution)/shard_map/ppermute | solution.py:475

commit v6 on v5

--- a/solution.py
+++ b/solution.py
@@ -9,9 +9,9 @@
 
 LANES = 128
 SUB = 8
-CHUNKS = 4
 PLANE = 8
-SCALE = 2.0**40
+SCALE = 2.0**30
+SHARE = 2.0**-26
 VMEM = pl.BlockSpec(memory_space=pltpu.VMEM)
 HBM = pl.BlockSpec(memory_space=pltpu.HBM)
 PARAMS = pltpu.CompilerParams(vmem_limit_bytes=32 * 1024 * 1024)
@@ -88,60 +88,37 @@
     msg_ref[...] = jnp.where(sub == 0, row_sum, jnp.where(sub == 1, share, 0.0))
 
 
-def first_kernel(cid_hbm, w_hbm, tgt_hbm, msg_ref, w_ref, tgt_ref, cid_ref, acc_w, acc_t, sems):
-    rows = w_ref.shape[1]
-    counties, width = tgt_ref.shape
-    tiles = width // LANES
-    chunks = CHUNKS
-    block = width // chunks
-    wide = chunks // 2
-    county_ids = pltpu.make_async_copy(cid_hbm, cid_ref, sems.at[0])
-    county_ids.start()
+def first_kernel(w_hbm, msg_ref, w_ref, acc_w, sems):
+    rows, half = w_ref.shape[1:]
+    tiles = half // LANES
+    cuts = [[0, tiles // 2, tiles], [0, tiles // 2, 5 * tiles // 6, tiles]]
     slabs = []
-    for q in range(chunks):
-        place = w_ref.at[q // wide, :, pl.ds(q % wide * block, block)]
-        slabs.append(pltpu.make_async_copy(w_hbm.at[:, pl.ds(q * block, block)], place, sems.at[1 + q]))
-        slabs[q].start()
+    for h, cut in enumerate(cuts):
+        for low, high in zip(cut, cut[1:]):
+            size = (high - low) * LANES
+            from_hbm = w_hbm.at[:, pl.ds(h * half + low * LANES, size)]
+            copy = pltpu.make_async_copy(from_hbm, w_ref.at[h, :, pl.ds(low * LANES, size)], sems.at[len(slabs)])
+            copy.start()
+            slabs.append((copy, h, low, high))
     acc_w[...] = jnp.zeros_like(acc_w)
-    acc_t[...] = jnp.zeros_like(acc_t)
-    county_ids.wait()
-
-    low = cid_ref[0] >> 3
-    high = (cid_ref[rows - 1] >> 3) + 1
-
-    def targets(b):
-        return pltpu.make_async_copy(tgt_hbm.at[rows_of(b)], tgt_ref.at[rows_of(b)], sems.at[1 + chunks + b])
-
-    @pl.loop(low, high)
-    def _(b):
-        targets(b).start()
-
-    for q in range(chunks):
-        slabs[q].wait()
+    for copy, h, low, high in slabs:
+        copy.wait()
 
         @pl.loop(0, rows // SUB)
         def _(b):
             part = rows_of(b)
             accs = [acc_w[part, :]] + [jnp.zeros((SUB, LANES), jnp.float32)] * 3
-            for i in range(block // LANES):
-                accs[i % 4] = accs[i % 4] + w_ref[q // wide, part, tile(q % wide * (block // LANES) + i)]
+            for i, t in enumerate(range(low, high)):
+                accs[i % 4] = accs[i % 4] + w_ref[h, part, tile(t)]
             acc_w[part, :] = (accs[0] + accs[1]) + (accs[2] + accs[3])
 
-    @pl.loop(low, high)
-    def _(b):
-        targets(b).wait()
-        part = rows_of(b)
-        accs = [jnp.zeros((SUB, LANES), jnp.float32)] * 4
-        for t in range(tiles):
-            accs[t % 4] = accs[t % 4] + tgt_ref[part, tile(t)].astype(jnp.float32)
-        acc_t[part, :] = (accs[0] + accs[1]) + (accs[2] + accs[3])
-
     row_sum = jnp.sum(acc_w[...].T, axis=0, keepdims=True)
-    share = jnp.sum(acc_t[...].T, axis=0, keepdims=True)
-    message(msg_ref, row_sum, share)
-
-
-def prepare_kernel(cid_hbm, cid_row_hbm, goal_row_hbm, tgt_ref, seg_ref, cols_ref, share_ref, cid_ref, cid_row, goal_row, sems):
+    message(msg_ref, row_sum, jnp.zeros((1, LANES), jnp.float32))
+
+
+def prepare_kernel(
+    cid_hbm, cid_row_hbm, goal_row_hbm, tgt_hbm, seg_ref, cols_ref, share_ref, share_row_ref, cid_ref, cid_row, goal_row, tgt_ref, acc_t, sems
+):
     copies = [
         pltpu.make_async_copy(cid_hbm, cid_ref, sems.at[0]),
         pltpu.make_async_copy(cid_row_hbm, cid_row, sems.at[1]),
@@ -149,11 +126,24 @@
     ]
     for copy in copies:
         copy.start()
+    acc_t[...] = jnp.zeros_like(acc_t)
     for copy in copies:
         copy.wait()
     rows = cid_ref.shape[0]
     counties, width = tgt_ref.shape
-    half = width // LANES // 2
+    tiles = width // LANES
+    half = tiles // 2
+
+    low = cid_ref[0] >> 3
+    high = (cid_ref[rows - 1] >> 3) + 1
+
+    def targets(b):
+        return pltpu.make_async_copy(tgt_hbm.at[rows_of(b)], tgt_ref.at[rows_of(b)], sems.at[3 + b])
+
+    @pl.loop(low, high)
+    def _(b):
+        targets(b).start()
+
     n, p, first = 0, 0, 0
     for g in range(rows):
         c = cid_ref[g]
@@ -175,6 +165,17 @@
     cols_ref[0] = column(cid_row[...].astype(jnp.float32))
     cols_ref[1] = column(goal_row[...].astype(jnp.float32))
 
+    @pl.loop(low, high)
+    def _(b):
+        targets(b).wait()
+        part = rows_of(b)
+        accs = [jnp.zeros((SUB, LANES), jnp.float32)] * 4
+        for t in range(tiles):
+            accs[t % 4] = accs[t % 4] + tgt_ref[part, tile(t)].astype(jnp.float32)
+        acc_t[part, :] = (accs[0] + accs[1]) + (accs[2] + accs[3])
+
+    message(share_row_ref, jnp.zeros((1, LANES), jnp.float32), jnp.sum(acc_t[...].T, axis=0, keepdims=True))
+
     sub = lax.broadcasted_iota(jnp.int32, (SUB, LANES), 0)
     none = jnp.zeros((SUB, LANES), jnp.float32)
 
@@ -184,7 +185,7 @@
         part = rows_of(c >> 3)
         mask = sub == (c & 7)
         for h in range(2):
-            own = [jnp.where(mask, tgt_ref[part, tile(h * half + t)].astype(jnp.float32), 0.0) for t in range(half)]
+            own = [jnp.where(mask, tgt_ref[part, tile(h * half + t)].astype(jnp.float32) * SHARE, 0.0) for t in range(half)]
             own += [none] * (-half % SUB)
             for t in range(0, len(own), SUB):
                 share_ref[k, h, t : t + SUB, :] = fold(own[t : t + SUB])
@@ -244,14 +245,14 @@
     seg_ref, refs = refs[0], refs[1:]
     msgs, refs, parts_ref = refs[:parts_n], refs[parts_n:-1], refs[-1]
     if second:
-        w_ref, cols_ref, r1_ref, edge_ref, sums_ref, rcol_ref = refs
+        w_ref, cols_ref, r1_ref, edge_ref, sums_ref, rcol_ref, total_ref = refs
     else:
-        _, w_ref, cols_ref, edge_ref, sums_ref, rcol_ref, total_ref = refs
+        _, w_ref, cols_ref, edge_ref, sums_ref, rcol_ref = refs
         r1_ref = rcol_ref
     total = msgs[0][...]
     for m in msgs[1:]:
         total = total + m[...]
-    if not second:
+    if second:
         total_ref[...] = total
     rcol = cols_ref[1] / column(total[0:1])
     rcol_ref[...] = rcol * SCALE if second else rcol
@@ -259,8 +260,20 @@
 
 
 def keep_kernel(second, seg_ref, w_ref, cols_ref, r1_ref, *refs):
-    r2_ref = refs[0] if second else None
-    sums_body(second, True, seg_ref, w_ref, cols_ref, r1_ref, r2_ref, *refs[-3:])
+    if not second:
+        sums_body(second, True, seg_ref, w_ref, cols_ref, r1_ref, None, *refs)
+        return
+    r2_ref, total_ref, scale_ref = refs[0], refs[1], refs[4]
+    sums_body(second, True, seg_ref, w_ref, cols_ref, r1_ref, r2_ref, refs[2], refs[3], refs[5])
+    share = total_ref[1:2, :]
+    lane = lax.broadcasted_iota(jnp.int32, (1, LANES), 1)
+
+    @pl.loop(0, (seg_counts(seg_ref)[0] + 3) // 4)
+    def _(g):
+        for i in range(4):
+            k = 4 * g + i
+            whole = jnp.sum(jnp.where(lane == seg_name(seg_ref, k), share, 0.0), axis=1, keepdims=True)
+            scale_ref[pl.ds(k, 1), :] = jnp.broadcast_to((1.0 / SHARE) / whole, (1, LANES))
 
 
 def join(refs):
@@ -340,21 +353,18 @@
     body(n - 1, edge_ref.at[1])
 
 
-def rows_kernel(mine, seg_ref, total_ref, w_ref, cols_ref, r1_ref, sums_ref, edge_ref, share_ref, *refs):
+def rows_kernel(mine, seg_ref, w_ref, cols_ref, r1_ref, sums_ref, edge_ref, share_ref, *refs):
     if mine:
         goal_ref, acc_ref, fac_ref = refs
     else:
-        part_ref, goal_ref, msg_ref, fac_ref, acc_ref = refs
+        part_ref, share_row_ref, goal_ref, msg_ref, fac_ref, acc_ref = refs
     w_ref = w_ref.at[side_of(mine)]
     half = w_ref.shape[1] // LANES
     side = side_of(mine)
     n = seg_counts(seg_ref)[0]
-    share = total_ref[1:2, :]
-    lane = lax.broadcasted_iota(jnp.int32, (1, LANES), 1)
 
     def factor(k, sum_ref):
-        whole = jnp.sum(jnp.where(lane == seg_name(seg_ref, k), share, 0.0), axis=1, keepdims=True)
-        goal = share_ref[k, side] * (sum_ref[half : half + 1, :] / whole)
+        goal = share_ref[k, side] * sum_ref[half : half + 1, :]
         goal_ref[k] = goal
         fac_ref[k] = goal / sum_ref[...]
 
@@ -371,16 +381,16 @@
 
     each_pair(seg_ref, cols_ref, pair)
     if not mine:
-        message(msg_ref, jnp.sum(acc_ref[...].T, axis=0, keepdims=True), jnp.zeros((1, LANES), jnp.float32))
-
-
-def fitted(mine, chunks, done, seg_ref, w_ref, cols_ref, r1_ref, r2_ref, goal_ref, sums_ref, edge_ref, out_ref, fac_ref):
+        message(msg_ref, jnp.sum(acc_ref[...].T, axis=0, keepdims=True), share_row_ref[1:2, :])
+
+
+def fitted(mine, chunks, done, seg_ref, w_ref, cols_ref, r1_ref, r2_ref, goal_ref, scale_ref, sums_ref, edge_ref, out_ref, fac_ref):
     w_ref = w_ref.at[side_of(mine)]
     half = w_ref.shape[1] // LANES
     n = seg_counts(seg_ref)[0]
 
     def factor(k, sum_ref):
-        fac_ref[k] = 100.0 * (goal_ref[k] / sum_ref[...])
+        fac_ref[k] = 100.0 * (goal_ref[k] * scale_ref[pl.ds(k, 1), :] / sum_ref[...])
 
     each_sum(n, edge_ref, sums_ref, factor)
     for q in range(chunks):
@@ -397,12 +407,12 @@
         done(q)
 
 
-def last_own_kernel(seg_ref, w_ref, cols_ref, r1_ref, r2_ref, goal_ref, sums_ref, edge_ref, out_ref, fac_ref):
-    fitted(True, 1, lambda q: None, seg_ref, w_ref, cols_ref, r1_ref, r2_ref, goal_ref, sums_ref, edge_ref, out_ref, fac_ref)
+def last_own_kernel(seg_ref, w_ref, cols_ref, r1_ref, r2_ref, goal_ref, scale_ref, sums_ref, edge_ref, out_ref, fac_ref):
+    fitted(True, 1, lambda q: None, seg_ref, w_ref, cols_ref, r1_ref, r2_ref, goal_ref, scale_ref, sums_ref, edge_ref, out_ref, fac_ref)
 
 
 def last_kernel(
-    chunks, seg_ref, w_ref, cols_ref, r1_ref, r2_ref, goal_ref, sums_ref, edge_ref, own_ref, out_hbm, out_ref, fac_ref, sems
+    chunks, seg_ref, w_ref, cols_ref, r1_ref, r2_ref, goal_ref, scale_ref, sums_ref, edge_ref, own_ref, out_hbm, out_ref, fac_ref, sems
 ):
     width = w_ref.shape[2]
     block = width // chunks
@@ -422,7 +432,7 @@
         copy.start()
         copies.append(copy)
 
-    fitted(False, chunks, done, seg_ref, w_ref, cols_ref, r1_ref, r2_ref, goal_ref, sums_ref, edge_ref, out_ref, fac_ref)
+    fitted(False, chunks, done, seg_ref, w_ref, cols_ref, r1_ref, r2_ref, goal_ref, scale_ref, sums_ref, edge_ref, out_ref, fac_ref)
     for copy in copies:
         copy.wait()
 
@@ -455,20 +465,16 @@
     column_of = f32(rows, LANES)
     small = f32(SUB, LANES)
     parts_scratch = [pltpu.VMEM((half_rows * SUB, LANES), jnp.float32)]
-    hbm = [pltpu.with_memory_space_constraint(x, pltpu.HBM) for x in (county_id, county_id.reshape(1, rows), row_target.reshape(1, rows))]
-    msg, slab, targets = call(
+    inputs = (county_id, county_id.reshape(1, rows), row_target.reshape(1, rows), county_target, seed_slab)
+    hbm = [pltpu.with_memory_space_constraint(x, pltpu.HBM) for x in inputs]
+    msg, slab = call(
         first_kernel,
         "row_sums_1",
-        [hbm[0]] + [pltpu.with_memory_space_constraint(x, pltpu.HBM) for x in (seed_slab, county_target)],
-        [HBM] * 3,
-        (small, f32(2, rows, width // 2), jax.ShapeDtypeStruct((counties, width), jnp.int32)),
-        None,
-        [
-            pltpu.SMEM((rows,), jnp.int32),
-            pltpu.VMEM((rows, LANES), jnp.float32),
-            pltpu.VMEM((LANES, LANES), jnp.float32),
-            pltpu.SemaphoreType.DMA((1 + CHUNKS + counties // SUB,)),
-        ],
+        hbm[4:],
+        [HBM],
+        (small, f32(2, rows, width // 2)),
+        None,
+        [pltpu.VMEM((rows, LANES), jnp.float32), pltpu.SemaphoreType.DMA((5,))],
     )
 
     def swap(x, axis, size, mask):
@@ -487,33 +493,35 @@
         send = call(plane_kernel, "plane_sums", [chip] + chips, [VMEM] * (PLANE // 2), f32(planes, half_rows, LANES))
         far = lax.all_to_all(send, "bg", 0, 0, axis_index_groups=lines)
         own, other = call(edge_kernel, "edge_sums", [keep[0], got, far] + chips, [VMEM] * (2 + PLANE // 2), (edge, edge))
-        return own, swap(other, "bg", device, 1), keep[1]
+        return own, swap(other, "bg", device, 1), keep[1:]
 
     msgs = over_type(msg)
-    seg, cols, share = call(
+    seg, cols, share, share_row = call(
         prepare_kernel,
         "prepare",
-        hbm + [targets],
-        [HBM] * 3 + [VMEM],
-        (jax.ShapeDtypeStruct((table_rows(counties), LANES), jnp.int32), f32(2, rows, LANES), f32(counties, 2, half_rows, LANES)),
+        hbm[:4],
+        [HBM] * 4,
+        (jax.ShapeDtypeStruct((table_rows(counties), LANES), jnp.int32), f32(2, rows, LANES), f32(counties, 2, half_rows, LANES), small),
         None,
         [
             pltpu.SMEM((rows,), jnp.int32),
             pltpu.VMEM((1, rows), jnp.int32),
             pltpu.VMEM((1, rows), jnp.int32),
-            pltpu.SemaphoreType.DMA((3,)),
+            pltpu.VMEM((counties, width), jnp.int32),
+            pltpu.VMEM((LANES, LANES), jnp.float32),
+            pltpu.SemaphoreType.DMA((3 + counties // SUB,)),
         ],
     )
-    give, sums_give, r1, total = call(
+    give, sums_give, r1 = call(
         functools.partial(give_kernel, False, parts),
         "county_sums_1a",
         [seg] + msgs + [share, slab, cols],
         [VMEM] * (parts + 4),
-        (edge, table, column_of, small),
+        (edge, table, column_of),
         None,
         parts_scratch,
     )
-    own, other, sums_keep = edges(
+    own, other, (sums_keep,) = edges(
         give,
         lambda: call(functools.partial(keep_kernel, False), "county_sums_1b", (seg, slab, cols, r1), [VMEM] * 4, (edge, table), None, parts_scratch),
     )
@@ -521,8 +529,8 @@
     goal_keep, part = call(
         functools.partial(rows_kernel, True),
         "row_sums_2a",
-        (seg, total, slab, cols, r1, sums_keep, own, share),
-        [VMEM] * 8,
+        (seg, slab, cols, r1, sums_keep, own, share),
+        [VMEM] * 7,
         (table, column_of),
         None,
         [fac],
@@ -530,30 +538,30 @@
     goal_give, msg = call(
         functools.partial(rows_kernel, False),
         "row_sums_2b",
-        (seg, total, slab, cols, r1, sums_give, other, share, part),
+        (seg, slab, cols, r1, sums_give, other, share, part, share_row),
         [VMEM] * 9,
         (table, small),
         None,
         [fac, pltpu.VMEM((rows, LANES), jnp.float32)],
     )
-    give, sums_give, r2 = call(
+    give, sums_give, r2, total = call(
         functools.partial(give_kernel, True, parts),
         "county_sums_2a",
         [seg] + over_type(msg) + [slab, cols, r1],
         [VMEM] * (parts + 4),
-        (edge, table, column_of),
+        (edge, table, column_of, small),
         None,
         parts_scratch,
     )
-    own, other, sums_keep = edges(
+    own, other, (sums_keep, scale) = edges(
         give,
-        lambda: call(functools.partial(keep_kernel, True), "county_sums_2b", (seg, slab, cols, r1, r2), [VMEM] * 5, (edge, table), None, parts_scratch),
+        lambda: call(functools.partial(keep_kernel, True), "county_sums_2b", (seg, slab, cols, r1, r2, total), [VMEM] * 6, (edge, table, f32(counties, LANES)), None, parts_scratch),
     )
     mine = call(
         last_own_kernel,
         "fitted_a",
-        (seg, slab, cols, r1, r2, goal_keep, sums_keep, own),
-        [VMEM] * 8,
+        (seg, slab, cols, r1, r2, goal_keep, scale, sums_keep, own),
+        [VMEM] * 9,
         f32(rows, width // 2),
         None,
         [fac],
@@ -561,8 +569,8 @@
     return call(
         functools.partial(last_kernel, out_chunks),
         "fitted_b",
-        (seg, slab, cols, r1, r2, goal_give, sums_give, other, mine),
-        [VMEM] * 9,
+        (seg, slab, cols, r1, r2, goal_give, scale, sums_give, other, mine),
+        [VMEM] * 10,
         f32(rows, width),
         HBM,
         [pltpu.VMEM((rows, width // 2), jnp.float32), fac, pltpu.SemaphoreType.DMA((2 * out_chunks,))],

time: 73.8 us -> 73.7 us (level)
    ppermute x16, waiting for transfers between devices: 10.8 us -> 10.1 us  [swap(): return lax.ppermute(x, axis, [(i, i ^ mask) for i in range(size)])]
  transfers between devices with their start and end apart: 16 -> 16, of which waited for: 11 -> 11; matrix products, arithmetic and copies ran while one was open for 0% -> 0% of each run, Pallas kernels for 5% -> 6%
where the time goes in v6:
time: 73.7 us; the launch traced here: 73.5 us
  blocking collectives  27.2 us (37%)
  starting transfers between devices  24.8 us (34%)
  Pallas kernels  11.4 us (15%)
  waiting for transfers between devices  10.1 us (14%)
    all_to_all x2, blocking collectives, edges(): far = lax.all_to_all(send, 'bg', 0, 0, axis_index_groups=lines)  27.2 us
    ppermute x16, starting transfers between devices, swap(): return lax.ppermute(x, axis, [(i, i ^ mask) for i in range(size)])  24.8 us
    pallas_call x16, Pallas kernels, call(): pl.pallas_call(kernel, out_shape=out_shape, in_specs=in_specs, out_specs=...  11.4 us
    ppermute x16, waiting for transfers between devices, swap(): return lax.ppermute(x, axis, [(i, i ^ mask) for i in range(size)])  10.1 us
  transfers between devices with their start and end apart: 16, of which 11 were waited for; matrix products, arithmetic and copies ran while one was open for 0% of the time, Pallas kernels for 6%

profile of v6, /device:TPU:1, one launch (start us, length us, event | category | flops | bytes accessed | tf_op | source)
XLA Modules:
  0.0 73.5 jit_solution(2058836419570600320)
XLA Ops:
  0.0 2.6 %row_sums_1.1 = (f32[8,128]{1,0:T(8,128)S(1)}, f32[2,128,4608]{2,1,0:T(8,128)S(1)}) custom-call(f32[128,9216]{1,0:T(8,128)} %w_hbm.1), custom_call_target="tpu_custom_call" | custom-call | flops 4194304 | bytes 4194304 | tf_op jit(solution)/shard_map/row_sums_1/pallas_call | solution.py:443
  2.6 3.7 %collective-permute-start.2 = (f32[8,128]{1,0:T(8,128)S(1)}, f32[8,128]{1,0:T(8,128)S(1)}, u32[]{:S(2)}, u32[]{:S(2)}) collective-permute-start(f32[8,128]{1,0:T(8,128)S(1)} %get-tuple-element.34.refs_1_), channel_id=1, source_target_pairs={{0,3},{1,2},{2,1},{3,0},{4,7},{5,6},{6,5},{7,4},{8,11},{9,10},{10,... | collective-permute-start | bytes 12296 | tf_op jit(solution)/shard_map/ppermute | solution.py:481
  7.0 2.0 %prepare.1 = (s32[216,128]{1,0:T(8,128)S(1)}, f32[2,128,128]{2,1,0:T(8,128)S(1)}, f32[64,2,40,128]{3,2,1,0:T(8,128)S(1)}, f32[8,128]{1,0:T(8,128)S(1)}) custom-call(s32[128]{0:T(128)} %cid_hbm.1, s32[1,128]{1,0:T(1,128)} %bitcast.2, s32[1,128]{1,0:T(1,128)} %bitcast.3, s32[64,9216]{1,0:T(8,128)} %tgt_hbm.1), custom_call_target="tpu_custom_call" | custom-call | flops 4194304 | bytes 4194304 | tf_op jit(solution)/shard_map/prepare/pallas_call | solution.py:443
  9.0 1.3 %collective-permute-done.1.refs_3_ = f32[8,128]{1,0:T(8,128)S(1)} collective-permute-done((f32[8,128]{1,0:T(8,128)S(1)}, f32[8,128]{1,0:T(8,128)S(1)}, u32[]{:S(2)}, u32[]{:S(2)}) %collective-permute-start.1) | collective-permute-done | bytes 4128 | tf_op jit(solution)/shard_map/ppermute | solution.py:481
  10.8 2.2 %collective-permute-start.3 = (f32[2,40,128]{2,1,0:T(8,128)S(1)}, f32[2,40,128]{2,1,0:T(8,128)S(1)}, u32[]{:S(2)}, u32[]{:S(2)}) collective-permute-start(f32[2,40,128]{2,1,0:T(8,128)S(1)} %get-tuple-element.39), channel_id=1, source_target_pairs={{0,4},{4,0},{8,12},{12,8},{16,20},{20,16},{24,28},{28,24},{32,36},... | collective-permute-start | bytes 122888 | tf_op jit(solution)/shard_map/ppermute | solution.py:481
  13.8 2.6 %collective-permute-start.6 = (f32[2,40,128]{2,1,0:T(8,128)S(1)}, f32[2,40,128]{2,1,0:T(8,128)S(1)}, u32[]{:S(2)}, u32[]{:S(2)}) collective-permute-start(f32[2,40,128]{2,1,0:T(8,128)S(1)} %chip_sums.2.refs_0_), channel_id=1, source_target_pairs={{0,24},{4,28},{8,16},{12,20},{16,8},{20,12},{24,0},{28,4},{32,56},... | collective-permute-start | bytes 122888 | tf_op jit(solution)/shard_map/ppermute | solution.py:481
  17.2 0.8 %collective-permute-done.6.refs_3_.refs_2_ = f32[2,40,128]{2,1,0:T(8,128)S(1)} collective-permute-done((f32[2,40,128]{2,1,0:T(8,128)S(1)}, f32[2,40,128]{2,1,0:T(8,128)S(1)}, u32[]{:S(2)}, u32[]{:S(2)}) %collective-permute-start.6) | collective-permute-done | bytes 40992 | tf_op jit(solution)/shard_map/ppermute | solution.py:481
  18.0 2.8 %collective-permute-done.5.refs_2_.refs_1_ = f32[2,40,128]{2,1,0:T(8,128)S(1)} collective-permute-done((f32[2,40,128]{2,1,0:T(8,128)S(1)}, f32[2,40,128]{2,1,0:T(8,128)S(1)}, u32[]{:S(2)}, u32[]{:S(2)}) %collective-permute-start.5) | collective-permute-done | bytes 40992 | tf_op jit(solution)/shard_map/ppermute | solution.py:481
  20.8 16.5 %all_to_all.10.far_ref = f32[8,40,128]{2,1,0:T(8,128)S(1)} all-to-all(f32[8,40,128]{2,1,0:T(8,128)S(1)} %plane_sums.2), channel_id=1, replica_groups={{0,32,64,96,128,160,192,224},{4,36,68,100,132,164,196,228},{8,40,72,104..., dimensions={0} | all-to-all | bytes 327680 | tf_op jit(solution)/shard_map/all_to_all | solution.py:494
  37.5 3.2 %collective-permute-start.7 = (f32[2,40,128]{2,1,0:T(8,128)S(1)}, f32[2,40,128]{2,1,0:T(8,128)S(1)}, u32[]{:S(2)}, u32[]{:S(2)}) collective-permute-start(f32[2,40,128]{2,1,0:T(8,128)S(1)} %get-tuple-element.40), channel_id=1, source_target_pairs={{0,4},{4,0},{8,12},{12,8},{16,20},{20,16},{24,28},{28,24},{32,36},... | collective-permute-start | bytes 122888 | tf_op jit(solution)/shard_map/ppermute | solution.py:481
  41.6 0.7 row_sums_2b.1
  42.3 1.1 %collective-permute-start.10 = (f32[8,128]{1,0:T(8,128)S(1)}, f32[8,128]{1,0:T(8,128)S(1)}, u32[]{:S(2)}, u32[]{:S(2)}) collective-permute-start(f32[8,128]{1,0:T(8,128)S(1)} %get-tuple-element.45.refs_1_), channel_id=1, source_target_pairs={{0,3},{1,2},{2,1},{3,0},{4,7},{5,6},{6,5},{7,4},{8,11},{9,10},{10,... | collective-permute-start | bytes 12296 | tf_op jit(solution)/shard_map/ppermute | solution.py:481
  43.4 0.8 %collective-permute-start.9 = (f32[8,128]{1,0:T(8,128)S(1)}, f32[8,128]{1,0:T(8,128)S(1)}, u32[]{:S(2)}, u32[]{:S(2)}) collective-permute-start(f32[8,128]{1,0:T(8,128)S(1)} %get-tuple-element.45.refs_1_), channel_id=1, source_target_pairs={{0,2},{1,3},{2,0},{3,1},{4,6},{5,7},{6,4},{7,5},{8,10},{9,11},{10,... | collective-permute-start | bytes 12296 | tf_op jit(solution)/shard_map/ppermute | solution.py:481
  44.2 1.4 %collective-permute-start.8 = (f32[8,128]{1,0:T(8,128)S(1)}, f32[8,128]{1,0:T(8,128)S(1)}, u32[]{:S(2)}, u32[]{:S(2)}) collective-permute-start(f32[8,128]{1,0:T(8,128)S(1)} %get-tuple-element.45.refs_1_), channel_id=1, source_target_pairs={{0,1},{1,0},{2,3},{3,2},{4,5},{5,4},{6,7},{7,6},{8,9},{9,8},{10,11... | collective-permute-start | bytes 12296 | tf_op jit(solution)/shard_map/ppermute | solution.py:481
  46.1 1.3 %collective-permute-done.9.refs_3_ = f32[8,128]{1,0:T(8,128)S(1)} collective-permute-done((f32[8,128]{1,0:T(8,128)S(1)}, f32[8,128]{1,0:T(8,128)S(1)}, u32[]{:S(2)}, u32[]{:S(2)}) %collective-permute-start.9) | collective-permute-done | bytes 4128 | tf_op jit(solution)/shard_map/ppermute | solution.py:481
  48.0 1.9 %collective-permute-start.11 = (f32[2,40,128]{2,1,0:T(8,128)S(1)}, f32[2,40,128]{2,1,0:T(8,128)S(1)}, u32[]{:S(2)}, u32[]{:S(2)}) collective-permute-start(f32[2,40,128]{2,1,0:T(8,128)S(1)} %get-tuple-element.52), channel_id=1, source_target_pairs={{0,4},{4,0},{8,12},{12,8},{16,20},{20,16},{24,28},{28,24},{32,36},... | collective-permute-start | bytes 122888 | tf_op jit(solution)/shard_map/ppermute | solution.py:481
  50.7 1.3 %collective-permute-start.14 = (f32[2,40,128]{2,1,0:T(8,128)S(1)}, f32[2,40,128]{2,1,0:T(8,128)S(1)}, u32[]{:S(2)}, u32[]{:S(2)}) collective-permute-start(f32[2,40,128]{2,1,0:T(8,128)S(1)} %chip_sums.3.refs_0_), channel_id=1, source_target_pairs={{0,24},{4,28},{8,16},{12,20},{16,8},{20,12},{24,0},{28,4},{32,56},... | collective-permute-start | bytes 122888 | tf_op jit(solution)/shard_map/ppermute | solution.py:481
  52.0 0.8 %collective-permute-start.13 = (f32[2,40,128]{2,1,0:T(8,128)S(1)}, f32[2,40,128]{2,1,0:T(8,128)S(1)}, u32[]{:S(2)}, u32[]{:S(2)}) collective-permute-start(f32[2,40,128]{2,1,0:T(8,128)S(1)} %chip_sums.3.refs_0_), channel_id=1, source_target_pairs={{0,16},{4,20},{8,24},{12,28},{16,0},{20,4},{24,8},{28,12},{32,48},... | collective-permute-start | bytes 122888 | tf_op jit(solution)/shard_map/ppermute | solution.py:481
  52.8 1.3 %collective-permute-start.12 = (f32[2,40,128]{2,1,0:T(8,128)S(1)}, f32[2,40,128]{2,1,0:T(8,128)S(1)}, u32[]{:S(2)}, u32[]{:S(2)}) collective-permute-start(f32[2,40,128]{2,1,0:T(8,128)S(1)} %chip_sums.3.refs_0_), channel_id=1, source_target_pairs={{0,8},{4,12},{8,0},{12,4},{16,24},{20,28},{24,16},{28,20},{32,40},... | collective-permute-start | bytes 122888 | tf_op jit(solution)/shard_map/ppermute | solution.py:481
  54.1 0.8 %collective-permute-done.14.refs_3_.refs_2_ = f32[2,40,128]{2,1,0:T(8,128)S(1)} collective-permute-done((f32[2,40,128]{2,1,0:T(8,128)S(1)}, f32[2,40,128]{2,1,0:T(8,128)S(1)}, u32[]{:S(2)}, u32[]{:S(2)}) %collective-permute-start.14) | collective-permute-done | bytes 40992 | tf_op jit(solution)/shard_map/ppermute | solution.py:481
  54.9 1.5 %collective-permute-done.13.refs_2_.refs_1_ = f32[2,40,128]{2,1,0:T(8,128)S(1)} collective-permute-done((f32[2,40,128]{2,1,0:T(8,128)S(1)}, f32[2,40,128]{2,1,0:T(8,128)S(1)}, u32[]{:S(2)}, u32[]{:S(2)}) %collective-permute-start.13) | collective-permute-done | bytes 40992 | tf_op jit(solution)/shard_map/ppermute | solution.py:481
  56.5 10.7 %all_to_all.11.far_ref = f32[8,40,128]{2,1,0:T(8,128)S(1)} all-to-all(f32[8,40,128]{2,1,0:T(8,128)S(1)} %plane_sums.3), channel_id=1, replica_groups={{0,32,64,96,128,160,192,224},{4,36,68,100,132,164,196,228},{8,40,72,104..., dimensions={0} | all-to-all | bytes 327680 | tf_op jit(solution)/shard_map/all_to_all | solution.py:494
  67.3 3.2 %collective-permute-start.15 = (f32[2,40,128]{2,1,0:T(8,128)S(1)}, f32[2,40,128]{2,1,0:T(8,128)S(1)}, u32[]{:S(2)}, u32[]{:S(2)}) collective-permute-start(f32[2,40,128]{2,1,0:T(8,128)S(1)} %get-tuple-element.53), channel_id=1, source_target_pairs={{0,4},{4,0},{8,12},{12,8},{16,20},{20,16},{24,28},{28,24},{32,36},... | collective-permute-start | bytes 122888 | tf_op jit(solution)/shard_map/ppermute | solution.py:481
  71.3 2.2 %fitted_b.1 = f32[128,9216]{1,0:T(8,128)} custom-call(s32[216,128]{1,0:T(8,128)S(1)} %get-tuple-element.31.refs_0_.seg_ref, f32[2,128,4608]{2,1,0:T(8,128)S(1)} %get-tuple-element.32.refs_6_.w_ref.refs_5_, f32[2,128,128]{2,1,0:T(8,128)S(1)} %get-tuple-element.33.refs_7_.cols_ref.refs_6_, f32[128,128]{1,0:T(8,128)S(1)} %get-tuple-element.36.r1_ref.refs_7_, ...), custom_call_target="tpu_custom_call" | custom-call | flops 4194304 | bytes 4194304 | tf_op jit(solution)/shard_map/fitted_b/pallas_call | solution.py:443
  (26 shorter events, 6.9 us)
Async XLA Ops:
  2.6 6.3 %collective-permute-start.2 = (f32[8,128]{1,0:T(8,128)S(1)}, f32[8,128]{1,0:T(8,128)S(1)}, u32[]{:S(2)}, u32[]{:S(2)}) collective-permute-start(f32[8,128]{1,0:T(8,128)S(1)} %get-tuple-element.34.refs_1_), channel_id=1, source_target_pairs={{0,3},{1,2},{2,1},{3,0},{4,7},{5,6},{6,5},{7,4},{8,11},{9,10},{10,... | collective-permute-start | bytes 12296 | tf_op jit(solution)/shard_map/ppermute | solution.py:481
  6.3 4.0 %collective-permute-start.1 = (f32[8,128]{1,0:T(8,128)S(1)}, f32[8,128]{1,0:T(8,128)S(1)}, u32[]{:S(2)}, u32[]{:S(2)}) collective-permute-start(f32[8,128]{1,0:T(8,128)S(1)} %get-tuple-element.34.refs_1_), channel_id=1, source_target_pairs={{0,2},{1,3},{2,0},{3,1},{4,6},{5,7},{6,4},{7,5},{8,10},{9,11},{10,... | collective-permute-start | bytes 12296 | tf_op jit(solution)/shard_map/ppermute | solution.py:481
  6.6 3.6 %collective-permute-start = (f32[8,128]{1,0:T(8,128)S(1)}, f32[8,128]{1,0:T(8,128)S(1)}, u32[]{:S(2)}, u32[]{:S(2)}) collective-permute-start(f32[8,128]{1,0:T(8,128)S(1)} %get-tuple-element.34.refs_1_), channel_id=1, source_target_pairs={{0,1},{1,0},{2,3},{3,2},{4,5},{5,4},{6,7},{7,6},{8,9},{9,8},{10,11... | collective-permute-start | bytes 12296 | tf_op jit(solution)/shard_map/ppermute | solution.py:481
  10.8 3.1 %collective-permute-start.3 = (f32[2,40,128]{2,1,0:T(8,128)S(1)}, f32[2,40,128]{2,1,0:T(8,128)S(1)}, u32[]{:S(2)}, u32[]{:S(2)}) collective-permute-start(f32[2,40,128]{2,1,0:T(8,128)S(1)} %get-tuple-element.39), channel_id=1, source_target_pairs={{0,4},{4,0},{8,12},{12,8},{16,20},{20,16},{24,28},{28,24},{32,36},... | collective-permute-start | bytes 122888 | tf_op jit(solution)/shard_map/ppermute | solution.py:481
  13.8 4.2 %collective-permute-start.6 = (f32[2,40,128]{2,1,0:T(8,128)S(1)}, f32[2,40,128]{2,1,0:T(8,128)S(1)}, u32[]{:S(2)}, u32[]{:S(2)}) collective-permute-start(f32[2,40,128]{2,1,0:T(8,128)S(1)} %chip_sums.2.refs_0_), channel_id=1, source_target_pairs={{0,24},{4,28},{8,16},{12,20},{16,8},{20,12},{24,0},{28,4},{32,56},... | collective-permute-start | bytes 122888 | tf_op jit(solution)/shard_map/ppermute | solution.py:481
  16.4 4.4 %collective-permute-start.5 = (f32[2,40,128]{2,1,0:T(8,128)S(1)}, f32[2,40,128]{2,1,0:T(8,128)S(1)}, u32[]{:S(2)}, u32[]{:S(2)}) collective-permute-start(f32[2,40,128]{2,1,0:T(8,128)S(1)} %chip_sums.2.refs_0_), channel_id=1, source_target_pairs={{0,16},{4,20},{8,24},{12,28},{16,0},{20,4},{24,8},{28,12},{32,48},... | collective-permute-start | bytes 122888 | tf_op jit(solution)/shard_map/ppermute | solution.py:481
  16.9 3.8 %collective-permute-start.4 = (f32[2,40,128]{2,1,0:T(8,128)S(1)}, f32[2,40,128]{2,1,0:T(8,128)S(1)}, u32[]{:S(2)}, u32[]{:S(2)}) collective-permute-start(f32[2,40,128]{2,1,0:T(8,128)S(1)} %chip_sums.2.refs_0_), channel_id=1, source_target_pairs={{0,8},{4,12},{8,0},{12,4},{16,24},{20,28},{24,16},{28,20},{32,40},... | collective-permute-start | bytes 122888 | tf_op jit(solution)/shard_map/ppermute | solution.py:481
  37.5 4.1 %collective-permute-start.7 = (f32[2,40,128]{2,1,0:T(8,128)S(1)}, f32[2,40,128]{2,1,0:T(8,128)S(1)}, u32[]{:S(2)}, u32[]{:S(2)}) collective-permute-start(f32[2,40,128]{2,1,0:T(8,128)S(1)} %get-tuple-element.40), channel_id=1, source_target_pairs={{0,4},{4,0},{8,12},{12,8},{16,20},{20,16},{24,28},{28,24},{32,36},... | collective-permute-start | bytes 122888 | tf_op jit(solution)/shard_map/ppermute | solution.py:481
  42.3 3.8 %collective-permute-start.10 = (f32[8,128]{1,0:T(8,128)S(1)}, f32[8,128]{1,0:T(8,128)S(1)}, u32[]{:S(2)}, u32[]{:S(2)}) collective-permute-start(f32[8,128]{1,0:T(8,128)S(1)} %get-tuple-element.45.refs_1_), channel_id=1, source_target_pairs={{0,3},{1,2},{2,1},{3,0},{4,7},{5,6},{6,5},{7,4},{8,11},{9,10},{10,... | collective-permute-start | bytes 12296 | tf_op jit(solution)/shard_map/ppermute | solution.py:481
  43.4 4.0 %collective-permute-start.9 = (f32[8,128]{1,0:T(8,128)S(1)}, f32[8,128]{1,0:T(8,128)S(1)}, u32[]{:S(2)}, u32[]{:S(2)}) collective-permute-start(f32[8,128]{1,0:T(8,128)S(1)} %get-tuple-element.45.refs_1_), channel_id=1, source_target_pairs={{0,2},{1,3},{2,0},{3,1},{4,6},{5,7},{6,4},{7,5},{8,10},{9,11},{10,... | collective-permute-start | bytes 12296 | tf_op jit(solution)/shard_map/ppermute | solution.py:481
  44.2 3.2 %collective-permute-start.8 = (f32[8,128]{1,0:T(8,128)S(1)}, f32[8,128]{1,0:T(8,128)S(1)}, u32[]{:S(2)}, u32[]{:S(2)}) collective-permute-start(f32[8,128]{1,0:T(8,128)S(1)} %get-tuple-element.45.refs_1_), channel_id=1, source_target_pairs={{0,1},{1,0},{2,3},{3,2},{4,5},{5,4},{6,7},{7,6},{8,9},{9,8},{10,11... | collective-permute-start | bytes 12296 | tf_op jit(solution)/shard_map/ppermute | solution.py:481
  48.0 2.7 %collective-permute-start.11 = (f32[2,40,128]{2,1,0:T(8,128)S(1)}, f32[2,40,128]{2,1,0:T(8,128)S(1)}, u32[]{:S(2)}, u32[]{:S(2)}) collective-permute-start(f32[2,40,128]{2,1,0:T(8,128)S(1)} %get-tuple-element.52), channel_id=1, source_target_pairs={{0,4},{4,0},{8,12},{12,8},{16,20},{20,16},{24,28},{28,24},{32,36},... | collective-permute-start | bytes 122888 | tf_op jit(solution)/shard_map/ppermute | solution.py:481
  50.7 4.2 %collective-permute-start.14 = (f32[2,40,128]{2,1,0:T(8,128)S(1)}, f32[2,40,128]{2,1,0:T(8,128)S(1)}, u32[]{:S(2)}, u32[]{:S(2)}) collective-permute-start(f32[2,40,128]{2,1,0:T(8,128)S(1)} %chip_sums.3.refs_0_), channel_id=1, source_target_pairs={{0,24},{4,28},{8,16},{12,20},{16,8},{20,12},{24,0},{28,4},{32,56},... | collective-permute-start | bytes 122888 | tf_op jit(solution)/shard_map/ppermute | solution.py:481
  52.0 4.4 %collective-permute-start.13 = (f32[2,40,128]{2,1,0:T(8,128)S(1)}, f32[2,40,128]{2,1,0:T(8,128)S(1)}, u32[]{:S(2)}, u32[]{:S(2)}) collective-permute-start(f32[2,40,128]{2,1,0:T(8,128)S(1)} %chip_sums.3.refs_0_), channel_id=1, source_target_pairs={{0,16},{4,20},{8,24},{12,28},{16,0},{20,4},{24,8},{28,12},{32,48},... | collective-permute-start | bytes 122888 | tf_op jit(solution)/shard_map/ppermute | solution.py:481
  52.8 3.6 %collective-permute-start.12 = (f32[2,40,128]{2,1,0:T(8,128)S(1)}, f32[2,40,128]{2,1,0:T(8,128)S(1)}, u32[]{:S(2)}, u32[]{:S(2)}) collective-permute-start(f32[2,40,128]{2,1,0:T(8,128)S(1)} %chip_sums.3.refs_0_), channel_id=1, source_target_pairs={{0,8},{4,12},{8,0},{12,4},{16,24},{20,28},{24,16},{28,20},{32,40},... | collective-permute-start | bytes 122888 | tf_op jit(solution)/shard_map/ppermute | solution.py:481
  67.3 4.0 %collective-permute-start.15 = (f32[2,40,128]{2,1,0:T(8,128)S(1)}, f32[2,40,128]{2,1,0:T(8,128)S(1)}, u32[]{:S(2)}, u32[]{:S(2)}) collective-permute-start(f32[2,40,128]{2,1,0:T(8,128)S(1)} %get-tuple-element.53), channel_id=1, source_target_pairs={{0,4},{4,0},{8,12},{12,8},{16,20},{20,16},{24,28},{28,24},{32,36},... | collective-permute-start | bytes 122888 | tf_op jit(solution)/shard_map/ppermute | solution.py:481

commit v7 on v6

--- a/solution.py
+++ b/solution.py
@@ -196,14 +196,15 @@
     return core if mine else 1 - core
 
 
-def sums_body(second, mine, seg_ref, w_ref, cols_ref, r1_ref, r2_ref, edge_ref, sums_ref, parts_ref):
+def sums_body(second, mine, ends, seg_ref, w_ref, cols_ref, r1_ref, r2_ref, sums_ref, parts_ref):
     w_ref = w_ref.at[side_of(mine)]
     half = w_ref.shape[1] // LANES
     n = seg_counts(seg_ref)[0]
     sub = lax.broadcasted_iota(jnp.int32, (SUB, LANES), 0)
     none = jnp.zeros((SUB, LANES), jnp.float32)
 
-    def county(k, place):
+    def county(at, place):
+        k = at * (n - 1) if ends else at
         name = seg_name(seg_ref, k).astype(jnp.float32)
 
         def block(b, accs):
@@ -222,7 +223,7 @@
             return tuple(out)
 
         parts = list(lax.fori_loop(place & 255, place >> 8, block, (none,) * (half if second else half + 1)))
-        following = seg_number(seg_ref, k + 1)
+        following = seg_number(seg_ref, n - 1 if ends else k + 1)
         if second:
             parts.append(none)
         parts.append(jnp.where(sub == 0, name, 0.0))
@@ -233,21 +234,27 @@
             folded = [parts_ref[pl.ds(t * SUB + i, SUB, stride=SUB), :] for i in range(SUB)]
             while len(folded) > 1:
                 folded = [x + y for x, y in zip(folded[0::2], folded[1::2])]
-            sums_ref[k, t : t + SUB, :] = folded[0]
+            sums_ref[at, t : t + SUB, :] = folded[0]
         return following
 
-    lax.fori_loop(0, n, county, seg_number(seg_ref, 0))
-    edge_ref[0] = sums_ref[0]
-    edge_ref[1] = sums_ref[n - 1]
+    if ends:
+        lax.fori_loop(0, jnp.minimum(n, 2), county, seg_number(seg_ref, 0))
+
+        @pl.when(n == 1)
+        def _():
+            sums_ref[1] = sums_ref[0]
+
+    else:
+        lax.fori_loop(1, n - 1, county, seg_number(seg_ref, 1))
 
 
 def give_kernel(second, parts_n, *refs):
     seg_ref, refs = refs[0], refs[1:]
     msgs, refs, parts_ref = refs[:parts_n], refs[parts_n:-1], refs[-1]
     if second:
-        w_ref, cols_ref, r1_ref, edge_ref, sums_ref, rcol_ref, total_ref = refs
+        w_ref, cols_ref, r1_ref, edge_ref, rcol_ref, total_ref = refs
     else:
-        _, w_ref, cols_ref, edge_ref, sums_ref, rcol_ref = refs
+        _, w_ref, cols_ref, edge_ref, rcol_ref = refs
         r1_ref = rcol_ref
     total = msgs[0][...]
     for m in msgs[1:]:
@@ -256,15 +263,19 @@
         total_ref[...] = total
     rcol = cols_ref[1] / column(total[0:1])
     rcol_ref[...] = rcol * SCALE if second else rcol
-    sums_body(second, False, seg_ref, w_ref, cols_ref, r1_ref, rcol_ref, edge_ref, sums_ref, parts_ref)
+    sums_body(second, False, True, seg_ref, w_ref, cols_ref, r1_ref, rcol_ref, edge_ref, parts_ref)
 
 
 def keep_kernel(second, seg_ref, w_ref, cols_ref, r1_ref, *refs):
+    if second:
+        r2_ref, total_ref, edge_ref, sums_ref, scale_ref, give_ref, parts_ref = refs
+    else:
+        edge_ref, sums_ref, give_ref, parts_ref = refs
+        r2_ref = None
+    for mine, ends, out_ref in ((True, True, edge_ref), (True, False, sums_ref), (False, False, give_ref)):
+        sums_body(second, mine, ends, seg_ref, w_ref, cols_ref, r1_ref, r2_ref, out_ref, parts_ref)
     if not second:
-        sums_body(second, True, seg_ref, w_ref, cols_ref, r1_ref, None, *refs)
         return
-    r2_ref, total_ref, scale_ref = refs[0], refs[1], refs[4]
-    sums_body(second, True, seg_ref, w_ref, cols_ref, r1_ref, r2_ref, refs[2], refs[3], refs[5])
     share = total_ref[1:2, :]
     lane = lax.broadcasted_iota(jnp.int32, (1, LANES), 1)
 
@@ -512,18 +523,18 @@
             pltpu.SemaphoreType.DMA((3 + counties // SUB,)),
         ],
     )
-    give, sums_give, r1 = call(
+    give, r1 = call(
         functools.partial(give_kernel, False, parts),
         "county_sums_1a",
         [seg] + msgs + [share, slab, cols],
         [VMEM] * (parts + 4),
-        (edge, table, column_of),
+        (edge, column_of),
         None,
         parts_scratch,
     )
-    own, other, (sums_keep,) = edges(
+    own, other, (sums_keep, sums_give) = edges(
         give,
-        lambda: call(functools.partial(keep_kernel, False), "county_sums_1b", (seg, slab, cols, r1), [VMEM] * 4, (edge, table), None, parts_scratch),
+        lambda: call(functools.partial(keep_kernel, False), "county_sums_1b", (seg, slab, cols, r1), [VMEM] * 4, (edge, table, table), None, parts_scratch),
     )
     fac = pltpu.VMEM((counties, half_rows, LANES), jnp.float32)
     goal_keep, part = call(
@@ -544,18 +555,18 @@
         None,
         [fac, pltpu.VMEM((rows, LANES), jnp.float32)],
     )
-    give, sums_give, r2, total = call(
+    give, r2, total = call(
         functools.partial(give_kernel, True, parts),
         "county_sums_2a",
         [seg] + over_type(msg) + [slab, cols, r1],
         [VMEM] * (parts + 4),
-        (edge, table, column_of, small),
+        (edge, column_of, small),
         None,
         parts_scratch,
     )
-    own, other, (sums_keep, scale) = edges(
+    own, other, (sums_keep, scale, sums_give) = edges(
         give,
-        lambda: call(functools.partial(keep_kernel, True), "county_sums_2b", (seg, slab, cols, r1, r2, total), [VMEM] * 6, (edge, table, f32(counties, LANES)), None, parts_scratch),
+        lambda: call(functools.partial(keep_kernel, True), "county_sums_2b", (seg, slab, cols, r1, r2, total), [VMEM] * 6, (edge, table, f32(counties, LANES), table), None, parts_scratch),
     )
     mine = call(
         last_own_kernel,

time: 73.7 us -> 73.5 us (level)
  no operation moved by 1% of the time
where the time goes in v7:
time: 73.5 us; the launch traced here: 73.3 us
  blocking collectives  27.2 us (37%)
  starting transfers between devices  24.8 us (34%)
  Pallas kernels  11.5 us (16%)
  waiting for transfers between devices  9.63 us (13%)
    all_to_all x2, blocking collectives, edges(): far = lax.all_to_all(send, 'bg', 0, 0, axis_index_groups=lines)  27.2 us
    ppermute x16, starting transfers between devices, swap(): return lax.ppermute(x, axis, [(i, i ^ mask) for i in range(size)])  24.8 us
    pallas_call x16, Pallas kernels, call(): pl.pallas_call(kernel, out_shape=out_shape, in_specs=in_specs, out_specs=...  11.5 us
    ppermute x16, waiting for transfers between devices, swap(): return lax.ppermute(x, axis, [(i, i ^ mask) for i in range(size)])  9.63 us
  transfers between devices with their start and end apart: 16, of which 11 were waited for; matrix products, arithmetic and copies ran while one was open for 0% of the time, Pallas kernels for 6%

profile of v7, /device:TPU:1, one launch (start us, length us, event | category | flops | bytes accessed | tf_op | source)
XLA Modules:
  0.0 73.3 jit_solution(6421775134850498317)
XLA Ops:
  0.0 2.6 %row_sums_1.1 = (f32[8,128]{1,0:T(8,128)S(1)}, f32[2,128,4608]{2,1,0:T(8,128)S(1)}) custom-call(f32[128,9216]{1,0:T(8,128)} %w_hbm.1), custom_call_target="tpu_custom_call" | custom-call | flops 4194304 | bytes 4194304 | tf_op jit(solution)/shard_map/row_sums_1/pallas_call | solution.py:454
  2.6 3.7 %collective-permute-start.2 = (f32[8,128]{1,0:T(8,128)S(1)}, f32[8,128]{1,0:T(8,128)S(1)}, u32[]{:S(2)}, u32[]{:S(2)}) collective-permute-start(f32[8,128]{1,0:T(8,128)S(1)} %get-tuple-element.34.refs_1_), channel_id=1, source_target_pairs={{0,3},{1,2},{2,1},{3,0},{4,7},{5,6},{6,5},{7,4},{8,11},{9,10},{10,... | collective-permute-start | bytes 12296 | tf_op jit(solution)/shard_map/ppermute | solution.py:492
  7.0 2.0 %prepare.1 = (s32[216,128]{1,0:T(8,128)S(1)}, f32[2,128,128]{2,1,0:T(8,128)S(1)}, f32[64,2,40,128]{3,2,1,0:T(8,128)S(1)}, f32[8,128]{1,0:T(8,128)S(1)}) custom-call(s32[128]{0:T(128)} %cid_hbm.1, s32[1,128]{1,0:T(1,128)} %bitcast.2, s32[1,128]{1,0:T(1,128)} %bitcast.3, s32[64,9216]{1,0:T(8,128)} %tgt_hbm.1), custom_call_target="tpu_custom_call" | custom-call | flops 4194304 | bytes 4194304 | tf_op jit(solution)/shard_map/prepare/pallas_call | solution.py:454
  9.0 1.3 %collective-permute-done.1.refs_3_ = f32[8,128]{1,0:T(8,128)S(1)} collective-permute-done((f32[8,128]{1,0:T(8,128)S(1)}, f32[8,128]{1,0:T(8,128)S(1)}, u32[]{:S(2)}, u32[]{:S(2)}) %collective-permute-start.1) | collective-permute-done | bytes 4128 | tf_op jit(solution)/shard_map/ppermute | solution.py:492
  10.8 2.2 %collective-permute-start.3 = (f32[2,40,128]{2,1,0:T(8,128)S(1)}, f32[2,40,128]{2,1,0:T(8,128)S(1)}, u32[]{:S(2)}, u32[]{:S(2)}) collective-permute-start(f32[2,40,128]{2,1,0:T(8,128)S(1)} %get-tuple-element.39), channel_id=1, source_target_pairs={{0,4},{4,0},{8,12},{12,8},{16,20},{20,16},{24,28},{28,24},{32,36},... | collective-permute-start | bytes 122888 | tf_op jit(solution)/shard_map/ppermute | solution.py:492
  13.8 2.6 %collective-permute-start.6 = (f32[2,40,128]{2,1,0:T(8,128)S(1)}, f32[2,40,128]{2,1,0:T(8,128)S(1)}, u32[]{:S(2)}, u32[]{:S(2)}) collective-permute-start(f32[2,40,128]{2,1,0:T(8,128)S(1)} %chip_sums.2.refs_0_), channel_id=1, source_target_pairs={{0,24},{4,28},{8,16},{12,20},{16,8},{20,12},{24,0},{28,4},{32,56},... | collective-permute-start | bytes 122888 | tf_op jit(solution)/shard_map/ppermute | solution.py:492
  17.2 0.8 %collective-permute-done.6.refs_3_.refs_2_ = f32[2,40,128]{2,1,0:T(8,128)S(1)} collective-permute-done((f32[2,40,128]{2,1,0:T(8,128)S(1)}, f32[2,40,128]{2,1,0:T(8,128)S(1)}, u32[]{:S(2)}, u32[]{:S(2)}) %collective-permute-start.6) | collective-permute-done | bytes 40992 | tf_op jit(solution)/shard_map/ppermute | solution.py:492
  18.0 2.8 %collective-permute-done.5.refs_2_.refs_1_ = f32[2,40,128]{2,1,0:T(8,128)S(1)} collective-permute-done((f32[2,40,128]{2,1,0:T(8,128)S(1)}, f32[2,40,128]{2,1,0:T(8,128)S(1)}, u32[]{:S(2)}, u32[]{:S(2)}) %collective-permute-start.5) | collective-permute-done | bytes 40992 | tf_op jit(solution)/shard_map/ppermute | solution.py:492
  20.8 16.4 %all_to_all.10.far_ref = f32[8,40,128]{2,1,0:T(8,128)S(1)} all-to-all(f32[8,40,128]{2,1,0:T(8,128)S(1)} %plane_sums.2), channel_id=1, replica_groups={{0,32,64,96,128,160,192,224},{4,36,68,100,132,164,196,228},{8,40,72,104..., dimensions={0} | all-to-all | bytes 327680 | tf_op jit(solution)/shard_map/all_to_all | solution.py:505
  37.4 3.2 %collective-permute-start.7 = (f32[2,40,128]{2,1,0:T(8,128)S(1)}, f32[2,40,128]{2,1,0:T(8,128)S(1)}, u32[]{:S(2)}, u32[]{:S(2)}) collective-permute-start(f32[2,40,128]{2,1,0:T(8,128)S(1)} %get-tuple-element.40), channel_id=1, source_target_pairs={{0,4},{4,0},{8,12},{12,8},{16,20},{20,16},{24,28},{28,24},{32,36},... | collective-permute-start | bytes 122888 | tf_op jit(solution)/shard_map/ppermute | solution.py:492
  41.5 0.7 row_sums_2b.1
  42.2 1.1 %collective-permute-start.10 = (f32[8,128]{1,0:T(8,128)S(1)}, f32[8,128]{1,0:T(8,128)S(1)}, u32[]{:S(2)}, u32[]{:S(2)}) collective-permute-start(f32[8,128]{1,0:T(8,128)S(1)} %get-tuple-element.45.refs_1_), channel_id=1, source_target_pairs={{0,3},{1,2},{2,1},{3,0},{4,7},{5,6},{6,5},{7,4},{8,11},{9,10},{10,... | collective-permute-start | bytes 12296 | tf_op jit(solution)/shard_map/ppermute | solution.py:492
  43.3 0.8 %collective-permute-start.9 = (f32[8,128]{1,0:T(8,128)S(1)}, f32[8,128]{1,0:T(8,128)S(1)}, u32[]{:S(2)}, u32[]{:S(2)}) collective-permute-start(f32[8,128]{1,0:T(8,128)S(1)} %get-tuple-element.45.refs_1_), channel_id=1, source_target_pairs={{0,2},{1,3},{2,0},{3,1},{4,6},{5,7},{6,4},{7,5},{8,10},{9,11},{10,... | collective-permute-start | bytes 12296 | tf_op jit(solution)/shard_map/ppermute | solution.py:492
  44.1 1.4 %collective-permute-start.8 = (f32[8,128]{1,0:T(8,128)S(1)}, f32[8,128]{1,0:T(8,128)S(1)}, u32[]{:S(2)}, u32[]{:S(2)}) collective-permute-start(f32[8,128]{1,0:T(8,128)S(1)} %get-tuple-element.45.refs_1_), channel_id=1, source_target_pairs={{0,1},{1,0},{2,3},{3,2},{4,5},{5,4},{6,7},{7,6},{8,9},{9,8},{10,11... | collective-permute-start | bytes 12296 | tf_op jit(solution)/shard_map/ppermute | solution.py:492
  46.0 1.3 %collective-permute-done.9.refs_3_ = f32[8,128]{1,0:T(8,128)S(1)} collective-permute-done((f32[8,128]{1,0:T(8,128)S(1)}, f32[8,128]{1,0:T(8,128)S(1)}, u32[]{:S(2)}, u32[]{:S(2)}) %collective-permute-start.9) | collective-permute-done | bytes 4128 | tf_op jit(solution)/shard_map/ppermute | solution.py:492
  47.9 1.9 %collective-permute-start.11 = (f32[2,40,128]{2,1,0:T(8,128)S(1)}, f32[2,40,128]{2,1,0:T(8,128)S(1)}, u32[]{:S(2)}, u32[]{:S(2)}) collective-permute-start(f32[2,40,128]{2,1,0:T(8,128)S(1)} %get-tuple-element.52), channel_id=1, source_target_pairs={{0,4},{4,0},{8,12},{12,8},{16,20},{20,16},{24,28},{28,24},{32,36},... | collective-permute-start | bytes 122888 | tf_op jit(solution)/shard_map/ppermute | solution.py:492
  50.6 1.0 %collective-permute-start.14 = (f32[2,40,128]{2,1,0:T(8,128)S(1)}, f32[2,40,128]{2,1,0:T(8,128)S(1)}, u32[]{:S(2)}, u32[]{:S(2)}) collective-permute-start(f32[2,40,128]{2,1,0:T(8,128)S(1)} %chip_sums.3.refs_0_), channel_id=1, source_target_pairs={{0,24},{4,28},{8,16},{12,20},{16,8},{20,12},{24,0},{28,4},{32,56},... | collective-permute-start | bytes 122888 | tf_op jit(solution)/shard_map/ppermute | solution.py:492
  51.6 1.0 %collective-permute-start.13 = (f32[2,40,128]{2,1,0:T(8,128)S(1)}, f32[2,40,128]{2,1,0:T(8,128)S(1)}, u32[]{:S(2)}, u32[]{:S(2)}) collective-permute-start(f32[2,40,128]{2,1,0:T(8,128)S(1)} %chip_sums.3.refs_0_), channel_id=1, source_target_pairs={{0,16},{4,20},{8,24},{12,28},{16,0},{20,4},{24,8},{28,12},{32,48},... | collective-permute-start | bytes 122888 | tf_op jit(solution)/shard_map/ppermute | solution.py:492
  52.6 1.4 %collective-permute-start.12 = (f32[2,40,128]{2,1,0:T(8,128)S(1)}, f32[2,40,128]{2,1,0:T(8,128)S(1)}, u32[]{:S(2)}, u32[]{:S(2)}) collective-permute-start(f32[2,40,128]{2,1,0:T(8,128)S(1)} %chip_sums.3.refs_0_), channel_id=1, source_target_pairs={{0,8},{4,12},{8,0},{12,4},{16,24},{20,28},{24,16},{28,20},{32,40},... | collective-permute-start | bytes 122888 | tf_op jit(solution)/shard_map/ppermute | solution.py:492
  54.0 0.8 %collective-permute-done.14.refs_3_.refs_2_ = f32[2,40,128]{2,1,0:T(8,128)S(1)} collective-permute-done((f32[2,40,128]{2,1,0:T(8,128)S(1)}, f32[2,40,128]{2,1,0:T(8,128)S(1)}, u32[]{:S(2)}, u32[]{:S(2)}) %collective-permute-start.14) | collective-permute-done | bytes 40992 | tf_op jit(solution)/shard_map/ppermute | solution.py:492
  54.8 1.2 %collective-permute-done.13.refs_2_.refs_1_ = f32[2,40,128]{2,1,0:T(8,128)S(1)} collective-permute-done((f32[2,40,128]{2,1,0:T(8,128)S(1)}, f32[2,40,128]{2,1,0:T(8,128)S(1)}, u32[]{:S(2)}, u32[]{:S(2)}) %collective-permute-start.13) | collective-permute-done | bytes 40992 | tf_op jit(solution)/shard_map/ppermute | solution.py:492
  56.1 10.8 %all_to_all.11.far_ref = f32[8,40,128]{2,1,0:T(8,128)S(1)} all-to-all(f32[8,40,128]{2,1,0:T(8,128)S(1)} %plane_sums.3), channel_id=1, replica_groups={{0,32,64,96,128,160,192,224},{4,36,68,100,132,164,196,228},{8,40,72,104..., dimensions={0} | all-to-all | bytes 327680 | tf_op jit(solution)/shard_map/all_to_all | solution.py:505
  67.0 3.2 %collective-permute-start.15 = (f32[2,40,128]{2,1,0:T(8,128)S(1)}, f32[2,40,128]{2,1,0:T(8,128)S(1)}, u32[]{:S(2)}, u32[]{:S(2)}) collective-permute-start(f32[2,40,128]{2,1,0:T(8,128)S(1)} %get-tuple-element.53), channel_id=1, source_target_pairs={{0,4},{4,0},{8,12},{12,8},{16,20},{20,16},{24,28},{28,24},{32,36},... | collective-permute-start | bytes 122888 | tf_op jit(solution)/shard_map/ppermute | solution.py:492
  71.1 2.2 %fitted_b.1 = f32[128,9216]{1,0:T(8,128)} custom-call(s32[216,128]{1,0:T(8,128)S(1)} %get-tuple-element.31.refs_0_.seg_ref, f32[2,128,4608]{2,1,0:T(8,128)S(1)} %get-tuple-element.32.refs_6_.w_ref.refs_5_, f32[2,128,128]{2,1,0:T(8,128)S(1)} %get-tuple-element.33.refs_7_.cols_ref.refs_6_, f32[128,128]{1,0:T(8,128)S(1)} %get-tuple-element.36.r1_ref.refs_7_, ...), custom_call_target="tpu_custom_call" | custom-call | flops 4194304 | bytes 4194304 | tf_op jit(solution)/shard_map/fitted_b/pallas_call | solution.py:454
  (26 shorter events, 6.9 us)
Async XLA Ops:
  2.6 6.3 %collective-permute-start.2 = (f32[8,128]{1,0:T(8,128)S(1)}, f32[8,128]{1,0:T(8,128)S(1)}, u32[]{:S(2)}, u32[]{:S(2)}) collective-permute-start(f32[8,128]{1,0:T(8,128)S(1)} %get-tuple-element.34.refs_1_), channel_id=1, source_target_pairs={{0,3},{1,2},{2,1},{3,0},{4,7},{5,6},{6,5},{7,4},{8,11},{9,10},{10,... | collective-permute-start | bytes 12296 | tf_op jit(solution)/shard_map/ppermute | solution.py:492
  6.3 4.0 %collective-permute-start.1 = (f32[8,128]{1,0:T(8,128)S(1)}, f32[8,128]{1,0:T(8,128)S(1)}, u32[]{:S(2)}, u32[]{:S(2)}) collective-permute-start(f32[8,128]{1,0:T(8,128)S(1)} %get-tuple-element.34.refs_1_), channel_id=1, source_target_pairs={{0,2},{1,3},{2,0},{3,1},{4,6},{5,7},{6,4},{7,5},{8,10},{9,11},{10,... | collective-permute-start | bytes 12296 | tf_op jit(solution)/shard_map/ppermute | solution.py:492
  6.6 3.6 %collective-permute-start = (f32[8,128]{1,0:T(8,128)S(1)}, f32[8,128]{1,0:T(8,128)S(1)}, u32[]{:S(2)}, u32[]{:S(2)}) collective-permute-start(f32[8,128]{1,0:T(8,128)S(1)} %get-tuple-element.34.refs_1_), channel_id=1, source_target_pairs={{0,1},{1,0},{2,3},{3,2},{4,5},{5,4},{6,7},{7,6},{8,9},{9,8},{10,11... | collective-permute-start | bytes 12296 | tf_op jit(solution)/shard_map/ppermute | solution.py:492
  10.8 3.1 %collective-permute-start.3 = (f32[2,40,128]{2,1,0:T(8,128)S(1)}, f32[2,40,128]{2,1,0:T(8,128)S(1)}, u32[]{:S(2)}, u32[]{:S(2)}) collective-permute-start(f32[2,40,128]{2,1,0:T(8,128)S(1)} %get-tuple-element.39), channel_id=1, source_target_pairs={{0,4},{4,0},{8,12},{12,8},{16,20},{20,16},{24,28},{28,24},{32,36},... | collective-permute-start | bytes 122888 | tf_op jit(solution)/shard_map/ppermute | solution.py:492
  13.8 4.2 %collective-permute-start.6 = (f32[2,40,128]{2,1,0:T(8,128)S(1)}, f32[2,40,128]{2,1,0:T(8,128)S(1)}, u32[]{:S(2)}, u32[]{:S(2)}) collective-permute-start(f32[2,40,128]{2,1,0:T(8,128)S(1)} %chip_sums.2.refs_0_), channel_id=1, source_target_pairs={{0,24},{4,28},{8,16},{12,20},{16,8},{20,12},{24,0},{28,4},{32,56},... | collective-permute-start | bytes 122888 | tf_op jit(solution)/shard_map/ppermute | solution.py:492
  16.4 4.4 %collective-permute-start.5 = (f32[2,40,128]{2,1,0:T(8,128)S(1)}, f32[2,40,128]{2,1,0:T(8,128)S(1)}, u32[]{:S(2)}, u32[]{:S(2)}) collective-permute-start(f32[2,40,128]{2,1,0:T(8,128)S(1)} %chip_sums.2.refs_0_), channel_id=1, source_target_pairs={{0,16},{4,20},{8,24},{12,28},{16,0},{20,4},{24,8},{28,12},{32,48},... | collective-permute-start | bytes 122888 | tf_op jit(solution)/shard_map/ppermute | solution.py:492
  16.9 3.8 %collective-permute-start.4 = (f32[2,40,128]{2,1,0:T(8,128)S(1)}, f32[2,40,128]{2,1,0:T(8,128)S(1)}, u32[]{:S(2)}, u32[]{:S(2)}) collective-permute-start(f32[2,40,128]{2,1,0:T(8,128)S(1)} %chip_sums.2.refs_0_), channel_id=1, source_target_pairs={{0,8},{4,12},{8,0},{12,4},{16,24},{20,28},{24,16},{28,20},{32,40},... | collective-permute-start | bytes 122888 | tf_op jit(solution)/shard_map/ppermute | solution.py:492
  37.4 4.1 %collective-permute-start.7 = (f32[2,40,128]{2,1,0:T(8,128)S(1)}, f32[2,40,128]{2,1,0:T(8,128)S(1)}, u32[]{:S(2)}, u32[]{:S(2)}) collective-permute-start(f32[2,40,128]{2,1,0:T(8,128)S(1)} %get-tuple-element.40), channel_id=1, source_target_pairs={{0,4},{4,0},{8,12},{12,8},{16,20},{20,16},{24,28},{28,24},{32,36},... | collective-permute-start | bytes 122888 | tf_op jit(solution)/shard_map/ppermute | solution.py:492
  42.2 3.8 %collective-permute-start.10 = (f32[8,128]{1,0:T(8,128)S(1)}, f32[8,128]{1,0:T(8,128)S(1)}, u32[]{:S(2)}, u32[]{:S(2)}) collective-permute-start(f32[8,128]{1,0:T(8,128)S(1)} %get-tuple-element.45.refs_1_), channel_id=1, source_target_pairs={{0,3},{1,2},{2,1},{3,0},{4,7},{5,6},{6,5},{7,4},{8,11},{9,10},{10,... | collective-permute-start | bytes 12296 | tf_op jit(solution)/shard_map/ppermute | solution.py:492
  43.3 4.0 %collective-permute-start.9 = (f32[8,128]{1,0:T(8,128)S(1)}, f32[8,128]{1,0:T(8,128)S(1)}, u32[]{:S(2)}, u32[]{:S(2)}) collective-permute-start(f32[8,128]{1,0:T(8,128)S(1)} %get-tuple-element.45.refs_1_), channel_id=1, source_target_pairs={{0,2},{1,3},{2,0},{3,1},{4,6},{5,7},{6,4},{7,5},{8,10},{9,11},{10,... | collective-permute-start | bytes 12296 | tf_op jit(solution)/shard_map/ppermute | solution.py:492
  44.1 3.1 %collective-permute-start.8 = (f32[8,128]{1,0:T(8,128)S(1)}, f32[8,128]{1,0:T(8,128)S(1)}, u32[]{:S(2)}, u32[]{:S(2)}) collective-permute-start(f32[8,128]{1,0:T(8,128)S(1)} %get-tuple-element.45.refs_1_), channel_id=1, source_target_pairs={{0,1},{1,0},{2,3},{3,2},{4,5},{5,4},{6,7},{7,6},{8,9},{9,8},{10,11... | collective-permute-start | bytes 12296 | tf_op jit(solution)/shard_map/ppermute | solution.py:492
  47.9 2.7 %collective-permute-start.11 = (f32[2,40,128]{2,1,0:T(8,128)S(1)}, f32[2,40,128]{2,1,0:T(8,128)S(1)}, u32[]{:S(2)}, u32[]{:S(2)}) collective-permute-start(f32[2,40,128]{2,1,0:T(8,128)S(1)} %get-tuple-element.52), channel_id=1, source_target_pairs={{0,4},{4,0},{8,12},{12,8},{16,20},{20,16},{24,28},{28,24},{32,36},... | collective-permute-start | bytes 122888 | tf_op jit(solution)/shard_map/ppermute | solution.py:492
  50.6 4.2 %collective-permute-start.14 = (f32[2,40,128]{2,1,0:T(8,128)S(1)}, f32[2,40,128]{2,1,0:T(8,128)S(1)}, u32[]{:S(2)}, u32[]{:S(2)}) collective-permute-start(f32[2,40,128]{2,1,0:T(8,128)S(1)} %chip_sums.3.refs_0_), channel_id=1, source_target_pairs={{0,24},{4,28},{8,16},{12,20},{16,8},{20,12},{24,0},{28,4},{32,56},... | collective-permute-start | bytes 122888 | tf_op jit(solution)/shard_map/ppermute | solution.py:492
  51.6 4.4 %collective-permute-start.13 = (f32[2,40,128]{2,1,0:T(8,128)S(1)}, f32[2,40,128]{2,1,0:T(8,128)S(1)}, u32[]{:S(2)}, u32[]{:S(2)}) collective-permute-start(f32[2,40,128]{2,1,0:T(8,128)S(1)} %chip_sums.3.refs_0_), channel_id=1, source_target_pairs={{0,16},{4,20},{8,24},{12,28},{16,0},{20,4},{24,8},{28,12},{32,48},... | collective-permute-start | bytes 122888 | tf_op jit(solution)/shard_map/ppermute | solution.py:492
  52.6 3.4 %collective-permute-start.12 = (f32[2,40,128]{2,1,0:T(8,128)S(1)}, f32[2,40,128]{2,1,0:T(8,128)S(1)}, u32[]{:S(2)}, u32[]{:S(2)}) collective-permute-start(f32[2,40,128]{2,1,0:T(8,128)S(1)} %chip_sums.3.refs_0_), channel_id=1, source_target_pairs={{0,8},{4,12},{8,0},{12,4},{16,24},{20,28},{24,16},{28,20},{32,40},... | collective-permute-start | bytes 122888 | tf_op jit(solution)/shard_map/ppermute | solution.py:492
  67.0 4.1 %collective-permute-start.15 = (f32[2,40,128]{2,1,0:T(8,128)S(1)}, f32[2,40,128]{2,1,0:T(8,128)S(1)}, u32[]{:S(2)}, u32[]{:S(2)}) collective-permute-start(f32[2,40,128]{2,1,0:T(8,128)S(1)} %get-tuple-element.53), channel_id=1, source_target_pairs={{0,4},{4,0},{8,12},{12,8},{16,20},{20,16},{24,28},{28,24},{32,36},... | collective-permute-start | bytes 122888 | tf_op jit(solution)/shard_map/ppermute | solution.py:492

commit v8 on v7

--- a/solution.py
+++ b/solution.py
@@ -268,23 +268,12 @@
 
 def keep_kernel(second, seg_ref, w_ref, cols_ref, r1_ref, *refs):
     if second:
-        r2_ref, total_ref, edge_ref, sums_ref, scale_ref, give_ref, parts_ref = refs
+        r2_ref, edge_ref, sums_ref, give_ref, parts_ref = refs
     else:
         edge_ref, sums_ref, give_ref, parts_ref = refs
         r2_ref = None
     for mine, ends, out_ref in ((True, True, edge_ref), (True, False, sums_ref), (False, False, give_ref)):
         sums_body(second, mine, ends, seg_ref, w_ref, cols_ref, r1_ref, r2_ref, out_ref, parts_ref)
-    if not second:
-        return
-    share = total_ref[1:2, :]
-    lane = lax.broadcasted_iota(jnp.int32, (1, LANES), 1)
-
-    @pl.loop(0, (seg_counts(seg_ref)[0] + 3) // 4)
-    def _(g):
-        for i in range(4):
-            k = 4 * g + i
-            whole = jnp.sum(jnp.where(lane == seg_name(seg_ref, k), share, 0.0), axis=1, keepdims=True)
-            scale_ref[pl.ds(k, 1), :] = jnp.broadcast_to((1.0 / SHARE) / whole, (1, LANES))
 
 
 def join(refs):
@@ -395,13 +384,16 @@
         message(msg_ref, jnp.sum(acc_ref[...].T, axis=0, keepdims=True), share_row_ref[1:2, :])
 
 
-def fitted(mine, chunks, done, seg_ref, w_ref, cols_ref, r1_ref, r2_ref, goal_ref, scale_ref, sums_ref, edge_ref, out_ref, fac_ref):
+def fitted(mine, chunks, done, seg_ref, w_ref, cols_ref, r1_ref, r2_ref, goal_ref, total_ref, sums_ref, edge_ref, out_ref, fac_ref):
     w_ref = w_ref.at[side_of(mine)]
     half = w_ref.shape[1] // LANES
     n = seg_counts(seg_ref)[0]
 
+    lane = lax.broadcasted_iota(jnp.int32, (1, LANES), 1)
+
     def factor(k, sum_ref):
-        fac_ref[k] = 100.0 * (goal_ref[k] * scale_ref[pl.ds(k, 1), :] / sum_ref[...])
+        whole = jnp.sum(jnp.where(lane == seg_name(seg_ref, k), total_ref[1:2, :], 0.0), axis=1, keepdims=True)
+        fac_ref[k] = 100.0 * (goal_ref[k] * ((1.0 / SHARE) / whole) / sum_ref[...])
 
     each_sum(n, edge_ref, sums_ref, factor)
     for q in range(chunks):
@@ -418,12 +410,12 @@
         done(q)
 
 
-def last_own_kernel(seg_ref, w_ref, cols_ref, r1_ref, r2_ref, goal_ref, scale_ref, sums_ref, edge_ref, out_ref, fac_ref):
-    fitted(True, 1, lambda q: None, seg_ref, w_ref, cols_ref, r1_ref, r2_ref, goal_ref, scale_ref, sums_ref, edge_ref, out_ref, fac_ref)
+def last_own_kernel(seg_ref, w_ref, cols_ref, r1_ref, r2_ref, goal_ref, total_ref, sums_ref, edge_ref, out_ref, fac_ref):
+    fitted(True, 1, lambda q: None, seg_ref, w_ref, cols_ref, r1_ref, r2_ref, goal_ref, total_ref, sums_ref, edge_ref, out_ref, fac_ref)
 
 
 def last_kernel(
-    chunks, seg_ref, w_ref, cols_ref, r1_ref, r2_ref, goal_ref, scale_ref, sums_ref, edge_ref, own_ref, out_hbm, out_ref, fac_ref, sems
+    chunks, seg_ref, w_ref, cols_ref, r1_ref, r2_ref, goal_ref, total_ref, sums_ref, edge_ref, own_ref, out_hbm, out_ref, fac_ref, sems
 ):
     width = w_ref.shape[2]
     block = width // chunks
@@ -443,7 +435,7 @@
         copy.start()
         copies.append(copy)
 
-    fitted(False, chunks, done, seg_ref, w_ref, cols_ref, r1_ref, r2_ref, goal_ref, scale_ref, sums_ref, edge_ref, out_ref, fac_ref)
+    fitted(False, chunks, done, seg_ref, w_ref, cols_ref, r1_ref, r2_ref, goal_ref, total_ref, sums_ref, edge_ref, out_ref, fac_ref)
     for copy in copies:
         copy.wait()
 
@@ -564,14 +556,14 @@
         None,
         parts_scratch,
     )
-    own, other, (sums_keep, scale, sums_give) = edges(
+    own, other, (sums_keep, sums_give) = edges(
         give,
-        lambda: call(functools.partial(keep_kernel, True), "county_sums_2b", (seg, slab, cols, r1, r2, total), [VMEM] * 6, (edge, table, f32(counties, LANES), table), None, parts_scratch),
+        lambda: call(functools.partial(keep_kernel, True), "county_sums_2b", (seg, slab, cols, r1, r2), [VMEM] * 5, (edge, table, table), None, parts_scratch),
     )
     mine = call(
         last_own_kernel,
         "fitted_a",
-        (seg, slab, cols, r1, r2, goal_keep, scale, sums_keep, own),
+        (seg, slab, cols, r1, r2, goal_keep, total, sums_keep, own),
         [VMEM] * 9,
         f32(rows, width // 2),
         None,
@@ -580,7 +572,7 @@
     return call(
         functools.partial(last_kernel, out_chunks),
         "fitted_b",
-        (seg, slab, cols, r1, r2, goal_give, scale, sums_give, other, mine),
+        (seg, slab, cols, r1, r2, goal_give, total, sums_give, other, mine),
         [VMEM] * 10,
         f32(rows, width),
         HBM,

time: 73.5 us -> 73.6 us (level)
  no operation moved by 1% of the time
where the time goes in v8:
time: 73.6 us; the launch traced here: 73.4 us
  blocking collectives  27.9 us (38%)
  starting transfers between devices  24.3 us (33%)
  Pallas kernels  11.5 us (16%)
  waiting for transfers between devices  9.73 us (13%)
    all_to_all x2, blocking collectives, edges(): far = lax.all_to_all(send, 'bg', 0, 0, axis_index_groups=lines)  27.9 us
    ppermute x16, starting transfers between devices, swap(): return lax.ppermute(x, axis, [(i, i ^ mask) for i in range(size)])  24.3 us
    pallas_call x16, Pallas kernels, call(): pl.pallas_call(kernel, out_shape=out_shape, in_specs=in_specs, out_specs=...  11.5 us
    ppermute x16, waiting for transfers between devices, swap(): return lax.ppermute(x, axis, [(i, i ^ mask) for i in range(size)])  9.73 us
  transfers between devices with their start and end apart: 16, of which 11 were waited for; matrix products, arithmetic and copies ran while one was open for 0% of the time, Pallas kernels for 6%

profile of v8, /device:TPU:1, one launch (start us, length us, event | category | flops | bytes accessed | tf_op | source)
XLA Modules:
  0.0 73.4 jit_solution(4045600401933085384)
XLA Ops:
  0.0 2.6 %row_sums_1.1 = (f32[8,128]{1,0:T(8,128)S(1)}, f32[2,128,4608]{2,1,0:T(8,128)S(1)}) custom-call(f32[128,9216]{1,0:T(8,128)} %w_hbm.1), custom_call_target="tpu_custom_call" | custom-call | flops 4194304 | bytes 4194304 | tf_op jit(solution)/shard_map/row_sums_1/pallas_call | solution.py:446
  2.6 3.7 %collective-permute-start.2 = (f32[8,128]{1,0:T(8,128)S(1)}, f32[8,128]{1,0:T(8,128)S(1)}, u32[]{:S(2)}, u32[]{:S(2)}) collective-permute-start(f32[8,128]{1,0:T(8,128)S(1)} %get-tuple-element.33.refs_1_), channel_id=1, source_target_pairs={{0,3},{1,2},{2,1},{3,0},{4,7},{5,6},{6,5},{7,4},{8,11},{9,10},{10,... | collective-permute-start | bytes 12296 | tf_op jit(solution)/shard_map/ppermute | solution.py:484
  7.0 2.0 %prepare.1 = (s32[216,128]{1,0:T(8,128)S(1)}, f32[2,128,128]{2,1,0:T(8,128)S(1)}, f32[64,2,40,128]{3,2,1,0:T(8,128)S(1)}, f32[8,128]{1,0:T(8,128)S(1)}) custom-call(s32[128]{0:T(128)} %cid_hbm.1, s32[1,128]{1,0:T(1,128)} %bitcast.2, s32[1,128]{1,0:T(1,128)} %bitcast.3, s32[64,9216]{1,0:T(8,128)} %tgt_hbm.1), custom_call_target="tpu_custom_call" | custom-call | flops 4194304 | bytes 4194304 | tf_op jit(solution)/shard_map/prepare/pallas_call | solution.py:446
  9.0 1.3 %collective-permute-done.1.refs_3_ = f32[8,128]{1,0:T(8,128)S(1)} collective-permute-done((f32[8,128]{1,0:T(8,128)S(1)}, f32[8,128]{1,0:T(8,128)S(1)}, u32[]{:S(2)}, u32[]{:S(2)}) %collective-permute-start.1) | collective-permute-done | bytes 4128 | tf_op jit(solution)/shard_map/ppermute | solution.py:484
  10.8 2.2 %collective-permute-start.3 = (f32[2,40,128]{2,1,0:T(8,128)S(1)}, f32[2,40,128]{2,1,0:T(8,128)S(1)}, u32[]{:S(2)}, u32[]{:S(2)}) collective-permute-start(f32[2,40,128]{2,1,0:T(8,128)S(1)} %get-tuple-element.38), channel_id=1, source_target_pairs={{0,4},{4,0},{8,12},{12,8},{16,20},{20,16},{24,28},{28,24},{32,36},... | collective-permute-start | bytes 122888 | tf_op jit(solution)/shard_map/ppermute | solution.py:484
  13.8 2.6 %collective-permute-start.6 = (f32[2,40,128]{2,1,0:T(8,128)S(1)}, f32[2,40,128]{2,1,0:T(8,128)S(1)}, u32[]{:S(2)}, u32[]{:S(2)}) collective-permute-start(f32[2,40,128]{2,1,0:T(8,128)S(1)} %chip_sums.2.refs_0_), channel_id=1, source_target_pairs={{0,24},{4,28},{8,16},{12,20},{16,8},{20,12},{24,0},{28,4},{32,56},... | collective-permute-start | bytes 122888 | tf_op jit(solution)/shard_map/ppermute | solution.py:484
  17.2 0.8 %collective-permute-done.6.refs_3_.refs_2_ = f32[2,40,128]{2,1,0:T(8,128)S(1)} collective-permute-done((f32[2,40,128]{2,1,0:T(8,128)S(1)}, f32[2,40,128]{2,1,0:T(8,128)S(1)}, u32[]{:S(2)}, u32[]{:S(2)}) %collective-permute-start.6) | collective-permute-done | bytes 40992 | tf_op jit(solution)/shard_map/ppermute | solution.py:484
  18.0 2.8 %collective-permute-done.5.refs_2_.refs_1_ = f32[2,40,128]{2,1,0:T(8,128)S(1)} collective-permute-done((f32[2,40,128]{2,1,0:T(8,128)S(1)}, f32[2,40,128]{2,1,0:T(8,128)S(1)}, u32[]{:S(2)}, u32[]{:S(2)}) %collective-permute-start.5) | collective-permute-done | bytes 40992 | tf_op jit(solution)/shard_map/ppermute | solution.py:484
  20.8 16.4 %all_to_all.10.far_ref = f32[8,40,128]{2,1,0:T(8,128)S(1)} all-to-all(f32[8,40,128]{2,1,0:T(8,128)S(1)} %plane_sums.2), channel_id=1, replica_groups={{0,32,64,96,128,160,192,224},{4,36,68,100,132,164,196,228},{8,40,72,104..., dimensions={0} | all-to-all | bytes 327680 | tf_op jit(solution)/shard_map/all_to_all | solution.py:497
  37.4 3.2 %collective-permute-start.7 = (f32[2,40,128]{2,1,0:T(8,128)S(1)}, f32[2,40,128]{2,1,0:T(8,128)S(1)}, u32[]{:S(2)}, u32[]{:S(2)}) collective-permute-start(f32[2,40,128]{2,1,0:T(8,128)S(1)} %get-tuple-element.39), channel_id=1, source_target_pairs={{0,4},{4,0},{8,12},{12,8},{16,20},{20,16},{24,28},{28,24},{32,36},... | collective-permute-start | bytes 122888 | tf_op jit(solution)/shard_map/ppermute | solution.py:484
  41.5 0.7 row_sums_2b.1
  42.2 1.1 %collective-permute-start.10 = (f32[8,128]{1,0:T(8,128)S(1)}, f32[8,128]{1,0:T(8,128)S(1)}, u32[]{:S(2)}, u32[]{:S(2)}) collective-permute-start(f32[8,128]{1,0:T(8,128)S(1)} %get-tuple-element.44.refs_1_), channel_id=1, source_target_pairs={{0,3},{1,2},{2,1},{3,0},{4,7},{5,6},{6,5},{7,4},{8,11},{9,10},{10,... | collective-permute-start | bytes 12296 | tf_op jit(solution)/shard_map/ppermute | solution.py:484
  43.3 0.8 %collective-permute-start.9 = (f32[8,128]{1,0:T(8,128)S(1)}, f32[8,128]{1,0:T(8,128)S(1)}, u32[]{:S(2)}, u32[]{:S(2)}) collective-permute-start(f32[8,128]{1,0:T(8,128)S(1)} %get-tuple-element.44.refs_1_), channel_id=1, source_target_pairs={{0,2},{1,3},{2,0},{3,1},{4,6},{5,7},{6,4},{7,5},{8,10},{9,11},{10,... | collective-permute-start | bytes 12296 | tf_op jit(solution)/shard_map/ppermute | solution.py:484
  44.1 1.4 %collective-permute-start.8 = (f32[8,128]{1,0:T(8,128)S(1)}, f32[8,128]{1,0:T(8,128)S(1)}, u32[]{:S(2)}, u32[]{:S(2)}) collective-permute-start(f32[8,128]{1,0:T(8,128)S(1)} %get-tuple-element.44.refs_1_), channel_id=1, source_target_pairs={{0,1},{1,0},{2,3},{3,2},{4,5},{5,4},{6,7},{7,6},{8,9},{9,8},{10,11... | collective-permute-start | bytes 12296 | tf_op jit(solution)/shard_map/ppermute | solution.py:484
  46.0 1.3 %collective-permute-done.9.refs_3_ = f32[8,128]{1,0:T(8,128)S(1)} collective-permute-done((f32[8,128]{1,0:T(8,128)S(1)}, f32[8,128]{1,0:T(8,128)S(1)}, u32[]{:S(2)}, u32[]{:S(2)}) %collective-permute-start.9) | collective-permute-done | bytes 4128 | tf_op jit(solution)/shard_map/ppermute | solution.py:484
  47.9 1.9 %collective-permute-start.11 = (f32[2,40,128]{2,1,0:T(8,128)S(1)}, f32[2,40,128]{2,1,0:T(8,128)S(1)}, u32[]{:S(2)}, u32[]{:S(2)}) collective-permute-start(f32[2,40,128]{2,1,0:T(8,128)S(1)} %get-tuple-element.50), channel_id=1, source_target_pairs={{0,4},{4,0},{8,12},{12,8},{16,20},{20,16},{24,28},{28,24},{32,36},... | collective-permute-start | bytes 122888 | tf_op jit(solution)/shard_map/ppermute | solution.py:484
  50.6 1.1 %collective-permute-start.14 = (f32[2,40,128]{2,1,0:T(8,128)S(1)}, f32[2,40,128]{2,1,0:T(8,128)S(1)}, u32[]{:S(2)}, u32[]{:S(2)}) collective-permute-start(f32[2,40,128]{2,1,0:T(8,128)S(1)} %chip_sums.3.refs_0_), channel_id=1, source_target_pairs={{0,24},{4,28},{8,16},{12,20},{16,8},{20,12},{24,0},{28,4},{32,56},... | collective-permute-start | bytes 122888 | tf_op jit(solution)/shard_map/ppermute | solution.py:484
  51.7 1.0 %collective-permute-start.13 = (f32[2,40,128]{2,1,0:T(8,128)S(1)}, f32[2,40,128]{2,1,0:T(8,128)S(1)}, u32[]{:S(2)}, u32[]{:S(2)}) collective-permute-start(f32[2,40,128]{2,1,0:T(8,128)S(1)} %chip_sums.3.refs_0_), channel_id=1, source_target_pairs={{0,16},{4,20},{8,24},{12,28},{16,0},{20,4},{24,8},{28,12},{32,48},... | collective-permute-start | bytes 122888 | tf_op jit(solution)/shard_map/ppermute | solution.py:484
  52.7 1.3 %collective-permute-start.12 = (f32[2,40,128]{2,1,0:T(8,128)S(1)}, f32[2,40,128]{2,1,0:T(8,128)S(1)}, u32[]{:S(2)}, u32[]{:S(2)}) collective-permute-start(f32[2,40,128]{2,1,0:T(8,128)S(1)} %chip_sums.3.refs_0_), channel_id=1, source_target_pairs={{0,8},{4,12},{8,0},{12,4},{16,24},{20,28},{24,16},{28,20},{32,40},... | collective-permute-start | bytes 122888 | tf_op jit(solution)/shard_map/ppermute | solution.py:484
  54.0 0.8 %collective-permute-done.14.refs_3_.refs_2_ = f32[2,40,128]{2,1,0:T(8,128)S(1)} collective-permute-done((f32[2,40,128]{2,1,0:T(8,128)S(1)}, f32[2,40,128]{2,1,0:T(8,128)S(1)}, u32[]{:S(2)}, u32[]{:S(2)}) %collective-permute-start.14) | collective-permute-done | bytes 40992 | tf_op jit(solution)/shard_map/ppermute | solution.py:484
  54.8 1.3 %collective-permute-done.13.refs_2_.refs_1_ = f32[2,40,128]{2,1,0:T(8,128)S(1)} collective-permute-done((f32[2,40,128]{2,1,0:T(8,128)S(1)}, f32[2,40,128]{2,1,0:T(8,128)S(1)}, u32[]{:S(2)}, u32[]{:S(2)}) %collective-permute-start.13) | collective-permute-done | bytes 40992 | tf_op jit(solution)/shard_map/ppermute | solution.py:484
  56.2 11.4 %all_to_all.11.far_ref = f32[8,40,128]{2,1,0:T(8,128)S(1)} all-to-all(f32[8,40,128]{2,1,0:T(8,128)S(1)} %plane_sums.3), channel_id=1, replica_groups={{0,32,64,96,128,160,192,224},{4,36,68,100,132,164,196,228},{8,40,72,104..., dimensions={0} | all-to-all | bytes 327680 | tf_op jit(solution)/shard_map/all_to_all | solution.py:497
  67.7 2.6 %collective-permute-start.15 = (f32[2,40,128]{2,1,0:T(8,128)S(1)}, f32[2,40,128]{2,1,0:T(8,128)S(1)}, u32[]{:S(2)}, u32[]{:S(2)}) collective-permute-start(f32[2,40,128]{2,1,0:T(8,128)S(1)} %get-tuple-element.51), channel_id=1, source_target_pairs={{0,4},{4,0},{8,12},{12,8},{16,20},{20,16},{24,28},{28,24},{32,36},... | collective-permute-start | bytes 122888 | tf_op jit(solution)/shard_map/ppermute | solution.py:484
  71.2 2.2 %fitted_b.1 = f32[128,9216]{1,0:T(8,128)} custom-call(s32[216,128]{1,0:T(8,128)S(1)} %get-tuple-element.30.refs_0_.seg_ref, f32[2,128,4608]{2,1,0:T(8,128)S(1)} %get-tuple-element.31.refs_6_.w_ref.refs_5_, f32[2,128,128]{2,1,0:T(8,128)S(1)} %get-tuple-element.32.refs_7_.cols_ref.refs_6_, f32[128,128]{1,0:T(8,128)S(1)} %get-tuple-element.35.r1_ref.refs_7_, ...), custom_call_target="tpu_custom_call" | custom-call | flops 4194304 | bytes 4194304 | tf_op jit(solution)/shard_map/fitted_b/pallas_call | solution.py:446
  (26 shorter events, 6.9 us)
Async XLA Ops:
  2.6 6.3 %collective-permute-start.2 = (f32[8,128]{1,0:T(8,128)S(1)}, f32[8,128]{1,0:T(8,128)S(1)}, u32[]{:S(2)}, u32[]{:S(2)}) collective-permute-start(f32[8,128]{1,0:T(8,128)S(1)} %get-tuple-element.33.refs_1_), channel_id=1, source_target_pairs={{0,3},{1,2},{2,1},{3,0},{4,7},{5,6},{6,5},{7,4},{8,11},{9,10},{10,... | collective-permute-start | bytes 12296 | tf_op jit(solution)/shard_map/ppermute | solution.py:484
  6.3 4.0 %collective-permute-start.1 = (f32[8,128]{1,0:T(8,128)S(1)}, f32[8,128]{1,0:T(8,128)S(1)}, u32[]{:S(2)}, u32[]{:S(2)}) collective-permute-start(f32[8,128]{1,0:T(8,128)S(1)} %get-tuple-element.33.refs_1_), channel_id=1, source_target_pairs={{0,2},{1,3},{2,0},{3,1},{4,6},{5,7},{6,4},{7,5},{8,10},{9,11},{10,... | collective-permute-start | bytes 12296 | tf_op jit(solution)/shard_map/ppermute | solution.py:484
  6.6 3.6 %collective-permute-start = (f32[8,128]{1,0:T(8,128)S(1)}, f32[8,128]{1,0:T(8,128)S(1)}, u32[]{:S(2)}, u32[]{:S(2)}) collective-permute-start(f32[8,128]{1,0:T(8,128)S(1)} %get-tuple-element.33.refs_1_), channel_id=1, source_target_pairs={{0,1},{1,0},{2,3},{3,2},{4,5},{5,4},{6,7},{7,6},{8,9},{9,8},{10,11... | collective-permute-start | bytes 12296 | tf_op jit(solution)/shard_map/ppermute | solution.py:484
  10.8 3.1 %collective-permute-start.3 = (f32[2,40,128]{2,1,0:T(8,128)S(1)}, f32[2,40,128]{2,1,0:T(8,128)S(1)}, u32[]{:S(2)}, u32[]{:S(2)}) collective-permute-start(f32[2,40,128]{2,1,0:T(8,128)S(1)} %get-tuple-element.38), channel_id=1, source_target_pairs={{0,4},{4,0},{8,12},{12,8},{16,20},{20,16},{24,28},{28,24},{32,36},... | collective-permute-start | bytes 122888 | tf_op jit(solution)/shard_map/ppermute | solution.py:484
  13.8 4.2 %collective-permute-start.6 = (f32[2,40,128]{2,1,0:T(8,128)S(1)}, f32[2,40,128]{2,1,0:T(8,128)S(1)}, u32[]{:S(2)}, u32[]{:S(2)}) collective-permute-start(f32[2,40,128]{2,1,0:T(8,128)S(1)} %chip_sums.2.refs_0_), channel_id=1, source_target_pairs={{0,24},{4,28},{8,16},{12,20},{16,8},{20,12},{24,0},{28,4},{32,56},... | collective-permute-start | bytes 122888 | tf_op jit(solution)/shard_map/ppermute | solution.py:484
  16.4 4.4 %collective-permute-start.5 = (f32[2,40,128]{2,1,0:T(8,128)S(1)}, f32[2,40,128]{2,1,0:T(8,128)S(1)}, u32[]{:S(2)}, u32[]{:S(2)}) collective-permute-start(f32[2,40,128]{2,1,0:T(8,128)S(1)} %chip_sums.2.refs_0_), channel_id=1, source_target_pairs={{0,16},{4,20},{8,24},{12,28},{16,0},{20,4},{24,8},{28,12},{32,48},... | collective-permute-start | bytes 122888 | tf_op jit(solution)/shard_map/ppermute | solution.py:484
  16.9 3.8 %collective-permute-start.4 = (f32[2,40,128]{2,1,0:T(8,128)S(1)}, f32[2,40,128]{2,1,0:T(8,128)S(1)}, u32[]{:S(2)}, u32[]{:S(2)}) collective-permute-start(f32[2,40,128]{2,1,0:T(8,128)S(1)} %chip_sums.2.refs_0_), channel_id=1, source_target_pairs={{0,8},{4,12},{8,0},{12,4},{16,24},{20,28},{24,16},{28,20},{32,40},... | collective-permute-start | bytes 122888 | tf_op jit(solution)/shard_map/ppermute | solution.py:484
  37.4 4.1 %collective-permute-start.7 = (f32[2,40,128]{2,1,0:T(8,128)S(1)}, f32[2,40,128]{2,1,0:T(8,128)S(1)}, u32[]{:S(2)}, u32[]{:S(2)}) collective-permute-start(f32[2,40,128]{2,1,0:T(8,128)S(1)} %get-tuple-element.39), channel_id=1, source_target_pairs={{0,4},{4,0},{8,12},{12,8},{16,20},{20,16},{24,28},{28,24},{32,36},... | collective-permute-start | bytes 122888 | tf_op jit(solution)/shard_map/ppermute | solution.py:484
  42.2 3.8 %collective-permute-start.10 = (f32[8,128]{1,0:T(8,128)S(1)}, f32[8,128]{1,0:T(8,128)S(1)}, u32[]{:S(2)}, u32[]{:S(2)}) collective-permute-start(f32[8,128]{1,0:T(8,128)S(1)} %get-tuple-element.44.refs_1_), channel_id=1, source_target_pairs={{0,3},{1,2},{2,1},{3,0},{4,7},{5,6},{6,5},{7,4},{8,11},{9,10},{10,... | collective-permute-start | bytes 12296 | tf_op jit(solution)/shard_map/ppermute | solution.py:484
  43.3 4.0 %collective-permute-start.9 = (f32[8,128]{1,0:T(8,128)S(1)}, f32[8,128]{1,0:T(8,128)S(1)}, u32[]{:S(2)}, u32[]{:S(2)}) collective-permute-start(f32[8,128]{1,0:T(8,128)S(1)} %get-tuple-element.44.refs_1_), channel_id=1, source_target_pairs={{0,2},{1,3},{2,0},{3,1},{4,6},{5,7},{6,4},{7,5},{8,10},{9,11},{10,... | collective-permute-start | bytes 12296 | tf_op jit(solution)/shard_map/ppermute | solution.py:484
  44.1 3.1 %collective-permute-start.8 = (f32[8,128]{1,0:T(8,128)S(1)}, f32[8,128]{1,0:T(8,128)S(1)}, u32[]{:S(2)}, u32[]{:S(2)}) collective-permute-start(f32[8,128]{1,0:T(8,128)S(1)} %get-tuple-element.44.refs_1_), channel_id=1, source_target_pairs={{0,1},{1,0},{2,3},{3,2},{4,5},{5,4},{6,7},{7,6},{8,9},{9,8},{10,11... | collective-permute-start | bytes 12296 | tf_op jit(solution)/shard_map/ppermute | solution.py:484
  47.9 2.7 %collective-permute-start.11 = (f32[2,40,128]{2,1,0:T(8,128)S(1)}, f32[2,40,128]{2,1,0:T(8,128)S(1)}, u32[]{:S(2)}, u32[]{:S(2)}) collective-permute-start(f32[2,40,128]{2,1,0:T(8,128)S(1)} %get-tuple-element.50), channel_id=1, source_target_pairs={{0,4},{4,0},{8,12},{12,8},{16,20},{20,16},{24,28},{28,24},{32,36},... | collective-permute-start | bytes 122888 | tf_op jit(solution)/shard_map/ppermute | solution.py:484
  50.6 4.2 %collective-permute-start.14 = (f32[2,40,128]{2,1,0:T(8,128)S(1)}, f32[2,40,128]{2,1,0:T(8,128)S(1)}, u32[]{:S(2)}, u32[]{:S(2)}) collective-permute-start(f32[2,40,128]{2,1,0:T(8,128)S(1)} %chip_sums.3.refs_0_), channel_id=1, source_target_pairs={{0,24},{4,28},{8,16},{12,20},{16,8},{20,12},{24,0},{28,4},{32,56},... | collective-permute-start | bytes 122888 | tf_op jit(solution)/shard_map/ppermute | solution.py:484
  51.7 4.4 %collective-permute-start.13 = (f32[2,40,128]{2,1,0:T(8,128)S(1)}, f32[2,40,128]{2,1,0:T(8,128)S(1)}, u32[]{:S(2)}, u32[]{:S(2)}) collective-permute-start(f32[2,40,128]{2,1,0:T(8,128)S(1)} %chip_sums.3.refs_0_), channel_id=1, source_target_pairs={{0,16},{4,20},{8,24},{12,28},{16,0},{20,4},{24,8},{28,12},{32,48},... | collective-permute-start | bytes 122888 | tf_op jit(solution)/shard_map/ppermute | solution.py:484
  52.7 3.4 %collective-permute-start.12 = (f32[2,40,128]{2,1,0:T(8,128)S(1)}, f32[2,40,128]{2,1,0:T(8,128)S(1)}, u32[]{:S(2)}, u32[]{:S(2)}) collective-permute-start(f32[2,40,128]{2,1,0:T(8,128)S(1)} %chip_sums.3.refs_0_), channel_id=1, source_target_pairs={{0,8},{4,12},{8,0},{12,4},{16,24},{20,28},{24,16},{28,20},{32,40},... | collective-permute-start | bytes 122888 | tf_op jit(solution)/shard_map/ppermute | solution.py:484
  67.7 3.5 %collective-permute-start.15 = (f32[2,40,128]{2,1,0:T(8,128)S(1)}, f32[2,40,128]{2,1,0:T(8,128)S(1)}, u32[]{:S(2)}, u32[]{:S(2)}) collective-permute-start(f32[2,40,128]{2,1,0:T(8,128)S(1)} %get-tuple-element.51), channel_id=1, source_target_pairs={{0,4},{4,0},{8,12},{12,8},{16,20},{20,16},{24,28},{28,24},{32,36},... | collective-permute-start | bytes 122888 | tf_op jit(solution)/shard_map/ppermute | solution.py:484
